TPU v7x, 32 devices: a whole 2x2x4 slice. The times are simulated.
32 devices in a mesh: fsdp: 32 (over z, y, x, core).
Axes of the slice: x: 2, y: 2, z: 4, core: 2. Of those that a mesh axis runs over, the one named last changes fastest.
Arguments:
- latents: float32 [64, 256, 16], P('fsdp'), may hold values from -6 to 6
- noise: float32 [64, 256, 16], P('fsdp'), may hold values from -6 to 6
- times: float32 [64], P('fsdp'), may hold values from 0 to 1, as said below
- labels: int32 [64], P('fsdp'), may hold values from 0 to 999
- dropped: int32 [64], P('fsdp'), may hold values 0 or 1
- features: bfloat16 [64, 256, 768], P('fsdp'), may hold values from -6 to 6
- layer_flat: float32 [2, 10627584], P(None, 'fsdp'), may hold values from -0.21875 to 0.21875
- layer_mean: float32 [2, 10627584], P(None, 'fsdp'), may hold values from -1.4284782e-06 to 1.4284782e-06
- layer_square: float32 [2, 10627584], P(None, 'fsdp'), may hold values from 1.2753436e-13 to 5.1013745e-13
- root_flat: float32 [10108928], P('fsdp'), may hold values from -0.21875 to 0.21875
- root_mean: float32 [10108928], P('fsdp'), may hold values from -1.4284782e-06 to 1.4284782e-06
- root_square: float32 [10108928], P('fsdp'), may hold values from 4.0810996e-12 to 1.6324398e-11
Outputs:
- loss_sum: float32 [], replicated
- grad_norm: float32 [], replicated
- activation_rms: float32 [2, 3], replicated
- new_layer: float32 [2, 10627584], P(None, 'fsdp')
- new_layer_mean: float32 [2, 10627584], P(None, 'fsdp')
- new_layer_square: float32 [2, 10627584], P(None, 'fsdp')
- new_root: float32 [10108928], P('fsdp')
- new_root_mean: float32 [10108928], P('fsdp')
- new_root_square: float32 [10108928], P('fsdp')
Inputs may be any that keep to these rules, and one draw needn't show every extreme that they name: `times`: sample s has its time in [s / 64, (s + 1) / 64).
All inputs are finite; a program needn't handle non-finite values. No bound on the sum of `dropped` on one device may be relied on, other than what follows from the above.
Results may differ from a plain program's by a relative error of at most 0.0052.
Values may be sent and summed in bfloat16 or wider, within the bound.
A program may use at most 704 MiB of HBM per device.

v0:
```python
import functools
import math

import jax
import jax.numpy as jnp
from jax import lax
from jax.experimental import pallas as pl
from jax.experimental.pallas import tpu as pltpu
from jax.sharding import PartitionSpec as P

D = 768
HD = 64
FF = 3072
PD = 16
CLS = 1001
PH = 2048
ZD = 768
FREQ = 256
GRID = 16
LAYERS = 2
DEPTH_Z = 2
STEP = 10
SEQ = 256


norm_eps = 1e-06
clip_limit = 0.002
learn_rate = 0.08
beta_one = 0.5
beta_two = 0.5
adam_eps = 1e-08
decay_rate = 0.01
proj_coeff = 0.5
low_type = jnp.bfloat16
full_type = jnp.float32


LANES = 128
ROWS = 16
UNIT = LANES * ROWS
MESH = pl.DeviceIdType.MESH

def up(value, step):
    return -(-value // step) * step

class Plan:
    def __init__(self, layout, length, devices):
        self.length = length
        self.devices = devices
        self.share = length // devices
        self.segments = []
        offset = units = 0
        for shape in layout:
            amount = math.prod(shape)
            matrix = len(shape) == 2 and shape[0] % ROWS == 0 and shape[1] % LANES == 0
            chunks = shape[1] // LANES if matrix else 1
            count = up(amount, UNIT) // UNIT
            self.segments.append((offset // LANES, chunks, count, units, shape, matrix))
            offset += amount
            units += count
        self.units = units
        self.per = up(up(units, devices) // devices, 4)
        rows_of = []
        for base, chunks, count, _, _, _ in self.segments:
            for u in range(count):
                b, c = divmod(u, chunks)
                first = base + b * ROWS * chunks + c
                rows_of.append((first, first + (ROWS - 1) * chunks))
        before = after = 0
        for d in range(devices):
            start, stop = d * self.share // LANES, (d + 1) * self.share // LANES
            for lo, hi in rows_of[self.per * d : self.per * d + self.per]:
                before, after = max(before, start - lo), max(after, hi + 1 - stop)
        self.before, self.after = up(before, 8), up(after, 8)
        units_before = units_after = 0
        for u, (lo, hi) in enumerate(rows_of):
            first = lo * LANES // self.share
            last = min(((hi + 1) * LANES - 1) // self.share, devices - 1)
            for d in range(first, last + 1):
                units_before = max(units_before, self.per * d - u)
                units_after = max(units_after, u + 1 - self.per * d - self.per)
        self.units_before, self.units_after = units_before, units_after
        self.half = self.per // 2
        self.raw = up(up(self.share, LANES) // LANES + 9, 64)
        self.ext = self.before + self.raw + self.after
        margin = tail = 0
        for d in range(devices):
            start = d * self.share // LANES
            lo = max(self.per * d - units_before, 0)
            for first, last in rows_of[lo : self.per * d + self.per + units_after]:
                margin, tail = max(margin, start - first), max(tail, last + 1 - start)
        self.margin = up(margin, 8)
        self.spread = up(max(tail, self.raw + 8), 8) + self.margin
        least = self.share // LANES
        self.fits = max(self.before, self.after) < least and max(units_before, units_after) < self.per

def place(index, zs):
    return index // 8, index // 4 % 2, index // 2 % 2, index % 2

def gather_kernel(plans, zs, *refs):
    nb = len(plans)
    raw_hbm = refs[:nb]
    outs = refs[nb : 2 * nb]
    raw, ext, tail, from_prev, from_next, slots = (refs[2 * nb + i * nb : 3 * nb + i * nb] for i in range(6))
    rest = refs[8 * nb :]
    load_sem, halo_send, halo_recv, own_sem, send_sem, zr, xa, xb, yb, ya, cr = rest
    n = zs * 8
    me = lax.axis_index("fsdp")
    z, y, x, c = place(me, zs)
    index = lambda zz, yy, xx, cc: ((zz * 2 + yy) * 2 + xx) * 2 + cc
    prev, following = lax.rem(me + n - 1, n), lax.rem(me + 1, n)
    xpeer, ypeer, cpeer = index(z, y, 1 - x, c), index(z, 1 - y, x, c), index(z, y, x, 1 - c)
    zpeer = [index(lax.rem(z + k, zs), y, x, c) for k in range(zs)]
    loads = []
    for b in range(nb):
        p = plans[b]
        loads.append(pltpu.make_async_copy(raw_hbm[b], raw[b].at[pl.ds(8, p.raw)], load_sem.at[b]))
        loads[b].start()
    barrier = pltpu.get_barrier_semaphore()
    peers = [prev, following, xpeer, ypeer, cpeer] + zpeer[1:]
    for peer in peers:
        pl.semaphore_signal(barrier, inc=1, device_id=(peer,), device_id_type=MESH)
    halos = []
    lane = lax.broadcasted_iota(jnp.int32, (64, LANES), 1)
    for b in range(nb):
        p = plans[b]
        shift = lax.rem(me * p.share, LANES)
        delta = (me + 1) * p.share // LANES - me * p.share // LANES
        raw[b][pl.ds(0, 8), :] = jnp.zeros((8, LANES), full_type)
        ext[b][pl.ds(0, p.before), :] = jnp.zeros((p.before, LANES), full_type)
        ext[b][pl.ds(p.before + p.raw, p.after), :] = jnp.zeros((p.after, LANES), full_type)
        loads[b].wait()

        def align(i, carry):
            row = pl.multiple_of(i * 64, 64)
            here = pltpu.roll(raw[b][pl.ds(row + 8, 64), :], shift, 1)
            above = pltpu.roll(raw[b][pl.ds(row + 7, 64), :], shift, 1)
            ext[b][pl.ds(row + p.before, 64), :] = jnp.where(lane >= shift, here, above)
            return carry

        lax.fori_loop(0, p.raw // 64, align, 0)
        tail[b][...] = ext[b][pl.ds(delta, p.before + 8), :]
        if b == 0:
            pl.semaphore_wait(barrier, len(peers))
        for s, (src, dst, to) in enumerate(((ext[b].at[pl.ds(p.before, p.after)], from_next[b], prev), (tail[b], from_prev[b], following))):
            copy = pltpu.make_async_remote_copy(src, dst, halo_send.at[2 * b + s], halo_recv.at[2 * b + s], device_id=(to,), device_id_type=MESH)
            copy.start()
            halos.append(copy)
    sends = []

    def send(src, dst, sem, to):
        copy = pltpu.make_async_remote_copy(src, dst, send_sem.at[len(sends)], sem, device_id=(to,), device_id_type=MESH)
        copy.start()
        sends.append(copy)

    def span(b, h):
        p = plans[b]
        return (0, p.half) if h == 0 else (p.half, p.per - p.half)

    def slot(k, dy, dx, dc):
        return index(lax.rem(z + zs - k, zs), 1 - y if dy else y, 1 - x if dx else x, 1 - c if dc else c)

    def part(b, h, k, dy, dx, dc=0):
        first, count = span(b, h)
        return outs[b].at[pl.ds(slot(k, dy, dx, dc) * plans[b].per + first, count)]

    def whole(b, k, dy, dx, dc=0):
        return outs[b].at[pl.ds(slot(k, dy, dx, dc) * plans[b].per, plans[b].per)]

    def arrived(ref, sem):
        pltpu.make_async_copy(ref, ref, sem).wait()

    owns = []
    for b in range(nb):
        p = plans[b]
        delta = (me + 1) * p.share // LANES - me * p.share // LANES
        for copy in halos[2 * b : 2 * b + 2]:
            copy.wait()
        ext[b][pl.ds(0, p.before + 8), :] += from_prev[b][...]
        ext[b][pl.ds(p.before + delta, p.after), :] += from_next[b][...]
        top = me * p.share // LANES - p.before
        for base, chunks, count, first_unit, _, _ in p.segments:
            lo = jnp.clip(p.per * me - first_unit, 0, count)
            hi = jnp.clip(p.per * me + p.per - first_unit, 0, count)

            def unit(u, carry):
                block = u // chunks
                row = base + block * (ROWS * chunks) + (u - block * chunks) - top
                if chunks == 1:
                    value = ext[b][pl.ds(row, ROWS), :]
                else:
                    value = ext[b][pl.ds(row, ROWS, stride=chunks), :]
                slots[b][first_unit + u - p.per * me] = value.astype(low_type)
                return carry

            lax.fori_loop(lo, hi, unit, 0)
        own = pltpu.make_async_copy(slots[b], whole(b, 0, 0, 0), own_sem.at[b])
        own.start()
        owns.append(own)
        mine = lambda h: slots[b].at[pl.ds(*span(b, h))]
        for k in range(1, zs):
            for h in range(2):
                send(mine(h), part(b, h, 0, 0, 0), zr.at[b, h, k], zpeer[k])
        send(mine(0), part(b, 0, 0, 0, 0), xa.at[b, 0], xpeer)
        send(mine(1), part(b, 1, 0, 0, 0), yb.at[b, 0], ypeer)
        send(mine(0), part(b, 0, 0, 0, 0), ya.at[b, 0, 0], ypeer)
        send(mine(1), part(b, 1, 0, 0, 0), xb.at[b, 0, 0], xpeer)
        send(slots[b], whole(b, 0, 0, 0), cr.at[b, 0, 0, 0], cpeer)
    for b in range(nb):
        for k in range(1, zs):
            arrived(part(b, 0, k, 0, 0), zr.at[b, 0, k])
            send(part(b, 0, k, 0, 0), part(b, 0, k, 0, 0), xa.at[b, k], xpeer)
            arrived(part(b, 1, k, 0, 0), zr.at[b, 1, k])
            send(part(b, 1, k, 0, 0), part(b, 1, k, 0, 0), yb.at[b, k], ypeer)
            send(part(b, 0, k, 0, 0), part(b, 0, k, 0, 0), ya.at[b, k, 0], ypeer)
            send(part(b, 1, k, 0, 0), part(b, 1, k, 0, 0), xb.at[b, k, 0], xpeer)
            send(whole(b, k, 0, 0), whole(b, k, 0, 0), cr.at[b, k, 0, 0], cpeer)
        for k in range(zs):
            arrived(part(b, 0, k, 0, 1), xa.at[b, k])
            send(part(b, 0, k, 0, 1), part(b, 0, k, 0, 1), ya.at[b, k, 1], ypeer)
            arrived(part(b, 1, k, 1, 0), yb.at[b, k])
            send(part(b, 1, k, 1, 0), part(b, 1, k, 1, 0), xb.at[b, k, 1], xpeer)
        for k in range(zs):
            arrived(part(b, 1, k, 0, 1), xb.at[b, k, 0])
            send(whole(b, k, 0, 1), whole(b, k, 0, 1), cr.at[b, k, 0, 1], cpeer)
            arrived(part(b, 0, k, 1, 0), ya.at[b, k, 0])
            send(whole(b, k, 1, 0), whole(b, k, 1, 0), cr.at[b, k, 1, 0], cpeer)
        for k in range(zs):
            arrived(part(b, 1, k, 1, 1), xb.at[b, k, 1])
            arrived(part(b, 0, k, 1, 1), ya.at[b, k, 1])
            send(whole(b, k, 1, 1), whole(b, k, 1, 1), cr.at[b, k, 1, 1], cpeer)
    for b in range(nb):
        owns[b].wait()
        for k in range(zs):
            for dy in range(2):
                for dx in range(2):
                    arrived(whole(b, k, dy, dx, 1), cr.at[b, k, dy, dx])
    for copy in sends:
        copy.wait_send()

def gather_units(plans, raws):
    n = plans[0].devices
    zs = n // 8
    nb = len(plans)
    per_bucket = 2 * (zs - 1) + 10 * zs
    dma = pltpu.SemaphoreType.DMA
    scratch = [pltpu.VMEM((p.raw + 8, LANES), full_type) for p in plans]
    scratch += [pltpu.VMEM((p.ext, LANES), full_type) for p in plans]
    scratch += [pltpu.VMEM((p.before + 8, LANES), full_type) for p in plans]
    scratch += [pltpu.VMEM((p.before + 8, LANES), full_type) for p in plans]
    scratch += [pltpu.VMEM((p.after, LANES), full_type) for p in plans]
    scratch += [pltpu.VMEM((p.per, ROWS, LANES), low_type) for p in plans]
    scratch += [dma((nb,)), dma((2 * nb,)), dma((2 * nb,)), dma((nb,)), dma((nb * per_bucket,))]
    scratch += [dma((nb, 2, zs)), dma((nb, zs)), dma((nb, zs, 2)), dma((nb, zs)), dma((nb, zs, 2)), dma((nb, zs, 2, 2))]
    return pl.pallas_call(
        functools.partial(gather_kernel, plans, zs),
        out_shape=[jax.ShapeDtypeStruct((n * p.per, ROWS, LANES), low_type) for p in plans],
        in_specs=[pl.BlockSpec(memory_space=pl.ANY)] * nb,
        out_specs=[pl.BlockSpec(memory_space=pl.ANY)] * nb,
        scratch_shapes=scratch,
        compiler_params=pltpu.CompilerParams(collective_id=0, has_side_effects=True, vmem_limit_bytes=48 * 1024 * 1024),
        name="gather_units",
    )(*raws)

def reduce_kernel(plans, zs, *refs):
    nb = len(plans)
    take = lambda count: tuple(next(feed) for _ in range(count))
    feed = iter(refs)
    grads, (stats_in,) = take(nb), take(1)
    outs, (stats_out,), first = take(nb), take(1), take(nb)
    kept_a, kept_b, two_a, two_b, three_a, three_b, four = (take(nb) for _ in range(7))
    local, other = take(1)[0], take(1)[0]
    units_f, rows_f, flat_f = take(1)[0], take(1)[0], take(1)[0]
    from_prev, from_next = take(nb), take(nb)
    total, total_in = take(1)[0], take(1)[0]
    s1, r1, s2a, r2a, s2b, r2b, s3a, r3a, s3b, r3b, s4, r4, load_sem, halo_s, halo_r, out_sem, ss, sr = take(18)
    n = zs * 8
    me = lax.axis_index("fsdp")
    z, y, x, c = place(me, zs)
    index = lambda zz, yy, xx, cc: ((zz * 2 + yy) * 2 + xx) * 2 + cc
    prev, following = lax.rem(me + n - 1, n), lax.rem(me + 1, n)
    xpeer, ypeer, cpeer = index(z, y, 1 - x, c), index(z, 1 - y, x, c), index(z, y, x, 1 - c)
    below = lambda k: index(lax.rem(z + zs - k, zs), y, x, c)
    above = lambda k: index(lax.rem(z + k, zs), y, x, c)
    barrier = pltpu.get_barrier_semaphore()
    peers = [prev, following, xpeer, ypeer, cpeer] + [above(k) for k in range(1, zs)]
    for peer in peers:
        pl.semaphore_signal(barrier, inc=1, device_id=(peer,), device_id_type=MESH)
    pl.semaphore_wait(barrier, len(peers))

    def remote(src, dst, send_sem, recv_sem, to):
        return pltpu.make_async_remote_copy(src, dst, send_sem, recv_sem, device_id=(to,), device_id_type=MESH)

    def arrived(ref, sem):
        pltpu.make_async_copy(ref, ref, sem).wait()

    def slot(b, k, dy, dx, dc):
        where = index(lax.rem(z + zs - k, zs), 1 - y if dy else y, 1 - x if dx else x, 1 - c if dc else c)
        return grads[b].at[pl.ds(where * plans[b].per, plans[b].per)]

    order = ((1, 1), (1, 0), (0, 1), (0, 0))

    def sibling(b, k, dy, dx):
        return remote(slot(b, k, dy, dx, 1), first[b].at[k, dy, dx], s1.at[b, k, dy, dx], r1.at[b, k, dy, dx], cpeer)

    for b in range(nb):
        for dy, dx in order:
            for k in range(zs):
                sibling(b, k, dy, dx).start()

    def add(p, dst, at, one, one_at, two, two_at):
        step = p.half // 2

        def body(i, carry):
            span = lambda ref, off: ref[pl.ds(off + i * step, step)].astype(full_type)
            dst[pl.ds(at + i * step, step)] = (span(one, one_at) + span(two, two_at)).astype(low_type)
            return carry

        lax.fori_loop(0, 2, body, 0)

    ring = local.shape[0]
    used = []

    def send_of(b, h, k, dy, dx, src):
        if h == 0:
            return remote(src, two_a[b].at[k, dx], s2a.at[b, k, dx], r2a.at[b, k, dx], ypeer)
        return remote(src, two_b[b].at[k, dy], s2b.at[b, k, dy], r2b.at[b, k, dy], xpeer)

    steps = [(b, dy, dx, k) for b in range(nb) for dy, dx in order for k in range(zs)]

    def loads(number):
        b, dy, dx, k = steps[number]
        at = number % ring
        p = plans[b]
        one = pltpu.make_async_copy(slot(b, k, dy, dx, 0), local.at[at, pl.ds(0, p.per)], load_sem.at[at, 0])
        two = pltpu.make_async_copy(first[b].at[k, dy, dx], other.at[number % 2, pl.ds(0, p.per)], load_sem.at[at, 1])
        return one, two

    pending = {}

    def prepare(number):
        b, dy, dx, k = steps[number]
        for copy in pending.pop(number % ring, ()):
            copy.wait_send()
        one, two = loads(number)
        one.start()
        arrived(first[b].at[k, dy, dx], r1.at[b, k, dy, dx])
        two.start()

    def phase_one(number):
        b, dy, dx, k = steps[number]
        p = plans[b]
        at = number % ring
        if number == 0:
            prepare(0)
        if number + 1 < len(steps):
            prepare(number + 1)
        for copy in loads(number):
            copy.wait()
        mine, theirs = local.at[at], other.at[number % 2]
        going = []
        if dy:
            add(p, mine, 0, mine, 0, theirs, 0)
            going.append(send_of(b, 0, k, dy, dx, local.at[at, pl.ds(0, p.half)]))
        else:
            add(p, kept_a[b].at[k, dx], 0, mine, 0, theirs, 0)
        if dx:
            add(p, mine, p.half, mine, p.half, theirs, p.half)
            going.append(send_of(b, 1, k, dy, dx, local.at[at, pl.ds(p.half, p.half)]))
        else:
            add(p, kept_b[b].at[k, dy], 0, mine, p.half, theirs, p.half)
        for copy in going:
            copy.start()
        pending[at] = going

    def three(b, h, k):
        if h == 0:
            return remote(two_a[b].at[k, 1], three_a[b].at[k], s3a.at[b, k], r3a.at[b, k], xpeer)
        return remote(two_b[b].at[k, 1], three_b[b].at[k], s3b.at[b, k], r3b.at[b, k], ypeer)

    def last(b, h, k):
        src = (three_a if h == 0 else three_b)[b].at[k]
        return remote(src, four[b].at[h, k - 1], s4.at[b, h, k - 1], r4.at[b, h, k - 1], below(k))

    def phase_two(b):
        p = plans[b]
        for far in (1, 0):
            for k in range(zs):
                for h, kept, two, sem in ((0, kept_a, two_a, r2a), (1, kept_b, two_b, r2b)):
                    arrived(two[b].at[k, far], sem.at[b, k, far])
                    if far:
                        add(p, two[b].at[k, 1], 0, two[b].at[k, 1], 0, kept[b].at[k, 1], 0)
                        three(b, h, k).start()
                    else:
                        add(p, kept[b].at[k, 0], 0, two[b].at[k, 0], 0, kept[b].at[k, 0], 0)

    def phase_three(b):
        p = plans[b]
        for k in list(range(1, zs)) + [0]:
            for h, kept, got, sem in ((0, kept_a, three_a, r3a), (1, kept_b, three_b, r3b)):
                arrived(got[b].at[k], sem.at[b, k])
                if k:
                    add(p, got[b].at[k], 0, got[b].at[k], 0, kept[b].at[k, 0], 0)
                    last(b, h, k).start()

    def finish(b):
        p = plans[b]
        base = p.units_before
        for h, kept, got in ((0, kept_a, three_a), (1, kept_b, three_b)):
            for k in range(1, zs):
                arrived(four[b].at[h, k - 1], r4.at[b, h, k - 1])
            step = p.half // 2

            def body(i, carry):
                part = pl.ds(i * step, step)
                value = kept[b][0, 0, part].astype(full_type) + got[b][0, part].astype(full_type)
                for k in range(1, zs):
                    value = value + four[b][h, k - 1, part].astype(full_type)
                units_f[pl.ds(base + h * p.half + i * step, step)] = value
                return carry

            lax.fori_loop(0, 2, body, 0)
        forward = remote(units_f.at[pl.ds(p.per, base)], from_prev[b], halo_s.at[b, 0], halo_r.at[b, 0], following)
        backward = remote(units_f.at[pl.ds(base, p.units_after)], from_next[b], halo_s.at[b, 1], halo_r.at[b, 1], prev)
        forward.start()
        backward.start()
        forward.wait()
        backward.wait()
        units_f[pl.ds(0, base)] = from_prev[b][...]
        units_f[pl.ds(base + p.per, p.units_after)] = from_next[b][...]
        top = me * p.share // LANES - p.margin
        for origin, chunks, count, first_unit, _, _ in p.segments:
            lo = jnp.clip(p.per * me - base - first_unit, 0, count)
            hi = jnp.clip(p.per * me + p.per + p.units_after - first_unit, 0, count)

            def unit(u, carry):
                block = u // chunks
                row = origin + block * (ROWS * chunks) + (u - block * chunks) - top
                value = units_f[first_unit + u - p.per * me + base]
                if chunks == 1:
                    rows_f[pl.ds(row, ROWS), :] = value
                else:
                    rows_f[pl.ds(row, ROWS, stride=chunks), :] = value
                return carry

            lax.fori_loop(lo, hi, unit, 0)
        shift = lax.rem(me * p.share, LANES)
        turn = lax.rem(LANES - shift, LANES)
        lane = lax.broadcasted_iota(jnp.int32, (64, LANES), 1)
        spot = lax.broadcasted_iota(jnp.int32, (64, LANES), 0) * LANES + lane
        if b:
            pltpu.make_async_copy(flat_f.at[pl.ds(0, plans[b - 1].raw)], outs[b - 1], out_sem.at[b - 1]).wait()

        def unalign(i, squares):
            row = pl.multiple_of(i * 64, 64)
            here = pltpu.roll(rows_f[pl.ds(row + p.margin, 64), :], turn, 1)
            below_row = pltpu.roll(rows_f[pl.ds(row + p.margin + 1, 64), :], turn, 1)
            value = jnp.where(lane < LANES - shift, here, below_row)
            value = jnp.where(spot + row * LANES < p.share, value, 0.0)
            flat_f[pl.ds(row, 64), :] = value
            return squares + jnp.sum((value * value).reshape(8, 8, LANES), axis=0)

        squares = lax.fori_loop(0, p.raw // 64, unalign, jnp.zeros((8, LANES), full_type))
        pltpu.make_async_copy(flat_f.at[pl.ds(0, p.raw)], outs[b], out_sem.at[b]).start()
        return squares

    per_bucket = 4 * zs
    for b in range(nb):
        for number in range(b * per_bucket, (b + 1) * per_bucket):
            phase_one(number)
        if b:
            phase_two(b - 1)
            phase_three(b - 1)
    phase_two(nb - 1)
    phase_three(nb - 1)
    squares = jnp.zeros((8, LANES), full_type)
    for b in range(nb):
        squares = squares + finish(b)
    pltpu.make_async_copy(flat_f.at[pl.ds(0, plans[nb - 1].raw)], outs[nb - 1], out_sem.at[nb - 1]).wait()
    total[0] = stats_in[...]
    total[1] = squares
    step = 0
    for to in ((cpeer,), (xpeer,), (ypeer,), tuple(above(k) for k in range(1, zs))):
        copies = []
        for peer in to:
            copies.append(remote(total, total_in.at[step], ss.at[step], sr.at[step], peer))
            copies[-1].start()
            step += 1
        for copy in copies:
            copy.wait()
        value = total[...]
        for i in range(len(to)):
            value = value + total_in[step - 1 - i]
        total[...] = value
    stats_out[...] = total[...]
    for group in pending.values():
        for copy in group:
            copy.wait_send()
    for b in range(nb):
        for dy, dx in order:
            for k in range(zs):
                sibling(b, k, dy, dx).wait_send()
        for h in range(2):
            for k in range(zs):
                three(b, h, k).wait_send()
                if k:
                    last(b, h, k).wait_send()

def reduce_units(plans, grads, stats):
    n = plans[0].devices
    zs = n // 8
    nb = len(plans)
    dma = pltpu.SemaphoreType.DMA
    most = max(p.per for p in plans)
    tile = (ROWS, LANES)
    half = lambda p, *lead: pltpu.VMEM(lead + (p.half,) + tile, low_type)
    scratch = [half(p, zs, 2) for p in plans] + [half(p, zs, 2) for p in plans]
    scratch += [half(p, zs, 2) for p in plans] + [half(p, zs, 2) for p in plans]
    scratch += [half(p, zs) for p in plans] + [half(p, zs) for p in plans]
    scratch += [half(p, 2, zs - 1) for p in plans]
    ring = 4
    scratch += [pltpu.VMEM((ring, most) + tile, low_type), pltpu.VMEM((2, most) + tile, low_type)]
    scratch += [pltpu.VMEM((max(p.units_before + p.per + p.units_after for p in plans),) + tile, full_type)]
    scratch += [pltpu.VMEM((max(p.spread for p in plans), LANES), full_type)]
    scratch += [pltpu.VMEM((max(p.raw for p in plans), LANES), full_type)]
    scratch += [pltpu.VMEM((p.units_before,) + tile, full_type) for p in plans]
    scratch += [pltpu.VMEM((p.units_after,) + tile, full_type) for p in plans]
    hops = 2 + zs
    scratch += [pltpu.VMEM((2, 8, LANES), full_type), pltpu.VMEM((hops, 2, 8, LANES), full_type)]
    scratch += [dma((nb, zs, 2, 2))] * 2 + [dma((nb, zs, 2))] * 4 + [dma((nb, zs))] * 4
    scratch += [dma((nb, 2, zs - 1))] * 2 + [dma((ring, 2)), dma((nb, 2)), dma((nb, 2)), dma((nb,)), dma((hops,)), dma((hops,))]
    anywhere = pl.BlockSpec(memory_space=pl.ANY)
    inside = pl.BlockSpec(memory_space=pltpu.VMEM)
    out_shape = [jax.ShapeDtypeStruct((p.raw, LANES), full_type) for p in plans]
    out_shape += [jax.ShapeDtypeStruct((2, 8, LANES), full_type)]
    out_shape += [jax.ShapeDtypeStruct((zs, 2, 2, p.per) + tile, low_type) for p in plans]
    results = pl.pallas_call(
        functools.partial(reduce_kernel, plans, zs),
        out_shape=out_shape,
        in_specs=[anywhere] * nb + [inside],
        out_specs=[anywhere] * nb + [inside] + [anywhere] * nb,
        scratch_shapes=scratch,
        compiler_params=pltpu.CompilerParams(collective_id=1, has_side_effects=True, vmem_limit_bytes=62 * 1024 * 1024),
        name="reduce_units",
    )(*grads, stats)
    return results[:nb], results[nb]

def to_rows(flat, plan):
    padded = jnp.pad(flat, ((0, plan.raw * LANES - flat.shape[0]),))
    return padded.reshape(plan.raw, LANES)


def layer_layout():
    return [
        (D, 3 * D),
        (D, D),
        (D, FF),
        (FF, D),
        (D, 6 * D),
        (D,),
        (D,),
        (D,),
        (FF,),
        (D,),
        (6 * D,),
    ]


def root_layout():
    return [
        (PD, D),
        (D,),
        (FREQ, D),
        (D,),
        (D, D),
        (D,),
        (CLS, D),
        (D, PH),
        (PH,),
        (PH, PH),
        (PH,),
        (PH, ZD),
        (ZD,),
        (D, 2 * D),
        (2 * D,),
        (D, PD),
        (PD,),
    ]


def unflatten(vector, layout):
    pieces = []
    offset = 0
    for dimensions in layout:
        amount = math.prod(dimensions)
        pieces.append(vector[offset : offset + amount].reshape(dimensions))
        offset += amount
    return pieces


def flatten_grads(grad_list, length):
    joined = jnp.concatenate([piece.reshape(-1) for piece in grad_list])
    return jnp.concatenate([joined, jnp.zeros((length - joined.shape[0],), full_type)])


def position_table():
    quarter = D // 4
    frequency = 1.0 / 10000.0 ** (jnp.arange(quarter, dtype=jnp.float32) / quarter)
    coords = jnp.arange(GRID, dtype=jnp.float32)
    angles = coords[:, None] * frequency[None, :]
    one_axis = jnp.concatenate([jnp.sin(angles), jnp.cos(angles)], axis=1)
    row_part = jnp.repeat(one_axis, GRID, axis=0)
    col_part = jnp.tile(one_axis, (GRID, 1))
    return jnp.concatenate([row_part, col_part], axis=1)


def time_features(times_in):
    half_freq = FREQ // 2
    frequency = jnp.exp(-math.log(10000.0) * jnp.arange(half_freq, dtype=jnp.float32) / half_freq)
    angles = times_in[:, None] * frequency[None, :]
    return jnp.concatenate([jnp.cos(angles), jnp.sin(angles)], axis=1)


def modulated_norm(values, offsets, scales):
    centred = values - jnp.mean(values, axis=-1, keepdims=True)
    spread = jnp.mean(centred * centred, axis=-1, keepdims=True)
    return centred * lax.rsqrt(spread + norm_eps) * (1.0 + scales) + offsets


def softmax_rows(scores):
    row_max = jnp.max(scores, axis=-1, keepdims=True)
    exponent = jnp.exp(scores - row_max)
    return exponent / jnp.sum(exponent, axis=-1, keepdims=True)


def gelu_tanh(values):
    return jax.nn.gelu(values, approximate=True)


def cosine_rows(predicted, target):
    target_full = target.astype(full_type)
    inner_sum = jnp.sum(predicted * target_full, axis=-1)
    return (
        inner_sum
        * lax.rsqrt(jnp.sum(predicted * predicted, axis=-1) + norm_eps)
        * lax.rsqrt(jnp.sum(target_full * target_full, axis=-1) + norm_eps)
    )


def silu_back(values, grad_in):
    _, pullback = jax.vjp(jax.nn.silu, values)
    return pullback(grad_in)[0]


def linear_fwd(inputs, weight):
    leading = inputs.shape[:-1]
    product = jnp.dot(
        inputs.reshape(-1, inputs.shape[-1]), weight, preferred_element_type=full_type
    )
    return product.reshape(leading + (weight.shape[1],))


def linear_back(inputs, weight, grad_out, with_input=True):
    rows_in = inputs.reshape(-1, inputs.shape[-1])
    rows_out = grad_out.reshape(-1, grad_out.shape[-1])
    grad_weight = lax.dot_general(
        rows_in, rows_out, (((0,), (0,)), ((), ())), preferred_element_type=full_type
    )
    grad_bias = jnp.sum(rows_out.astype(full_type), axis=0)
    grad_in = None
    if with_input:
        grad_in = lax.dot_general(
            rows_out, weight, (((1,), (1,)), ((), ())), preferred_element_type=full_type
        ).reshape(inputs.shape)
    return (grad_in, grad_weight, grad_bias)


def layer_forward(weights, residual, modulator):
    (
        w_attn_in,
        w_attn_out,
        w_mlp_in,
        w_mlp_out,
        w_modulate,
        b_query,
        b_value,
        b_attn_out,
        b_mlp_in,
        b_mlp_out,
        b_modulate,
    ) = weights
    samples_mb, seq_len = (residual.shape[0], residual.shape[1])
    head_count = D // HD
    modulation = jnp.split((linear_fwd(modulator, w_modulate) + b_modulate)[:, None, :], 6, axis=-1)
    normed_a = modulated_norm(residual, modulation[0], modulation[1]).astype(low_type)
    bias_qkv = jnp.concatenate([b_query, jnp.zeros_like(b_query), b_value])
    qkv_low = (linear_fwd(normed_a, w_attn_in) + bias_qkv).astype(low_type)
    qkv_low = qkv_low.reshape(samples_mb, seq_len, 3, head_count, HD)
    query_bf, key_bf, value_bf = (qkv_low[:, :, 0], qkv_low[:, :, 1], qkv_low[:, :, 2])
    scores = jnp.einsum(
        "bqhd,bkhd->bhqk", query_bf, key_bf, preferred_element_type=full_type
    ) * HD ** (-0.5)
    attn_probs = softmax_rows(scores)
    probs_bf = attn_probs.astype(low_type)
    heads_bf = jnp.einsum("bhqk,bkhd->bqhd", probs_bf, value_bf, preferred_element_type=full_type)
    heads_bf = heads_bf.astype(low_type).reshape(samples_mb, seq_len, D)
    attn_out = linear_fwd(heads_bf, w_attn_out) + b_attn_out
    middle = residual + modulation[2] * attn_out
    normed_m = modulated_norm(middle, modulation[3], modulation[4]).astype(low_type)
    mlp_pre = linear_fwd(normed_m, w_mlp_in) + b_mlp_in
    act_bf = gelu_tanh(mlp_pre).astype(low_type)
    mlp_out = linear_fwd(act_bf, w_mlp_out) + b_mlp_out
    residual_out = middle + modulation[5] * mlp_out
    square_sums = jnp.stack(
        [
            jnp.sum(residual_out * residual_out),
            jnp.sum(attn_out * attn_out),
            jnp.sum(mlp_out * mlp_out),
        ]
    )
    saved = (
        modulation,
        normed_a,
        query_bf,
        key_bf,
        value_bf,
        attn_probs,
        probs_bf,
        heads_bf,
        attn_out,
        middle,
        normed_m,
        mlp_pre,
        act_bf,
        mlp_out,
    )
    return (residual_out, saved, square_sums)


def layer_backward(weights, saved, residual, modulator, grad_out):
    w_attn_in, w_attn_out, w_mlp_in, w_mlp_out, w_modulate = weights[:5]
    (
        modulation,
        normed_a,
        query_bf,
        key_bf,
        value_bf,
        attn_probs,
        probs_bf,
        heads_bf,
        attn_out,
        middle,
        normed_m,
        mlp_pre,
        act_bf,
        mlp_out,
    ) = saved
    samples_mb, seq_len = (residual.shape[0], residual.shape[1])
    grad_mlp = (modulation[5] * grad_out).astype(low_type)
    grad_act, grad_w_mlp_out, grad_b_mlp_out = linear_back(act_bf, w_mlp_out, grad_mlp)
    _, gelu_pull = jax.vjp(gelu_tanh, mlp_pre)
    grad_pre = gelu_pull(grad_act)[0].astype(low_type)
    grad_normed_m, grad_w_mlp_in, grad_b_mlp_in = linear_back(normed_m, w_mlp_in, grad_pre)
    _, norm_pull_m = jax.vjp(modulated_norm, middle, modulation[3], modulation[4])
    grad_from_m, grad_shift_m, grad_scale_m = norm_pull_m(grad_normed_m)
    grad_middle = grad_out + grad_from_m
    grad_attn = (modulation[2] * grad_middle).astype(low_type)
    grad_heads, grad_w_attn_out, grad_b_attn_out = linear_back(heads_bf, w_attn_out, grad_attn)
    grad_heads_bf = grad_heads.astype(low_type).reshape(samples_mb, seq_len, D // HD, HD)
    grad_probs = jnp.einsum(
        "bqhd,bkhd->bhqk", grad_heads_bf, value_bf, preferred_element_type=full_type
    )
    grad_value = jnp.einsum(
        "bhqk,bqhd->bkhd", probs_bf, grad_heads_bf, preferred_element_type=full_type
    )
    grad_scores = attn_probs * (
        grad_probs - jnp.sum(attn_probs * grad_probs, axis=-1, keepdims=True)
    )
    grad_scores = grad_scores.astype(low_type)
    grad_query = jnp.einsum(
        "bhqk,bkhd->bqhd", grad_scores, key_bf, preferred_element_type=full_type
    ) * HD ** (-0.5)
    grad_key = jnp.einsum(
        "bhqk,bqhd->bkhd", grad_scores, query_bf, preferred_element_type=full_type
    ) * HD ** (-0.5)
    grad_qkv = jnp.stack([grad_query, grad_key, grad_value], axis=2).reshape(
        samples_mb, seq_len, 3 * D
    )
    grad_normed_a, grad_w_attn_in, grad_b_qkv = linear_back(
        normed_a, w_attn_in, grad_qkv.astype(low_type)
    )
    _, norm_pull_a = jax.vjp(modulated_norm, residual, modulation[0], modulation[1])
    grad_from_a, grad_shift_a, grad_scale_a = norm_pull_a(grad_normed_a)
    grad_gate_a = jnp.sum(attn_out * grad_middle, axis=1, keepdims=True)
    grad_gate_m = jnp.sum(mlp_out * grad_out, axis=1, keepdims=True)
    grad_mod = jnp.concatenate(
        [grad_shift_a, grad_scale_a, grad_gate_a, grad_shift_m, grad_scale_m, grad_gate_m], axis=-1
    )[:, 0, :].astype(low_type)
    grad_cond, grad_w_mod, grad_b_mod = linear_back(modulator, w_modulate, grad_mod)
    grad_list = [
        grad_w_attn_in,
        grad_w_attn_out,
        grad_w_mlp_in,
        grad_w_mlp_out,
        grad_w_mod,
        grad_b_qkv[:D],
        grad_b_qkv[2 * D :],
        grad_b_attn_out,
        grad_b_mlp_in,
        grad_b_mlp_out,
        grad_b_mod,
    ]
    return (grad_middle + grad_from_a, grad_cond, grad_list)


def embed_forward(pieces, latent_part, noise_part, times_part, labels_part, dropped_part):
    mixing = times_part[:, None, None]
    noisy_bf = ((1.0 - mixing) * latent_part + mixing * noise_part).astype(low_type)
    tokens = linear_fwd(noisy_bf, pieces[0]) + pieces[1] + position_table()
    basis_bf = time_features(times_part).astype(low_type)
    time_pre = linear_fwd(basis_bf, pieces[2]) + pieces[3]
    time_act = jax.nn.silu(time_pre).astype(low_type)
    time_emb = linear_fwd(time_act, pieces[4]) + pieces[5]
    classes = jnp.where(dropped_part == 1, CLS - 1, labels_part)
    onehot = (classes[:, None] == jnp.arange(CLS, dtype=jnp.int32)[None, :]).astype(low_type)
    condition = time_emb + jnp.dot(onehot, pieces[6], preferred_element_type=full_type)
    saved = (noisy_bf, basis_bf, time_pre, time_act, onehot, condition)
    return (tokens, jax.nn.silu(condition).astype(low_type), saved)


def embed_backward(pieces, saved, grad_tokens, grad_modulator):
    noisy_bf, basis_bf, time_pre, time_act, onehot, condition = saved
    grad_cond = silu_back(condition, grad_modulator)
    grad_table = lax.dot_general(
        onehot.astype(full_type),
        grad_cond,
        (((0,), (0,)), ((), ())),
        precision=lax.Precision.HIGHEST,
    )
    grad_time_act, grad_w_time_out, grad_b_time_out = linear_back(
        time_act, pieces[4], grad_cond.astype(low_type)
    )
    grad_time_pre = silu_back(time_pre, grad_time_act).astype(low_type)
    _, grad_w_time_in, grad_b_time_in = linear_back(basis_bf, pieces[2], grad_time_pre, False)
    _, grad_w_patch, grad_b_patch = linear_back(
        noisy_bf, pieces[0], grad_tokens.astype(low_type), False
    )
    return [
        grad_w_patch,
        grad_b_patch,
        grad_w_time_in,
        grad_b_time_in,
        grad_w_time_out,
        grad_b_time_out,
        grad_table,
    ]


def projector_forward(pieces, residual, features_part):
    residual_bf = residual.astype(low_type)
    pre_a = linear_fwd(residual_bf, pieces[7]) + pieces[8]
    act_a = jax.nn.silu(pre_a).astype(low_type)
    pre_b = linear_fwd(act_a, pieces[9]) + pieces[10]
    act_b = jax.nn.silu(pre_b).astype(low_type)
    predicted = linear_fwd(act_b, pieces[11]) + pieces[12]
    loss_part = -proj_coeff * jnp.sum(cosine_rows(predicted, features_part)) / residual.shape[1]
    return (loss_part, (residual_bf, pre_a, act_a, pre_b, act_b, predicted))


def projector_backward(pieces, saved, features_part, seq_len, sample_total):
    residual_bf, pre_a, act_a, pre_b, act_b, predicted = saved
    _, cosine_pull = jax.vjp(
        lambda predicted_in: cosine_rows(predicted_in, features_part), predicted
    )
    seed = jnp.full(predicted.shape[:2], -proj_coeff / (seq_len * sample_total), full_type)
    grad_pred = cosine_pull(seed)[0].astype(low_type)
    grad_act_b, grad_w_c, grad_b_c = linear_back(act_b, pieces[11], grad_pred)
    grad_pre_b = silu_back(pre_b, grad_act_b).astype(low_type)
    grad_act_a, grad_w_b, grad_b_b = linear_back(act_a, pieces[9], grad_pre_b)
    grad_pre_a = silu_back(pre_a, grad_act_a).astype(low_type)
    grad_residual, grad_w_a, grad_b_a = linear_back(residual_bf, pieces[7], grad_pre_a)
    return (grad_residual, [grad_w_a, grad_b_a, grad_w_b, grad_b_b, grad_w_c, grad_b_c])


def head_forward(pieces, residual, modulator, target, weight_t):
    modulation = (linear_fwd(modulator, pieces[13]) + pieces[14])[:, None, :]
    shift_f, scale_f = jnp.split(modulation, 2, axis=-1)
    normed = modulated_norm(residual, shift_f, scale_f).astype(low_type)
    deviation = linear_fwd(normed, pieces[15]) + pieces[16] - target
    loss_part = jnp.sum(weight_t * jnp.mean(deviation * deviation, axis=(1, 2)))
    return (loss_part, (shift_f, scale_f, normed, deviation))


def head_backward(pieces, saved, residual, modulator, weight_t, sample_total):
    shift_f, scale_f, normed, deviation = saved
    scaled = (
        2.0 * weight_t[:, None, None] / (deviation.shape[1] * deviation.shape[2] * sample_total)
    )
    grad_output = (scaled * deviation).astype(low_type)
    grad_normed, grad_w_head, grad_b_head = linear_back(normed, pieces[15], grad_output)
    _, pullback = jax.vjp(modulated_norm, residual, shift_f, scale_f)
    grad_residual, grad_shift, grad_scale = pullback(grad_normed)
    grad_mod = jnp.concatenate([grad_shift, grad_scale], axis=-1)[:, 0, :].astype(low_type)
    grad_cond, grad_w_mod, grad_b_mod = linear_back(modulator, pieces[13], grad_mod)
    return (grad_residual, grad_cond, [grad_w_mod, grad_b_mod, grad_w_head, grad_b_head])


def from_units(units, plan):
    pieces = []
    for _, chunks, count, first, shape, matrix in plan.segments:
        part = units[first : first + count]
        if matrix:
            part = part.reshape(shape[0] // ROWS, chunks, ROWS, LANES).transpose(0, 2, 1, 3)
            pieces.append(part.reshape(shape))
        else:
            pieces.append(part.reshape(-1)[: math.prod(shape)].reshape(shape))
    return pieces


def into_units(grad_list, plan):
    parts = []
    for grad, (_, chunks, count, _, shape, matrix) in zip(grad_list, plan.segments):
        low = grad.astype(low_type)
        if matrix:
            low = low.reshape(shape[0] // ROWS, ROWS, chunks, LANES).transpose(0, 2, 1, 3)
            parts.append(low.reshape(count, ROWS, LANES))
        else:
            flat = jnp.pad(low.reshape(-1), ((0, count * UNIT - low.size),))
            parts.append(flat.reshape(count, ROWS, LANES))
    missing = plan.devices * plan.per - plan.units
    parts.append(jnp.zeros((missing, ROWS, LANES), low_type))
    return jnp.concatenate(parts)


def model_step(layer_lists, pieces, latents, noise, times, labels, dropped, features, devices):
    sample_total = latents.shape[0] * devices
    residual, modulator, embed_saved = embed_forward(
        pieces, latents, noise, times, labels, dropped
    )
    loss_total = jnp.zeros((), full_type)
    inputs, kept, square_sums = [], [], []
    for ordinal in range(LAYERS):
        inputs.append(residual)
        residual, saved, sums = layer_forward(layer_lists[ordinal], residual, modulator)
        kept.append(saved)
        square_sums.append(sums)
        if ordinal + 1 == DEPTH_Z:
            part, proj_saved = projector_forward(pieces, residual, features)
            loss_total = loss_total + part
    target = noise - latents
    weight_t = 1.0 + 2.0 * times
    part, head_saved = head_forward(pieces, residual, modulator, target, weight_t)
    loss_total = loss_total + part
    grad_residual, grad_cond, head_grads = head_backward(
        pieces, head_saved, residual, modulator, weight_t, sample_total
    )
    layer_grads = [None] * LAYERS
    for ordinal in reversed(range(LAYERS)):
        if ordinal + 1 == DEPTH_Z:
            grad_proj, proj_grads = projector_backward(
                pieces, proj_saved, features, residual.shape[1], sample_total
            )
            grad_residual = grad_residual + grad_proj
        grad_residual, cond_part, layer_grads[ordinal] = layer_backward(
            layer_lists[ordinal], kept[ordinal], inputs[ordinal], modulator, grad_residual
        )
        grad_cond = grad_cond + cond_part
    embed_grads = embed_backward(pieces, embed_saved, grad_residual, grad_cond)
    return (loss_total, jnp.stack(square_sums), layer_grads, embed_grads + proj_grads + head_grads)


def adam_update(weight, grad, first, second, clip_factor):
    clipped = grad * clip_factor
    first_new = beta_one * first + (1.0 - beta_one) * clipped
    second_new = beta_two * second + (1.0 - beta_two) * clipped * clipped
    first_hat = first_new / (1.0 - beta_one**STEP)
    second_hat = second_new / (1.0 - beta_two**STEP)
    weight_new = weight - learn_rate * (
        first_hat / (jnp.sqrt(second_hat) + adam_eps) + decay_rate * weight
    )
    return (weight_new, first_new, second_new)


def by_kernels(plan, root_plan, layer_flat, root_flat, data, devices):
    plans = (root_plan,) + (plan,) * LAYERS
    raws = [to_rows(root_flat, root_plan)]
    raws += [to_rows(layer_flat[ordinal], plan) for ordinal in range(LAYERS)]
    gathered = gather_units(plans, raws)
    pieces = from_units(gathered[0], root_plan)
    layer_lists = [from_units(units, plan) for units in gathered[1:]]
    loss_part, square_sums, layer_grads, root_grads = model_step(
        layer_lists, pieces, *data, devices
    )
    grads = [into_units(root_grads, root_plan)]
    grads += [into_units(grad_list, plan) for grad_list in layer_grads]
    numbers = jnp.concatenate([loss_part[None], square_sums.reshape(-1)])
    stats = jnp.pad(numbers, (0, 8 * LANES - numbers.shape[0])).reshape(8, LANES)
    rows, stats = reduce_units(plans, grads, stats)
    numbers = stats[0].reshape(-1)
    shard_root = rows[0].reshape(-1)[: root_plan.share]
    shard_layers = jnp.stack([r.reshape(-1)[: plan.share] for r in rows[1:]])
    sums = numbers[1 : 1 + 3 * LAYERS].reshape(LAYERS, 3)
    return (shard_layers, shard_root, numbers[0], sums, jnp.sum(stats[1]))


def by_collectives(layer_flat, root_flat, data, devices):
    whole = lambda part: lax.all_gather(part.astype(low_type), "fsdp", axis=0, tiled=True)
    layer_lists = [unflatten(whole(layer_flat[i]), layer_layout()) for i in range(LAYERS)]
    pieces = unflatten(whole(root_flat), root_layout())
    loss_part, square_sums, layer_grads, root_grads = model_step(
        layer_lists, pieces, *data, devices
    )

    def owned(grad_list, share):
        joined = jnp.concatenate([piece.reshape(-1) for piece in grad_list])
        joined = jnp.pad(joined, (0, share * devices - joined.shape[0]))
        return lax.psum_scatter(joined, "fsdp", scatter_dimension=0, tiled=True)

    shard_layers = jnp.stack([owned(grads, layer_flat.shape[1]) for grads in layer_grads])
    shard_root = owned(root_grads, root_flat.shape[0])
    local = jnp.sum(shard_layers * shard_layers) + jnp.sum(shard_root * shard_root)
    loss_sum, sums, square_total = lax.psum((loss_part, square_sums, local), "fsdp")
    return (shard_layers, shard_root, loss_sum, sums, square_total)


def shards(
    latents,
    noise,
    times,
    labels,
    dropped,
    features,
    layer_flat,
    layer_mean,
    layer_square,
    root_flat,
    root_mean,
    root_square,
):
    devices = lax.axis_size("fsdp")
    data = (latents, noise, times, labels, dropped, features)
    plan = Plan(layer_layout(), layer_flat.shape[1] * devices, devices)
    root_plan = Plan(root_layout(), root_flat.shape[0] * devices, devices)
    if devices % 8 == 0 and plan.fits and root_plan.fits:
        reduced = by_kernels(plan, root_plan, layer_flat, root_flat, data, devices)
    else:
        reduced = by_collectives(layer_flat, root_flat, data, devices)
    shard_layers, shard_root, loss_sum, stream_sums, square_total = reduced
    sample_total = latents.shape[0] * devices
    grad_norm = jnp.sqrt(square_total)
    clip_factor = clip_limit / jnp.maximum(grad_norm, clip_limit)
    activation_rms = jnp.sqrt(stream_sums / (sample_total * SEQ * D))
    new_layer, new_layer_mean, new_layer_square = adam_update(
        layer_flat, shard_layers, layer_mean, layer_square, clip_factor
    )
    new_root, new_root_mean, new_root_square = adam_update(
        root_flat, shard_root, root_mean, root_square, clip_factor
    )
    return (
        loss_sum,
        grad_norm,
        activation_rms,
        new_layer,
        new_layer_mean,
        new_layer_square,
        new_root,
        new_root_mean,
        new_root_square,
    )


def solution(mesh):
    in_specs = (
        P("fsdp", None, None),
        P("fsdp", None, None),
        P("fsdp"),
        P("fsdp"),
        P("fsdp"),
        P("fsdp", None, None),
        P(None, "fsdp"),
        P(None, "fsdp"),
        P(None, "fsdp"),
        P("fsdp"),
        P("fsdp"),
        P("fsdp"),
    )
    out_specs = (
        P(),
        P(),
        P(),
        P(None, "fsdp"),
        P(None, "fsdp"),
        P(None, "fsdp"),
        P("fsdp"),
        P("fsdp"),
        P("fsdp"),
    )
    return jax.shard_map(shards, mesh=mesh, in_specs=in_specs, out_specs=out_specs, check_vma=False)
```

profile of v0, /device:TPU:6, one launch (start us, length us, event | category | flops | bytes accessed | tf_op | source)
XLA Modules:
  0.0 1543.3 jit_solution(8788477043647360462)
XLA Ops:
  4.6 13.9 slice_reduce_fusion
  18.8 290.0 %gather_units.1 = (bf16[4992,16,128]{2,1,0:T(8,128)(2,1)}, bf16[5248,16,128]{2,1,0:T(8,128)(2,1)}, bf16[5248,16,128]{2,1,0:T(8,128)(2,1)}) custom-call(f32[2496,128]{1,0:T(8,128)S(1)} %pad_bitcast_fusion.2.refs_0_, f32[2624,128]{1,0:T(8,128)S(1)} %get-tuple-element.183.refs_1_, f32[2624,128]{1,0:T(8,128)S(1)} %get-tuple-element.182.refs_2_), custom_call_target="tpu_custom_call" | custom-call | tf_op jit(solution)/shard_map/gather_units/pallas_call | solution.py:255
  350.7 7.2 reshape.1071
  363.9 7.2 reshape.1075
  377.6 7.8 slice.289
  385.4 10.9 copy.183
  396.3 13.3 reshape.1082
  425.5 7.7 reshape.1083
  433.2 7.3 slice.250
  450.0 8.6 reshape.1073
  464.7 9.2 copy.339
  474.0 10.9 reshape.1074
  514.3 8.8 fusion.200
  533.6 8.4 reshape.1077
  548.2 9.2 copy.338
  557.4 10.9 reshape.1078
  651.8 9.5 fusion.212
  667.8 8.4 fusion.215
  716.8 7.8 reshape.1003
  729.2 10.8 reshape.1041
  753.3 7.1 fusion.42
  760.4 10.0 copy.267
  770.5 11.1 copy.203
  812.3 6.6 fusion.214
  872.3 11.1 reshape.1020
  927.6 7.2 reshape.1013
  948.5 12.3 reshape.1026
  960.9 7.7 copy.217
  973.5 12.2 reshape.1047
  1000.5 8.0 constant_dynamic-update-slice_fusion.65
  1046.6 460.4 %reduce_units.1 = (f32[2496,128]{1,0:T(8,128)}, f32[2624,128]{1,0:T(8,128)}, f32[2624,128]{1,0:T(8,128)}, f32[2,8,128]{2,1,0:T(8,128)}, bf16[4,2,2,156,16,128]{5...) custom-call(bf16[4992,16,128]{2,1,0:T(8,128)(2,1)} %constant_dynamic-update-s, ...), custom_call_target="tpu_custom_call" | custom-call | tf_op jit(solution)/shard_map/reduce_units/pallas_call | solution.py:537
  1529.1 12.7 multiply_subtract_fusion
  (777 shorter events, 502.2 us)
Async XLA Ops:
  1.5 338.3 %copy-start.168 = (s32[2]{0:T(128)}, s32[2]{0:T(128)S(1)}, u32[]{:S(2)}) copy-start(s32[2]{0:T(128)S(1)} %compare_select_fusion) | copy-start | bytes 28
  3.3 317.6 %copy-start.159 = (bf16[2,128]{1,0:T(2,128)(2,1)}, bf16[2,128]{1,0:T(2,128)(2,1)S(1)}, u32[]{:S(2)}) copy-start(bf16[2,128]{1,0:T(2,128)(2,1)S(1)} %get-tuple-element.140) | copy-start | bytes 1540
  3.3 317.6 %copy-start.161 = (bf16[2,128]{1,0:T(2,128)(2,1)}, bf16[2,128]{1,0:T(2,128)(2,1)S(1)}, u32[]{:S(2)}) copy-start(bf16[2,128]{1,0:T(2,128)(2,1)S(1)} %get-tuple-element.141) | copy-start | bytes 1540
  4.2 316.9 %copy-start.66 = (bf16[2,256,16]{1,2,0:T(8,128)(2,1)}, bf16[2,256,16]{1,2,0:T(8,128)(2,1)S(1)}, u32[]{:S(2)}) copy-start(bf16[2,256,16]{1,2,0:T(8,128)(2,1)S(1)} %add_convert_fusion.6) | copy-start | bytes 49156
  309.5 204.6 %copy-start.136 = (f32[3072]{0:T(1024)}, f32[3072]{0:T(1024)S(1)}, u32[]{:S(2)}) copy-start(f32[3072]{0:T(1024)S(1)} %slice_convert_fusion.3) | copy-start | bytes 36868
  321.6 185.0 %copy-start.2 = (f32[2,256,768]{2,1,0:T(8,128)}, f32[2,256,768]{2,1,0:T(8,128)S(1)}, u32[]{:S(2)}) copy-start(f32[2,256,768]{2,1,0:T(8,128)S(1)} %get-tuple-element.145) | copy-start | bytes 4718596
  321.6 163.2 %copy-start.93 = (f32[2,256]{1,0:T(2,128)}, f32[2,256]{1,0:T(2,128)S(1)}, u32[]{:S(2)}) copy-start(f32[2,256]{1,0:T(2,128)S(1)} %broadcast_multiply_fusion.4) | copy-start | bytes 6148
  322.0 162.9 %copy-start.117 = (f32[2,256]{1,0:T(2,128)}, f32[2,256]{1,0:T(2,128)S(1)}, u32[]{:S(2)}) copy-start(f32[2,256]{1,0:T(2,128)S(1)} %fusion.172) | copy-start | bytes 6148
  340.2 272.0 %copy-start.62 = (f32[2,768]{1,0:T(2,128)}, f32[2,768]{1,0:T(2,128)S(1)}, u32[]{:S(2)}) copy-start(f32[2,768]{1,0:T(2,128)S(1)} %convolution_add_fusion.8) | copy-start | bytes 18436
  464.7 20.2 %copy-start.91 = (f32[2,768]{1,0:T(2,128)}, f32[2,768]{1,0:T(2,128)S(1)}, u32[]{:S(2)}) copy-start(f32[2,768]{1,0:T(2,128)S(1)} %get-tuple-element.123) | copy-start | bytes 18436
  464.7 20.1 %copy-start.149 = (f32[2,768]{1,0:T(2,128)}, f32[2,768]{1,0:T(2,128)S(1)}, u32[]{:S(2)}) copy-start(f32[2,768]{1,0:T(2,128)S(1)} %get-tuple-element.122) | copy-start | bytes 18436
  464.7 41.9 %copy-start.82 = (f32[2,768]{1,0:T(2,128)}, f32[2,768]{1,0:T(2,128)S(1)}, u32[]{:S(2)}) copy-start(f32[2,768]{1,0:T(2,128)S(1)} %get-tuple-element.124) | copy-start | bytes 18436
  464.7 44.3 %copy-start.80 = (f32[2,768]{1,0:T(2,128)}, f32[2,768]{1,0:T(2,128)S(1)}, u32[]{:S(2)}) copy-start(f32[2,768]{1,0:T(2,128)S(1)} %get-tuple-element.119) | copy-start | bytes 18436
  464.7 44.3 %copy-start.151 = (f32[2,768]{1,0:T(2,128)}, f32[2,768]{1,0:T(2,128)S(1)}, u32[]{:S(2)}) copy-start(f32[2,768]{1,0:T(2,128)S(1)} %get-tuple-element.120) | copy-start | bytes 18436
  464.7 49.4 %copy-start.113 = (f32[2,768]{1,0:T(2,128)}, f32[2,768]{1,0:T(2,128)S(1)}, u32[]{:S(2)}) copy-start(f32[2,768]{1,0:T(2,128)S(1)} %get-tuple-element.121) | copy-start | bytes 18436
  497.0 17.2 %slice-start.32 = ((s8[4718592]{0:T(1024)(128)(4,1)}), s8[4194304]{0:T(1024)(128)(4,1)S(1)}, s32[]{:S(2)}) async-start(s8[4718592]{0:T(1024)(128)(4,1)} %bitcast.659), calls=%async_computation.32 | async-start | bytes 8388608
  523.1 67.1 %copy-start.7 = (f32[2,256,768]{2,1,0:T(8,128)}, f32[2,256,768]{2,1,0:T(8,128)S(1)}, u32[]{:S(2)}) copy-start(f32[2,256,768]{2,1,0:T(8,128)S(1)} %get-tuple-element.87) | copy-start | bytes 4718596
  523.1 45.2 %copy-start.101 = (f32[2,256]{1,0:T(2,128)}, f32[2,256]{1,0:T(2,128)S(1)}, u32[]{:S(2)}) copy-start(f32[2,256]{1,0:T(2,128)S(1)} %broadcast_multiply_fusion.2) | copy-start | bytes 6148
  523.5 44.8 %copy-start.132 = (f32[2,256]{1,0:T(2,128)}, f32[2,256]{1,0:T(2,128)S(1)}, u32[]{:S(2)}) copy-start(f32[2,256]{1,0:T(2,128)S(1)} %fusion.174) | copy-start | bytes 6148
  548.2 20.1 %copy-start.89 = (f32[2,768]{1,0:T(2,128)}, f32[2,768]{1,0:T(2,128)S(1)}, u32[]{:S(2)}) copy-start(f32[2,768]{1,0:T(2,128)S(1)} %get-tuple-element.117) | copy-start | bytes 18436
  548.2 20.1 %copy-start.153 = (f32[2,768]{1,0:T(2,128)}, f32[2,768]{1,0:T(2,128)S(1)}, u32[]{:S(2)}) copy-start(f32[2,768]{1,0:T(2,128)S(1)} %get-tuple-element.116) | copy-start | bytes 18436
  548.2 42.0 %copy-start.86 = (f32[2,768]{1,0:T(2,128)}, f32[2,768]{1,0:T(2,128)S(1)}, u32[]{:S(2)}) copy-start(f32[2,768]{1,0:T(2,128)S(1)} %get-tuple-element.118) | copy-start | bytes 18436
  548.2 44.4 %copy-start.84 = (f32[2,768]{1,0:T(2,128)}, f32[2,768]{1,0:T(2,128)S(1)}, u32[]{:S(2)}) copy-start(f32[2,768]{1,0:T(2,128)S(1)} %get-tuple-element.115) | copy-start | bytes 18436
  548.2 44.4 %copy-start.155 = (f32[2,768]{1,0:T(2,128)}, f32[2,768]{1,0:T(2,128)S(1)}, u32[]{:S(2)}) copy-start(f32[2,768]{1,0:T(2,128)S(1)} %get-tuple-element.114) | copy-start | bytes 18436
  548.2 48.3 %copy-start.157 = (f32[2,768]{1,0:T(2,128)}, f32[2,768]{1,0:T(2,128)S(1)}, u32[]{:S(2)}) copy-start(f32[2,768]{1,0:T(2,128)S(1)} %get-tuple-element.113) | copy-start | bytes 18436
  661.4 20.8 %slice-start.30 = ((s8[4718592]{0:T(1024)(128)(4,1)}), s8[4194304]{0:T(1024)(128)(4,1)S(1)}, s32[]{:S(2)}) async-start(s8[4718592]{0:T(1024)(128)(4,1)} %bitcast.651), calls=%async_computation.30 | async-start | bytes 8388608
  760.4 21.1 %slice-start.6 = ((s8[6291456]{0:T(1024)(128)(4,1)}), s8[4194304]{0:T(1024)(128)(4,1)S(1)}, s32[]{:S(2)}) async-start(s8[6291456]{0:T(1024)(128)(4,1)} %bitcast.582), calls=%async_computation.6 | async-start | bytes 8388608
  806.7 17.9 %slice-start.26 = ((s8[4718592]{0:T(1024)(128)(4,1)}), s8[4194304]{0:T(1024)(128)(4,1)S(1)}, s32[]{:S(2)}) async-start(s8[4718592]{0:T(1024)(128)(4,1)} %bitcast.647), calls=%async_computation.26 | async-start | bytes 8388608
  872.3 17.7 %slice-start.4 = ((s8[6291456]{0:T(1024)(128)(4,1)}), s8[2097152]{0:T(1024)(128)(4,1)S(1)}, s32[]{:S(2)}) async-start(s8[6291456]{0:T(1024)(128)(4,1)} %bitcast.580), calls=%async_computation.4 | async-start | bytes 4194304
  973.5 20.3 %slice-start.16 = ((s8[4718592]{0:T(1024)(128)(4,1)}), s8[524288]{0:T(1024)(128)(4,1)S(1)}, s32[]{:S(2)}) async-start(s8[4718592]{0:T(1024)(128)(4,1)} %bitcast.593), calls=%async_computation.16 | async-start | bytes 1048576
  1014.6 19.8 %slice-start = ((s8[8388608]{0:T(1024)(128)(4,1)}), s8[4194304]{0:T(1024)(128)(4,1)S(1)}, s32[]{:S(2)}) async-start(s8[8388608]{0:T(1024)(128)(4,1)} %bitcast.567), calls=%async_computation | async-start | bytes 8388608
  1017.5 16.9 %slice-start.1 = ((s8[8388608]{0:T(1024)(128)(4,1)}), s8[4194304]{0:T(1024)(128)(4,1)S(1)}, s32[]{:S(2)}) async-start(s8[8388608]{0:T(1024)(128)(4,1)} %bitcast.567), calls=%async_computation.1 | async-start | bytes 8388608
  (194 other events, 950.1 us)
where the time goes:
time: 1560 us; the launch traced here: 1540 us
  Pallas kernels  750 us (48%)
  local copies, waits for them, and re-layouts  495 us (32%)
  matrix products  215 us (14%)
  other arithmetic  75.9 us (5%)
    pallas_call x1, Pallas kernels, reduce_units(): pl.pallas_call(functools.partial(reduce_kernel, plans, zs), out_shape=out...  460 us
    pallas_call x1, Pallas kernels, gather_units(): pl.pallas_call(functools.partial(gather_kernel, plans, zs), out_shape=[ja...  290 us
    reshape x17, local copies, waits for them, and re-layouts, into_units(): low.reshape(shape[0] // ROWS, ROWS, chunks, LANES).transpose(0, 2, 1, 3)  97.6 us
    unnamed x517, local copies, waits for them, and re-layouts  87.1 us
    reshape x12, local copies, waits for them, and re-layouts, from_units(): pieces.append(part.reshape(shape))  84.6 us
    dot_general x16, matrix products, linear_back(): lax.dot_general(rows_out, weight, (((1,), (1,)), ((), ())), preferred_ele...  68.3 us
    dot_general x18, matrix products, linear_back(): lax.dot_general(rows_in, rows_out, (((0,), (0,)), ((), ())), preferred_el...  60.2 us
    dot_general x18, matrix products, linear_fwd(): jnp.dot(inputs.reshape(-1, inputs.shape[-1]), weight, preferred_element_t...  52.9 us

commit v1 on v0

--- a/solution.py
+++ b/solution.py
@@ -905,31 +905,689 @@
     return (grad_residual, grad_cond, [grad_w_mod, grad_b_mod, grad_w_head, grad_b_head])
 
 
-def from_units(units, plan):
-    pieces = []
-    for _, chunks, count, first, shape, matrix in plan.segments:
-        part = units[first : first + count]
-        if matrix:
-            part = part.reshape(shape[0] // ROWS, chunks, ROWS, LANES).transpose(0, 2, 1, 3)
-            pieces.append(part.reshape(shape))
-        else:
-            pieces.append(part.reshape(-1)[: math.prod(shape)].reshape(shape))
-    return pieces
-
-
-def into_units(grad_list, plan):
-    parts = []
-    for grad, (_, chunks, count, _, shape, matrix) in zip(grad_list, plan.segments):
-        low = grad.astype(low_type)
-        if matrix:
-            low = low.reshape(shape[0] // ROWS, ROWS, chunks, LANES).transpose(0, 2, 1, 3)
-            parts.append(low.reshape(count, ROWS, LANES))
-        else:
-            flat = jnp.pad(low.reshape(-1), ((0, count * UNIT - low.size),))
-            parts.append(flat.reshape(count, ROWS, LANES))
-    missing = plan.devices * plan.per - plan.units
-    parts.append(jnp.zeros((missing, ROWS, LANES), low_type))
-    return jnp.concatenate(parts)
+WIDE = 2 * LANES
+HEADS = D // HD
+CHUNK = 64
+MB = 1024 * 1024
+
+
+def dot(one, two):
+    return jnp.dot(one, two, preferred_element_type=full_type)
+
+
+def dot_nt(one, two):
+    return lax.dot_general(one, two, (((1,), (1,)), ((), ())), preferred_element_type=full_type)
+
+
+def dot_tn(one, two):
+    return lax.dot_general(one, two, (((0,), (0,)), ((), ())), preferred_element_type=full_type)
+
+
+def block_of(w, block, blocks, chunk, chunks):
+    pieces = [w[pl.ds(block, blocks), chunk + i].reshape(blocks * ROWS, LANES) for i in range(chunks)]
+    return jnp.concatenate(pieces, axis=1) if chunks > 1 else pieces[0]
+
+
+def put_block(out, block, chunk, value):
+    blocks = value.shape[0] // ROWS
+    for i in range(value.shape[1] // LANES):
+        piece = value[:, i * LANES : (i + 1) * LANES].astype(low_type)
+        out[pl.ds(block, blocks), chunk + i] = piece.reshape(blocks, ROWS, LANES)
+
+
+def loop(count, body):
+    lax.fori_loop(0, count, lambda i, carry: (body(i), carry)[1], 0)
+
+
+def norm_parts(values):
+    centred = values - jnp.mean(values, axis=-1, keepdims=True)
+    spread = jnp.mean(centred * centred, axis=-1, keepdims=True)
+    scale = lax.rsqrt(spread + norm_eps)
+    return centred * scale, scale
+
+
+def norm_back(values, grad, gain):
+    hat, scale = norm_parts(values)
+    inner = grad * gain
+    mean_a = jnp.mean(inner, axis=-1, keepdims=True)
+    mean_b = jnp.mean(inner * hat, axis=-1, keepdims=True)
+    return scale * (inner - mean_a - hat * mean_b), grad * hat
+
+
+def gelu_parts(values):
+    root = math.sqrt(2.0 / math.pi)
+    square = values * values
+    bend = jnp.tanh(root * values * (1.0 + 0.044715 * square))
+    half = 0.5 * (1.0 + bend)
+    slope = half + 0.5 * values * (1.0 - bend * bend) * root * (1.0 + 3.0 * 0.044715 * square)
+    return values * half, slope
+
+
+def rows_sum(values):
+    return jnp.sum(values, axis=0, keepdims=True)
+
+
+def segment_ref(units, plan, number):
+    _, chunks, count, first, shape, matrix = plan.segments[number]
+    part = units.at[pl.ds(first, count)]
+    if not matrix:
+        return part
+    return part.reshape(shape[0] // ROWS, chunks, ROWS, LANES)
+
+
+def segment_scratch(plan, number):
+    _, chunks, _, _, shape, _ = plan.segments[number]
+    return pltpu.VMEM((shape[0] // ROWS, chunks, ROWS, LANES), low_type)
+
+
+def attention_pairs(rows):
+    return (rows // SEQ) * (HEADS // 2)
+
+
+def head_masks():
+    lane = lax.broadcasted_iota(jnp.int32, (SEQ, LANES), 1)
+    return lane < HD
+
+
+def softmax_f32(scores):
+    exponent = jnp.exp(scores - jnp.max(scores, axis=-1, keepdims=True))
+    return exponent * (1.0 / jnp.sum(exponent, axis=-1, keepdims=True))
+
+
+def mods_kernel(plan, modulator, bias, units, out, w, sem):
+    load = pltpu.make_async_copy(segment_ref(units, plan, 4), w, sem)
+    load.start()
+    load.wait()
+    value = modulator[...]
+
+    def body(j):
+        cols = pl.ds(pl.multiple_of(j * WIDE, WIDE), WIDE)
+        out[:, cols] = dot(value, block_of(w, 0, D // ROWS, 2 * j, 2)) + bias[:, cols]
+
+    loop(6 * D // WIDE, body)
+
+
+def mods_call(plan, modulator, bias, units):
+    vm = pl.BlockSpec(memory_space=pltpu.VMEM)
+    return pl.pallas_call(
+        functools.partial(mods_kernel, plan),
+        out_shape=jax.ShapeDtypeStruct((modulator.shape[0], 6 * D), full_type),
+        in_specs=[vm, vm, pl.BlockSpec(memory_space=pl.ANY)],
+        out_specs=vm,
+        scratch_shapes=[segment_scratch(plan, 4), pltpu.SemaphoreType.DMA],
+        compiler_params=pltpu.CompilerParams(vmem_limit_bytes=32 * MB),
+        name="modulation",
+    )(modulator, bias, units)
+
+
+def mods_back_kernel(plan, modulator, grad, units, before, grads, cond, w, dw, sem):
+    load = pltpu.make_async_copy(segment_ref(units, plan, 4), w, sem.at[0])
+    load.start()
+    turned = modulator[...].astype(full_type).T.astype(low_type)
+
+    def weight(j):
+        cols = pl.ds(pl.multiple_of(j * WIDE, WIDE), WIDE)
+        put_block(dw, 0, 2 * j, dot(turned, grad[:, cols]))
+
+    loop(6 * D // WIDE, weight)
+    store = pltpu.make_async_copy(dw, segment_ref(grads, plan, 4), sem.at[1])
+    store.start()
+    load.wait()
+    cond[...] = jnp.zeros(cond.shape, full_type)
+
+    def back(j):
+        cols = pl.ds(pl.multiple_of(j * WIDE, WIDE), WIDE)
+        cond[...] += dot_nt(grad[:, cols], block_of(w, 0, D // ROWS, 2 * j, 2))
+
+    loop(6 * D // WIDE, back)
+    store.wait()
+
+
+def mods_back_call(plan, modulator, grad, units, grads):
+    vm = pl.BlockSpec(memory_space=pltpu.VMEM)
+    anywhere = pl.BlockSpec(memory_space=pl.ANY)
+    return pl.pallas_call(
+        functools.partial(mods_back_kernel, plan),
+        out_shape=[jax.ShapeDtypeStruct(grads.shape, low_type), jax.ShapeDtypeStruct((modulator.shape[0], D), full_type)],
+        in_specs=[vm, vm, anywhere, anywhere],
+        out_specs=[anywhere, vm],
+        input_output_aliases={3: 0},
+        scratch_shapes=[segment_scratch(plan, 4), segment_scratch(plan, 4), pltpu.SemaphoreType.DMA((2,))],
+        compiler_params=pltpu.CompilerParams(vmem_limit_bytes=40 * MB),
+        name="modulation_back",
+    )(modulator, grad, units, grads)
+
+
+SAVED = (("h1", D, low_type), ("qkv", 3 * D, low_type), ("heads", D, low_type), ("attn", D, full_type), ("middle", D, full_type), ("h2", D, low_type), ("pre", FF, full_type), ("mlp", D, full_type))
+
+
+def layer_forward_kernel(plan, rows, x, mod, bias_qkv, bias_o, bias_1, bias_2, units, out, sums, *refs):
+    ns = len(SAVED)
+    saved_out = refs[:ns]
+    h1, qkv, heads, attn, middle, h2, pre, mlp = refs[ns : 2 * ns]
+    w_qkv, w_o, w_1, w_2, load_sem, save_sem = refs[2 * ns :]
+    weights = (w_qkv, w_o, w_1, w_2)
+    loads = [pltpu.make_async_copy(segment_ref(units, plan, i), weights[i], load_sem.at[i]) for i in range(4)]
+    for copy in loads:
+        copy.start()
+    saves = [pltpu.make_async_copy(refs[ns + i], saved_out[i], save_sem.at[i]) for i in range(ns)]
+    part = lambda s, i: mod[pl.ds(s, 1), i * D : (i + 1) * D]
+    per = SEQ // CHUNK
+
+    def norm_a(i):
+        at = pl.ds(pl.multiple_of(i * CHUNK, CHUNK), CHUNK)
+        s = i // per
+        hat, _ = norm_parts(x[at, :])
+        h1[at, :] = (hat * (1.0 + part(s, 1)) + part(s, 0)).astype(low_type)
+
+    loop(rows // CHUNK, norm_a)
+    saves[0].start()
+    loads[0].wait()
+
+    def project(j):
+        cols = pl.ds(pl.multiple_of(j * WIDE, WIDE), WIDE)
+        value = dot(h1[...], block_of(w_qkv, 0, D // ROWS, 2 * j, 2)) + bias_qkv[:, cols]
+        qkv[:, cols] = value.astype(low_type)
+
+    loop(3 * D // WIDE, project)
+    saves[1].start()
+    first = head_masks()
+
+    def attend(i):
+        s, j = i // (HEADS // 2), i % (HEADS // 2)
+        at = pl.ds(pl.multiple_of(s * SEQ, SEQ), SEQ)
+        cut = lambda o: qkv[at, pl.ds(pl.multiple_of(o * D + j * LANES, LANES), LANES)]
+        q, k, v = cut(0), cut(1), cut(2)
+        q = q * jnp.asarray(HD ** (-0.5), low_type)
+        zero = jnp.zeros_like(q)
+        halves = []
+        for mask in (first, ~first):
+            probs = softmax_f32(dot_nt(jnp.where(mask, q, zero), k)).astype(low_type)
+            halves.append(dot(probs, v))
+        heads[at, pl.ds(pl.multiple_of(j * LANES, LANES), LANES)] = jnp.where(first, halves[0], halves[1]).astype(low_type)
+
+    loop(attention_pairs(rows), attend)
+    saves[2].start()
+    loads[1].wait()
+
+    def project_out(j):
+        cols = pl.ds(pl.multiple_of(j * WIDE, WIDE), WIDE)
+        attn[:, cols] = dot(heads[...], block_of(w_o, 0, D // ROWS, 2 * j, 2)) + bias_o[:, cols]
+
+    loop(D // WIDE, project_out)
+    saves[3].start()
+    zero_sum = jnp.zeros((1, D), full_type)
+
+    def norm_m(i, total):
+        at = pl.ds(pl.multiple_of(i * CHUNK, CHUNK), CHUNK)
+        s = i // per
+        value = attn[at, :]
+        mid = x[at, :] + part(s, 2) * value
+        middle[at, :] = mid
+        hat, _ = norm_parts(mid)
+        h2[at, :] = (hat * (1.0 + part(s, 4)) + part(s, 3)).astype(low_type)
+        return total + rows_sum(value * value)
+
+    attn_sum = lax.fori_loop(0, rows // CHUNK, norm_m, zero_sum)
+    saves[4].start()
+    saves[5].start()
+    loads[2].wait()
+    loads[3].wait()
+    mlp[...] = jnp.broadcast_to(bias_2[...], (rows, D))
+
+    def feed(j):
+        cols = pl.ds(pl.multiple_of(j * WIDE, WIDE), WIDE)
+        value = dot(h2[...], block_of(w_1, 0, D // ROWS, 2 * j, 2)) + bias_1[:, cols]
+        pre[:, cols] = value
+        act = gelu_parts(value)[0].astype(low_type)
+        mlp[...] += dot(act, block_of(w_2, j * (WIDE // ROWS), WIDE // ROWS, 0, D // LANES))
+
+    loop(FF // WIDE, feed)
+    saves[6].start()
+    saves[7].start()
+
+    def finish(i, carry):
+        at = pl.ds(pl.multiple_of(i * CHUNK, CHUNK), CHUNK)
+        value = mlp[at, :]
+        result = middle[at, :] + part(i // per, 5) * value
+        out[at, :] = result
+        return (carry[0] + rows_sum(result * result), carry[1] + rows_sum(value * value))
+
+    out_sum, mlp_sum = lax.fori_loop(0, rows // CHUNK, finish, (zero_sum, zero_sum))
+    sums[...] = jnp.zeros(sums.shape, full_type)
+    sums[0:1, :] = out_sum
+    sums[1:2, :] = attn_sum
+    sums[2:3, :] = mlp_sum
+    for copy in saves:
+        copy.wait()
+
+
+def layer_forward_call(plan, x, mod, biases, units):
+    rows = x.shape[0]
+    vm = pl.BlockSpec(memory_space=pltpu.VMEM)
+    anywhere = pl.BlockSpec(memory_space=pl.ANY)
+    dma = pltpu.SemaphoreType.DMA
+    shapes = [((rows, width), kind) for _, width, kind in SAVED]
+    results = pl.pallas_call(
+        functools.partial(layer_forward_kernel, plan, rows),
+        out_shape=[jax.ShapeDtypeStruct((rows, D), full_type), jax.ShapeDtypeStruct((8, D), full_type)]
+        + [jax.ShapeDtypeStruct(*s) for s in shapes],
+        in_specs=[vm] * 6 + [anywhere],
+        out_specs=[vm, vm] + [anywhere] * len(SAVED),
+        scratch_shapes=[pltpu.VMEM(*s) for s in shapes] + [segment_scratch(plan, i) for i in range(4)] + [dma((4,)), dma((len(SAVED),))],
+        compiler_params=pltpu.CompilerParams(vmem_limit_bytes=56 * MB),
+        name="layer_forward",
+    )(x, mod, *biases, units)
+    return results[0], results[1], results[2:]
+
+
+def layer_backward_kernel(plan, rows, x, grad_in, mod, *refs):
+    ns = len(SAVED)
+    saved_hbm = refs[:ns]
+    units, grad_out, grad_mod, bias_out, grads = refs[ns : ns + 5]
+    h1, qkv, heads, attn, middle, h2, pre, mlp = refs[ns + 5 : 2 * ns + 5]
+    w_qkv, w_o, w_1, w_2, d_qkv, g_low, wide, turned, dx, d_one, d_two, load_sem, save_sem, out_sem = refs[2 * ns + 5 :]
+    weights = (w_qkv, w_o, w_1, w_2)
+    inside = dict(zip(range(ns), refs[ns + 5 : 2 * ns + 5]))
+    saves = [pltpu.make_async_copy(saved_hbm[i], inside[i], save_sem.at[i]) for i in range(ns)]
+    loads = [pltpu.make_async_copy(segment_ref(units, plan, i), weights[i], load_sem.at[i]) for i in range(4)]
+    for copy in (saves[7], saves[6], loads[3], saves[5], loads[2], saves[4], saves[3], loads[1], saves[2], saves[1], loads[0], saves[0]):
+        copy.start()
+    part = lambda s, i: mod[pl.ds(s, 1), i * D : (i + 1) * D]
+    per = SEQ // CHUNK
+    grad_mod[...] = jnp.zeros(grad_mod.shape, full_type)
+    bias_out[...] = jnp.zeros(bias_out.shape, full_type)
+
+    def add_mod(s, i, value):
+        grad_mod[pl.ds(s, 1), i * D : (i + 1) * D] += value
+
+    def each_chunk(body):
+        loop(rows // CHUNK, lambda i: body(pl.ds(pl.multiple_of(i * CHUNK, CHUNK), CHUNK), i // per))
+
+    B_Q, B_V, B_O, B_1, B_2 = 0, D, 2 * D, 3 * D, 3 * D + FF
+    saves[7].wait()
+
+    def start_mlp(at, s):
+        grad = grad_in[at, :]
+        low = (part(s, 5) * grad).astype(low_type)
+        g_low[at, :] = low
+        bias_out[:, B_2 : B_2 + D] += rows_sum(low.astype(full_type))
+        add_mod(s, 5, rows_sum(mlp[at, :] * grad))
+
+    each_chunk(start_mlp)
+    saves[5].wait()
+    turned[...] = h2[...].astype(full_type).T.astype(low_type)
+    saves[6].wait()
+    loads[3].wait()
+    loads[2].wait()
+    dx[...] = jnp.zeros(dx.shape, full_type)
+    half = WIDE // ROWS
+
+    def outer(slot, segment, block, blocks, chunk, chunks, buffer):
+        target = segment_ref(grads, plan, segment).at[pl.ds(block, blocks), pl.ds(chunk, chunks)]
+        return pltpu.make_async_copy(buffer, target, out_sem.at[slot])
+
+    def mlp_store(j, kind):
+        at = j % 2
+        if kind == 0:
+            return outer(2 * at, 3, j * half, half, 0, D // LANES, d_one.at[at])
+        return outer(2 * at + 1, 2, 0, D // ROWS, 2 * j, 2, d_two.at[at])
+
+    def feed_back(j):
+        cols = pl.ds(pl.multiple_of(j * WIDE, WIDE), WIDE)
+        at = j % 2
+
+        @pl.when(j >= 2)
+        def _():
+            mlp_store(j - 2, 0).wait()
+            mlp_store(j - 2, 1).wait()
+
+        act, slope = gelu_parts(pre[:, cols])
+        grad_act = dot_nt(g_low[...], block_of(w_2, j * half, half, 0, D // LANES))
+        low = (grad_act * slope).astype(low_type)
+        wide[...] = low
+        bias_out[:, pl.ds(pl.multiple_of(B_1 + j * WIDE, WIDE), WIDE)] += rows_sum(low.astype(full_type))
+        put_block(d_one.at[at], 0, 0, dot_tn(act.astype(low_type), g_low[...]))
+        mlp_store(j, 0).start()
+        put_block(d_two.at[at], 0, 0, dot(turned[...], wide[...]))
+        mlp_store(j, 1).start()
+        dx[...] += dot_nt(wide[...], block_of(w_1, 0, D // ROWS, 2 * j, 2))
+
+    steps = FF // WIDE
+    loop(steps, feed_back)
+    saves[4].wait()
+    saves[3].wait()
+
+    def middle_back(at, s):
+        grad = dx[at, :]
+        back, scaled = norm_back(middle[at, :], grad, 1.0 + part(s, 4))
+        add_mod(s, 3, rows_sum(grad))
+        add_mod(s, 4, rows_sum(scaled))
+        total = grad_in[at, :] + back
+        grad_out[at, :] = total
+        low = (part(s, 2) * total).astype(low_type)
+        g_low[at, :] = low
+        bias_out[:, B_O : B_O + D] += rows_sum(low.astype(full_type))
+        add_mod(s, 2, rows_sum(attn[at, :] * total))
+
+    each_chunk(middle_back)
+    loads[1].wait()
+    saves[2].wait()
+    for j in (steps - 2, steps - 1):
+        mlp_store(j, 0).wait()
+        mlp_store(j, 1).wait()
+    turned[...] = heads[...].astype(full_type).T.astype(low_type)
+
+    def wo_store(j):
+        return outer(j % 2, 1, 0, D // ROWS, 2 * j, 2, d_two.at[j % 2])
+
+    def out_back(j):
+        cols = pl.ds(pl.multiple_of(j * WIDE, WIDE), WIDE)
+
+        @pl.when(j >= 2)
+        def _():
+            wo_store(j - 2).wait()
+
+        put_block(d_two.at[j % 2], 0, 0, dot(turned[...], g_low[:, cols]))
+        wo_store(j).start()
+        heads[:, cols] = dot_nt(g_low[...], block_of(w_o, j * half, half, 0, D // LANES)).astype(low_type)
+
+    loop(D // WIDE, out_back)
+    saves[1].wait()
+    first = head_masks()
+
+    def attend_back(i):
+        s, j = i // (HEADS // 2), i % (HEADS // 2)
+        at = pl.ds(pl.multiple_of(s * SEQ, SEQ), SEQ)
+        cut = lambda o: qkv[at, pl.ds(pl.multiple_of(o * D + j * LANES, LANES), LANES)]
+        q, k, v = cut(0), cut(1), cut(2)
+        go = heads[at, pl.ds(pl.multiple_of(j * LANES, LANES), LANES)]
+        q = q * jnp.asarray(HD ** (-0.5), low_type)
+        zero = jnp.zeros_like(q)
+        dq, dk, dv = [], 0.0, 0.0
+        for mask in (first, ~first):
+            q_h, go_h = jnp.where(mask, q, zero), jnp.where(mask, go, zero)
+            probs = softmax_f32(dot_nt(q_h, k))
+            grad_probs = dot_nt(go_h, v)
+            dv = dv + dot_tn(probs.astype(low_type), go_h)
+            inner = jnp.sum(probs * grad_probs, axis=-1, keepdims=True)
+            ds = (probs * (grad_probs - inner)).astype(low_type)
+            dq.append(dot(ds, k) * HD ** (-0.5))
+            dk = dk + dot_tn(ds, q_h)
+        put = lambda o, value: d_qkv.at[at, pl.ds(pl.multiple_of(o * D + j * LANES, LANES), LANES)].set(value)
+        for o, value in enumerate((jnp.where(first, dq[0], dq[1]), dk, dv)):
+            low = value.astype(low_type)
+            d_qkv[at, pl.ds(pl.multiple_of(o * D + j * LANES, LANES), LANES)] = low
+            if o != 1:
+                start = (B_Q if o == 0 else B_V) + j * LANES
+                bias_out[:, pl.ds(pl.multiple_of(start, LANES), LANES)] += rows_sum(low.astype(full_type))
+
+    loop(attention_pairs(rows), attend_back)
+    saves[0].wait()
+    loads[0].wait()
+    wo_store(1).wait()
+    wo_store(2).wait()
+    turned[...] = h1[...].astype(full_type).T.astype(low_type)
+    dx[...] = jnp.zeros(dx.shape, full_type)
+
+    def qkv_store(j):
+        return outer(j % 2, 0, 0, D // ROWS, 2 * j, 2, d_two.at[j % 2])
+
+    def project_back(j):
+        cols = pl.ds(pl.multiple_of(j * WIDE, WIDE), WIDE)
+
+        @pl.when(j >= 2)
+        def _():
+            qkv_store(j - 2).wait()
+
+        put_block(d_two.at[j % 2], 0, 0, dot(turned[...], d_qkv[:, cols]))
+        qkv_store(j).start()
+        dx[...] += dot_nt(d_qkv[:, cols], block_of(w_qkv, 0, D // ROWS, 2 * j, 2))
+
+    count = 3 * D // WIDE
+    loop(count, project_back)
+
+    def input_back(at, s):
+        grad = dx[at, :]
+        back, scaled = norm_back(x[at, :], grad, 1.0 + part(s, 1))
+        add_mod(s, 0, rows_sum(grad))
+        add_mod(s, 1, rows_sum(scaled))
+        grad_out[at, :] += back
+
+    each_chunk(input_back)
+    for j in (count - 2, count - 1):
+        qkv_store(j).wait()
+
+
+def layer_backward_call(plan, x, grad, mod, saved, units):
+    rows = x.shape[0]
+    vm = pl.BlockSpec(memory_space=pltpu.VMEM)
+    anywhere = pl.BlockSpec(memory_space=pl.ANY)
+    dma = pltpu.SemaphoreType.DMA
+    shapes = [((rows, width), kind) for _, width, kind in SAVED]
+    tile = (ROWS, LANES)
+    return pl.pallas_call(
+        functools.partial(layer_backward_kernel, plan, rows),
+        out_shape=[
+            jax.ShapeDtypeStruct((rows, D), full_type),
+            jax.ShapeDtypeStruct((8, 6 * D), full_type),
+            jax.ShapeDtypeStruct((1, 4 * D + FF), full_type),
+            jax.ShapeDtypeStruct(units.shape, low_type),
+        ],
+        in_specs=[vm] * 3 + [anywhere] * (len(SAVED) + 1),
+        out_specs=[vm, vm, vm, anywhere],
+        scratch_shapes=[pltpu.VMEM(*s) for s in shapes]
+        + [segment_scratch(plan, i) for i in range(4)]
+        + [
+            pltpu.VMEM((rows, 3 * D), low_type),
+            pltpu.VMEM((rows, D), low_type),
+            pltpu.VMEM((rows, WIDE), low_type),
+            pltpu.VMEM((D, rows), low_type),
+            pltpu.VMEM((rows, D), full_type),
+            pltpu.VMEM((2, WIDE // ROWS, D // LANES) + tile, low_type),
+            pltpu.VMEM((2, D // ROWS, 2) + tile, low_type),
+            dma((4,)),
+            dma((len(SAVED),)),
+            dma((4,)),
+        ],
+        compiler_params=pltpu.CompilerParams(vmem_limit_bytes=60 * MB),
+        name="layer_backward",
+    )(x, grad, mod, *saved, units)
+
+
+def sigmoid(values):
+    return 1.0 / (1.0 + jnp.exp(-values))
+
+
+def silu_parts(values):
+    gate = sigmoid(values)
+    return values * gate, gate * (1.0 + values * (1.0 - gate))
+
+
+TOP = (7, 9, 11, 13)
+
+
+def top_kernel(plan, rows, sample_total, x, features, target, weight_t, modulator, b_1, b_2, b_3, b_f, w_h, b_h, units, *refs):
+    grad_x, stats, cond, bias_out, dw_h, grads = refs[:6]
+    p_1, p_2, p_3, w_f, pre_a, act_a, pre_b, act_b, pred, low, g_b, g_a, hidden, modf, d_modf, stage, dw_f, load_sem, out_sem = refs[6:]
+    weights = (p_1, p_2, p_3, w_f)
+    loads = [pltpu.make_async_copy(segment_ref(units, plan, s), weights[i], load_sem.at[i]) for i, s in enumerate(TOP)]
+    for copy in loads:
+        copy.start()
+    per = SEQ // CHUNK
+    half = WIDE // ROWS
+    stats[...] = jnp.zeros(stats.shape, full_type)
+    bias_out[...] = jnp.zeros(bias_out.shape, full_type)
+    d_modf[...] = jnp.zeros(d_modf.shape, full_type)
+    A_1, A_2, A_3, A_F, A_H = 0, PH, 2 * PH, 2 * PH + ZD, 2 * PH + ZD + 2 * D
+    wide_at = lambda j, base=0: pl.ds(pl.multiple_of(base + j * WIDE, LANES), WIDE)
+
+    def each_chunk(body):
+        loop(rows // CHUNK, lambda i: body(pl.ds(pl.multiple_of(i * CHUNK, CHUNK), CHUNK), i // per))
+
+    def to_low(at, s):
+        low[at, :] = x[at, :].astype(low_type)
+
+    each_chunk(to_low)
+    loads[0].wait()
+
+    def first_layer(j):
+        value = dot(low[...], block_of(p_1, 0, D // ROWS, 2 * j, 2)) + b_1[:, wide_at(j)]
+        pre_a[:, wide_at(j)] = value
+        act_a[:, wide_at(j)] = silu_parts(value)[0].astype(low_type)
+
+    loop(PH // WIDE, first_layer)
+    loads[1].wait()
+
+    def second_layer(j):
+        value = dot(act_a[...], block_of(p_2, 0, PH // ROWS, 2 * j, 2)) + b_2[:, wide_at(j)]
+        pre_b[:, wide_at(j)] = value
+        act_b[:, wide_at(j)] = silu_parts(value)[0].astype(low_type)
+
+    loop(PH // WIDE, second_layer)
+    loads[2].wait()
+
+    def third_layer(j):
+        pred[:, wide_at(j)] = dot(act_b[...], block_of(p_3, 0, PH // ROWS, 2 * j, 2)) + b_3[:, wide_at(j)]
+
+    loop(ZD // WIDE, third_layer)
+    seed = -proj_coeff / (SEQ * sample_total)
+
+    def cosine(at, s):
+        value = pred[at, :]
+        want = features[at, :].astype(full_type)
+        inner = jnp.sum(value * want, axis=-1, keepdims=True)
+        scale_a = lax.rsqrt(jnp.sum(value * value, axis=-1, keepdims=True) + norm_eps)
+        scale_b = lax.rsqrt(jnp.sum(want * want, axis=-1, keepdims=True) + norm_eps)
+        both = scale_a * scale_b
+        stats[0:1, 0:1] += jnp.sum(inner * both, axis=0, keepdims=True)
+        grad = seed * (want * both - value * (inner * both * scale_a * scale_a))
+        grad = grad.astype(low_type)
+        hidden[at, :] = grad
+        bias_out[:, A_3 : A_3 + ZD] += rows_sum(grad.astype(full_type))
+
+    each_chunk(cosine)
+
+    def store(segment, j, chunks):
+        where = segment_ref(grads, plan, segment).at[pl.ds(j * half, half)]
+        return pltpu.make_async_copy(stage.at[j % 2, :, pl.ds(0, chunks)], where, out_sem.at[j % 2])
+
+    def stored(segment, j, chunks):
+        @pl.when(j >= 2)
+        def _():
+            store(segment, j - 2, chunks).wait()
+
+    def third_back(j):
+        stored(11, j, ZD // LANES)
+        put_block(stage.at[j % 2], 0, 0, dot_tn(act_b[:, wide_at(j)], hidden[...]))
+        store(11, j, ZD // LANES).start()
+        grad = dot_nt(hidden[...], block_of(p_3, j * half, half, 0, ZD // LANES))
+        grad = (grad * silu_parts(pre_b[:, wide_at(j)])[1]).astype(low_type)
+        g_b[:, wide_at(j)] = grad
+        bias_out[:, wide_at(j, A_2)] += rows_sum(grad.astype(full_type))
+
+    def drain(segment, count, chunks):
+        for j in range(max(0, count - 2), count):
+            store(segment, j, chunks).wait()
+
+    loop(PH // WIDE, third_back)
+    drain(11, PH // WIDE, ZD // LANES)
+    span = 4 * LANES
+
+    def second_back(j):
+        stored(9, j, PH // LANES)
+        for i in range(PH // span):
+            put_block(stage.at[j % 2], 0, i * (span // LANES), dot_tn(act_a[:, wide_at(j)], g_b[:, i * span : (i + 1) * span]))
+        store(9, j, PH // LANES).start()
+        grad = dot_nt(g_b[...], block_of(p_2, j * half, half, 0, PH // LANES))
+        grad = (grad * silu_parts(pre_a[:, wide_at(j)])[1]).astype(low_type)
+        g_a[:, wide_at(j)] = grad
+        bias_out[:, wide_at(j, A_1)] += rows_sum(grad.astype(full_type))
+
+    loop(PH // WIDE, second_back)
+    drain(9, PH // WIDE, PH // LANES)
+
+    def first_back(j):
+        stored(7, j, PH // LANES)
+        for i in range(PH // span):
+            put_block(stage.at[j % 2], 0, i * (span // LANES), dot_tn(low[:, wide_at(j)], g_a[:, i * span : (i + 1) * span]))
+        store(7, j, PH // LANES).start()
+        grad_x[:, wide_at(j)] = dot_nt(g_a[...], block_of(p_1, j * half, half, 0, PH // LANES))
+
+    loop(D // WIDE, first_back)
+    loads[3].wait()
+
+    def final_mod(j):
+        modf[:, wide_at(j)] = dot(modulator[...], block_of(w_f, 0, D // ROWS, 2 * j, 2)) + b_f[:, wide_at(j)]
+
+    loop(2 * D // WIDE, final_mod)
+    part = lambda s, i: modf[pl.ds(s, 1), i * D : (i + 1) * D]
+    dw_h[...] = jnp.zeros(dw_h.shape, full_type)
+
+    def head(at, s):
+        hat, scale = norm_parts(x[at, :])
+        gain = 1.0 + part(s, 1)
+        normed = (hat * gain + part(s, 0)).astype(low_type)
+        off = dot(normed, w_h[...]) + b_h[...] - target[at, :]
+        weight = weight_t[pl.ds(s, 1), :]
+        stats[1:2, :] += rows_sum(weight * off * off)
+        grad = (2.0 * weight / (SEQ * PD * sample_total) * off).astype(low_type)
+        bias_out[:, A_H : A_H + LANES] += rows_sum(grad.astype(full_type))
+        dw_h[...] += dot_tn(normed, grad)
+        back = dot_nt(grad, w_h[...])
+        d_modf[pl.ds(s, 1), 0:D] += rows_sum(back)
+        d_modf[pl.ds(s, 1), D : 2 * D] += rows_sum(back * hat)
+        inner = back * gain
+        mean_a = jnp.mean(inner, axis=-1, keepdims=True)
+        mean_b = jnp.mean(inner * hat, axis=-1, keepdims=True)
+        grad_x[at, :] += scale * (inner - mean_a - hat * mean_b)
+
+    each_chunk(head)
+    turned = modulator[...].astype(full_type).T.astype(low_type)
+    cond[...] = jnp.zeros(cond.shape, full_type)
+
+    def final_back(j):
+        grad = d_modf[:, wide_at(j)].astype(low_type)
+        bias_out[:, wide_at(j, A_F)] += rows_sum(grad.astype(full_type))
+        put_block(dw_f, 0, 2 * j, dot(turned, grad))
+        cond[...] += dot_nt(grad, block_of(w_f, 0, D // ROWS, 2 * j, 2))
+
+    loop(2 * D // WIDE, final_back)
+    last = pltpu.make_async_copy(dw_f, segment_ref(grads, plan, 13), out_sem.at[2])
+    last.start()
+    last.wait()
+    drain(7, D // WIDE, PH // LANES)
+
+
+def top_call(plan, sample_total, x, features, target, weight_t, modulator, biases, w_h, b_h, units):
+    rows = x.shape[0]
+    vm = pl.BlockSpec(memory_space=pltpu.VMEM)
+    anywhere = pl.BlockSpec(memory_space=pl.ANY)
+    dma = pltpu.SemaphoreType.DMA
+    few = modulator.shape[0]
+    f32 = lambda *shape: pltpu.VMEM(shape, full_type)
+    bf16 = lambda *shape: pltpu.VMEM(shape, low_type)
+    shape = lambda *dims: jax.ShapeDtypeStruct(dims, full_type)
+    return pl.pallas_call(
+        functools.partial(top_kernel, plan, rows, sample_total),
+        out_shape=[
+            shape(rows, D),
+            shape(8, LANES),
+            shape(few, D),
+            shape(1, 2 * PH + ZD + 2 * D + LANES),
+            shape(D, LANES),
+            jax.ShapeDtypeStruct(units.shape, low_type),
+        ],
+        in_specs=[vm] * 11 + [anywhere],
+        out_specs=[vm] * 5 + [anywhere],
+        scratch_shapes=[segment_scratch(plan, s) for s in TOP]
+        + [f32(rows, PH), bf16(rows, PH), f32(rows, PH), bf16(rows, PH), f32(rows, ZD), bf16(rows, D)]
+        + [bf16(rows, PH), bf16(rows, PH), bf16(rows, ZD), f32(few, 2 * D), f32(few, 2 * D)]
+        + [bf16(2, WIDE // ROWS, PH // LANES, ROWS, LANES), segment_scratch(plan, 13)]
+        + [dma((4,)), dma((3,))],
+        compiler_params=pltpu.CompilerParams(vmem_limit_bytes=60 * MB),
+        name="projector_and_head",
+    )(x, features, target, weight_t, modulator, *biases, w_h, b_h, units)
 
 
 def model_step(layer_lists, pieces, latents, noise, times, labels, dropped, features, devices):
@@ -981,26 +1639,128 @@
     return (weight_new, first_new, second_new)
 
 
+def vector_of(units, plan, number):
+    _, _, count, first, shape, _ = plan.segments[number]
+    flat = units[first : first + count].reshape(-1)[: math.prod(shape)]
+    return flat.reshape(shape)
+
+
+def matrix_of(units, plan, number):
+    _, chunks, count, first, shape, _ = plan.segments[number]
+    part = units[first : first + count].reshape(shape[0] // ROWS, chunks, ROWS, LANES)
+    return part.transpose(0, 2, 1, 3).reshape(shape)
+
+
+def units_of(grad, plan, number):
+    _, chunks, count, _, shape, matrix = plan.segments[number]
+    low = grad.astype(low_type)
+    if matrix:
+        low = low.reshape(shape[0] // ROWS, ROWS, chunks, LANES).transpose(0, 2, 1, 3)
+        return low.reshape(count, ROWS, LANES)
+    flat = jnp.pad(low.reshape(-1), ((0, count * UNIT - low.size),))
+    return flat.reshape(count, ROWS, LANES)
+
+
+def put_units(grads, plan, first_number, values):
+    parts = [units_of(value, plan, first_number + i) for i, value in enumerate(values)]
+    joined = jnp.concatenate(parts) if len(parts) > 1 else parts[0]
+    return lax.dynamic_update_slice(grads, joined, (plan.segments[first_number][3], 0, 0))
+
+
+def as_row(vector):
+    return vector.astype(full_type).reshape(1, -1)
+
+
+def embed_step(pieces, table_rows, latents, noise, times):
+    mixing = times[:, None, None]
+    noisy_bf = ((1.0 - mixing) * latents + mixing * noise).astype(low_type)
+    tokens = linear_fwd(noisy_bf, pieces[0]) + pieces[1] + position_table()
+    basis_bf = time_features(times).astype(low_type)
+    time_pre = linear_fwd(basis_bf, pieces[2]) + pieces[3]
+    time_act = jax.nn.silu(time_pre).astype(low_type)
+    condition = linear_fwd(time_act, pieces[4]) + pieces[5] + table_rows.astype(full_type)
+    saved = (noisy_bf, basis_bf, time_pre, time_act, condition)
+    return (tokens, jax.nn.silu(condition).astype(low_type), saved)
+
+
+def embed_step_back(pieces, saved, classes, grad_tokens, grad_modulator):
+    noisy_bf, basis_bf, time_pre, time_act, condition = saved
+    onehot = (classes[:, None] == jnp.arange(CLS, dtype=jnp.int32)[None, :]).astype(low_type)
+    return embed_backward(
+        pieces, (noisy_bf, basis_bf, time_pre, time_act, onehot, condition), grad_tokens, grad_modulator
+    )
+
+
 def by_kernels(plan, root_plan, layer_flat, root_flat, data, devices):
+    latents, noise, times, labels, dropped, features = data
+    samples = latents.shape[0]
+    sample_total = samples * devices
+    rows = samples * SEQ
     plans = (root_plan,) + (plan,) * LAYERS
     raws = [to_rows(root_flat, root_plan)]
     raws += [to_rows(layer_flat[ordinal], plan) for ordinal in range(LAYERS)]
-    gathered = gather_units(plans, raws)
-    pieces = from_units(gathered[0], root_plan)
-    layer_lists = [from_units(units, plan) for units in gathered[1:]]
-    loss_part, square_sums, layer_grads, root_grads = model_step(
-        layer_lists, pieces, *data, devices
-    )
-    grads = [into_units(root_grads, root_plan)]
-    grads += [into_units(grad_list, plan) for grad_list in layer_grads]
+    root_units, *layer_units = gather_units(plans, raws)
+    early = [matrix_of(root_units, root_plan, i) if i % 2 == 0 else vector_of(root_units, root_plan, i) for i in range(6)]
+    classes = jnp.where(dropped == 1, CLS - 1, labels)
+    table_first = root_plan.segments[6][3]
+    table = root_units[table_first : table_first + root_plan.segments[6][2]].reshape(-1, LANES)
+    wide = D // LANES
+    table_rows = jnp.stack(
+        [lax.dynamic_slice(table, (classes[s] * wide, 0), (wide, LANES)).reshape(D) for s in range(samples)]
+    )
+    tokens, modulator, embed_saved = embed_step(early, table_rows, latents, noise, times)
+    few = up(samples, ROWS)
+    modulator_rows = jnp.pad(modulator, ((0, few - samples), (0, 0)))
+    residual = tokens.reshape(rows, D)
+    inputs, mods, kept, sums = [], [], [], []
+    for ordinal in range(LAYERS):
+        units = layer_units[ordinal]
+        b_q, b_v, b_o, b_1, b_2, b_mod = (as_row(vector_of(units, plan, i)) for i in range(5, 11))
+        bias_qkv = jnp.concatenate([b_q, jnp.zeros_like(b_q), b_v], axis=1)
+        mods.append(mods_call(plan, modulator_rows, b_mod, units))
+        inputs.append(residual)
+        residual, total, saved = layer_forward_call(
+            plan, residual, mods[ordinal], (bias_qkv, b_o, b_1, b_2), units
+        )
+        kept.append(saved)
+        sums.append(total)
+    target = jnp.pad((noise - latents).reshape(rows, PD), ((0, 0), (0, LANES - PD)))
+    weight_t = jnp.broadcast_to(jnp.pad(1.0 + 2.0 * times, (0, 8 - samples))[:, None], (8, LANES))
+    w_h = jnp.pad(vector_of(root_units, root_plan, 15), ((0, 0), (0, LANES - PD)))
+    b_h = jnp.pad(as_row(vector_of(root_units, root_plan, 16)), ((0, 0), (0, LANES - PD)))
+    biases = [as_row(vector_of(root_units, root_plan, i)) for i in (8, 10, 12, 14)]
+    grad, losses, grad_cond, bias_grads, grad_w_h, root_grads = top_call(
+        root_plan, sample_total, residual, features.reshape(rows, ZD), target, weight_t, modulator_rows, biases, w_h, b_h, root_units
+    )
+    loss_part = -proj_coeff / SEQ * losses[0, 0] + jnp.sum(losses[1]) / (SEQ * PD)
+    grad_cond = grad_cond[:samples]
+    layer_grads = [None] * LAYERS
+    for ordinal in reversed(range(LAYERS)):
+        units = layer_units[ordinal]
+        grad, grad_mod, bias_grad, grads = layer_backward_call(
+            plan, inputs[ordinal], grad, mods[ordinal], kept[ordinal], units
+        )
+        low_mod = jnp.pad(grad_mod.astype(low_type), ((0, few - grad_mod.shape[0]), (0, 0)))
+        grads, cond_part = mods_back_call(plan, modulator_rows, low_mod, units, grads)
+        grad_cond = grad_cond + cond_part[:samples]
+        cuts = jnp.split(bias_grad[0], (D, 2 * D, 3 * D, 3 * D + FF))
+        grad_b_mod = jnp.sum(low_mod.astype(full_type), axis=0)
+        layer_grads[ordinal] = put_units(grads, plan, 5, cuts + [grad_b_mod])
+    embed_grads = embed_step_back(early, embed_saved, classes, grad.reshape(samples, SEQ, D), grad_cond)
+    cuts = jnp.split(bias_grads[0], (PH, 2 * PH, 2 * PH + ZD, 2 * PH + ZD + 2 * D))
+    for number, value in zip((8, 10, 12), cuts):
+        root_grads = put_units(root_grads, root_plan, number, [value])
+    root_grads = put_units(root_grads, root_plan, 14, [cuts[3], grad_w_h[:, :PD], cuts[4][:PD]])
+    root_grads = put_units(root_grads, root_plan, 0, embed_grads)
+    square_sums = jnp.stack([jnp.sum(total[:3], axis=1) for total in sums])
     numbers = jnp.concatenate([loss_part[None], square_sums.reshape(-1)])
     stats = jnp.pad(numbers, (0, 8 * LANES - numbers.shape[0])).reshape(8, LANES)
-    rows, stats = reduce_units(plans, grads, stats)
+    rows_out, stats = reduce_units(plans, [root_grads] + layer_grads, stats)
     numbers = stats[0].reshape(-1)
-    shard_root = rows[0].reshape(-1)[: root_plan.share]
-    shard_layers = jnp.stack([r.reshape(-1)[: plan.share] for r in rows[1:]])
-    sums = numbers[1 : 1 + 3 * LAYERS].reshape(LAYERS, 3)
-    return (shard_layers, shard_root, numbers[0], sums, jnp.sum(stats[1]))
+    shard_root = rows_out[0].reshape(-1)[: root_plan.share]
+    shard_layers = jnp.stack([r.reshape(-1)[: plan.share] for r in rows_out[1:]])
+    stream = numbers[1 : 1 + 3 * LAYERS].reshape(LAYERS, 3)
+    return (shard_layers, shard_root, numbers[0], stream, jnp.sum(stats[1]))
 
 
 def by_collectives(layer_flat, root_flat, data, devices):

time: 1560 us -> 1130 us (0.72)
  local copies, waits for them, and re-layouts: 495 us -> 78.5 us
  Pallas kernels: 750 us -> 1000 us
  matrix products: 215 us -> 5.05 us
  other arithmetic: 75.9 us -> 34.9 us
    pallas_call x0 -> x9, Pallas kernels: none -> 251 us  [the longest x2 102 us: layer_backward_call(): pl.pallas_call(functools.partial(layer_backward_kernel, plan, rows), out_...]
    reshape x44 -> x13, local copies, waits for them, and re-layouts: 230 us -> 4.21 us  [the longest x3 2.1 us: units_of(): low.reshape(shape[0] // ROWS, ROWS, chunks, LANES).transpose(0, 2, 1, 3)]
    transpose x17 -> x3, local copies, waits for them, and re-layouts: 70.4 us -> 1.29 us  [the longest x2 1.28 us: units_of(): low.reshape(shape[0] // ROWS, ROWS, chunks, LANES).transpose(0, 2, 1, 3)]
    dot_general x16 -> x1, matrix products: 68.3 us -> 0.47 us  [linear_back(): lax.dot_general(rows_out, weight, (((1,), (1,)), ((), ())), preferred_ele...]
    unnamed x517 -> x69, local copies, waits for them, and re-layouts: 87.1 us -> 24.4 us
    dot_general x18 -> x3, matrix products: 60.2 us -> 1.05 us  [linear_back(): lax.dot_general(rows_in, rows_out, (((0,), (0,)), ((), ())), preferred_el...]
    dot_general x18 -> x3, matrix products: 52.9 us -> 2.03 us  [linear_fwd(): jnp.dot(inputs.reshape(-1, inputs.shape[-1]), weight, preferred_element_t...]
    slice x25 -> x14, local copies, waits for them, and re-layouts: 56 us -> 12.6 us  [the longest x5 3.58 us: vector_of(): flat = units[first:first + count].reshape(-1)[:math.prod(shape)]]
where the time goes in v1:
time: 1130 us
  Pallas kernels  1000 us (88%)
  local copies, waits for them, and re-layouts  78.5 us (7%)
  other arithmetic  34.9 us (3%)
    pallas_call x1, Pallas kernels, reduce_units(): pl.pallas_call(functools.partial(reduce_kernel, plans, zs), out_shape=out...  460 us
    pallas_call x1, Pallas kernels, gather_units(): pl.pallas_call(functools.partial(gather_kernel, plans, zs), out_shape=[ja...  290 us
    pallas_call x2, Pallas kernels, layer_backward_call(): pl.pallas_call(functools.partial(layer_backward_kernel, plan, rows), out_...  102 us
    pallas_call x2, Pallas kernels, layer_forward_call(): pl.pallas_call(functools.partial(layer_forward_kernel, plan, rows), out_s...  74.3 us
    pallas_call x1, Pallas kernels, top_call(): pl.pallas_call(functools.partial(top_kernel, plan, rows, sample_total), o...  49 us
    unnamed x69, local copies, waits for them, and re-layouts  24.4 us

profile of v1, /device:TPU:6, one launch (start us, length us, event | category | flops | bytes accessed | tf_op | source)
XLA Modules:
  0.0 1125.7 jit_solution(13858412717222664914)
XLA Ops:
  7.6 1.5 copy-done.6
  9.1 13.9 %slice_reduce_fusion = (f32[332112]{0:T(1024)S(1)}, f32[332112]{0:T(1024)S(1)}) fusion(f32[2,332112]{1,0:T(2,128)S(1)} %copy-done.6), kind=kLoop, calls=%fused_computation.12 | loop fusion | bytes 5313792 | tf_op jit(solution)/shard_map/slice | solution.py:1701
  23.3 290.0 %gather_units.1 = (bf16[4992,16,128]{2,1,0:T(8,128)(2,1)}, bf16[5248,16,128]{2,1,0:T(8,128)(2,1)}, bf16[5248,16,128]{2,1,0:T(8,128)(2,1)}) custom-call(f32[2496,128]{1,0:T(8,128)S(1)} %pad_bitcast_fusion.2.refs_0_, f32[2624,128]{1,0:T(8,128)S(1)} %get-tuple-element.163.refs_1_, f32[2624,128]{1,0:T(8,128)S(1)} %get-tuple-element.162.refs_2_), custom_call_target="tpu_custom_call" | custom-call | tf_op jit(solution)/shard_map/gather_units/pallas_call | solution.py:255
  324.4 1.3 slice_bitcast_fusion.2
  329.3 1.6 add_add_fusion
  330.8 1.5 slice.229
  332.7 1.7 slice.231
  334.8 7.1 copy-done.1
  341.9 4.3 modulation.3.mod
  346.9 7.1 copy-done
  354.0 3.8 modulation.2.mod
  358.5 37.1 %layer_forward.2 = (f32[512,768]{1,0:T(8,128)}, f32[8,768]{1,0:T(8,128)}, bf16[512,768]{1,0:T(8,128)(2,1)}, bf16[512,2304]{1,0:T(8,128)(2,1)}, bf16[512,768]{1,0...) custom-call(f32[512,768]{1,0:T(8,128)} %bitcast.203, ...), custom_call_target="tpu_custom_call" | custom-call | tf_op jit(solution)/shard_map/layer_forward/pallas_call | solution.py:1171
  396.5 37.2 %layer_forward.3 = (f32[512,768]{1,0:T(8,128)}, f32[8,768]{1,0:T(8,128)}, bf16[512,768]{1,0:T(8,128)(2,1)}, bf16[512,2304]{1,0:T(8,128)(2,1)}, bf16[512,768]{1,0...) custom-call(f32[512,768]{1,0:T(8,128)} %get-tuple-element.56.x, ...), custom_call_target="tpu_custom_call" | custom-call | tf_op jit(solution)/shard_map/layer_forward/pallas_call | solution.py:1171
  433.7 49.0 %projector_and_head.1 = (f32[512,768]{1,0:T(8,128)}, f32[8,128]{1,0:T(8,128)}, f32[16,768]{1,0:T(8,128)}, f32[1,6528]{1,0:T(1,128)}, f32[768,128]{1,0:T(8,128)}, /*index=5*/bf16[4992,16,128]{2,1,0:T(8,128)(2,1)}) custom-call(f32[512,768]{1,0:T(8,128)} %get-tuple-element.58.x, bf16[512,768]{1,0:T(8,128)(2,1)} %bitcast.222, f32[512,128]{1,0:T(8,128)} %pad.111.target, ...), custom_call_target="tpu_custom_call" | custom-call | tf_op jit(solution)/shard_map/projector_and_head/pallas_call | solution.py:1571
  482.7 1.3 slice_reduce_fusion.19
  491.9 50.8 %layer_backward.2 = (f32[512,768]{1,0:T(8,128)}, f32[8,4608]{1,0:T(8,128)}, f32[1,6144]{1,0:T(1,128)}, bf16[5248,16,128]{2,1,0:T(8,128)(2,1)}) custom-call(f32[512,768]{1,0:T(8,128)} %get-tuple-element.56.x, f32[512,768]{1,0:T(8,128)} %get-tuple-element.62.grad_in, f32[16,4608]{1,0:T(8,128)} %copy-done.3, bf16[512,768]{1,0:T(8,128)(2,1)} %get-tuple-element.63.refs_0_, ...), custom_call_target="tpu_custom_call" | custom-call | tf_op jit(solution)/shard_map/layer_backward/pallas_call | solution.py:1369
  544.6 8.9 modulation_back.2
  554.2 50.7 %layer_backward.3 = (f32[512,768]{1,0:T(8,128)}, f32[8,4608]{1,0:T(8,128)}, f32[1,6144]{1,0:T(1,128)}, bf16[5248,16,128]{2,1,0:T(8,128)(2,1)}) custom-call(f32[512,768]{1,0:T(8,128)} %bitcast.204, f32[512,768]{1,0:T(8,128)} %get-tuple-element.71.grad_in, f32[16,4608]{1,0:T(8,128)} %copy-done.2, bf16[512,768]{1,0:T(8,128)(2,1)} %get-tuple-element.72.refs_0_, ...), custom_call_target="tpu_custom_call" | custom-call | tf_op jit(solution)/shard_map/layer_backward/pallas_call | solution.py:1369
  605.0 1.6 fusion.41
  607.1 8.9 modulation_back.3
  619.4 1.6 reshape.534
  622.2 1.5 convolution_convert_fusion
  623.7 1.3 reshape.537
  626.9 2.2 constant_dynamic-update-slice_fusion.21.refs_0_
  629.1 460.2 %reduce_units.1 = (f32[2496,128]{1,0:T(8,128)}, f32[2624,128]{1,0:T(8,128)}, f32[2624,128]{1,0:T(8,128)}, f32[2,8,128]{2,1,0:T(8,128)}, bf16[4,2,2,156,16,128]{5...) custom-call(bf16[4992,16,128]{2,1,0:T(8,128)(2,1)} %constant_dynamic-update-s, ...), custom_call_target="tpu_custom_call" | custom-call | tf_op jit(solution)/shard_map/reduce_units/pallas_call | solution.py:537
  1089.4 1.3 slice_reduce_fusion.9
  1092.0 1.5 slice.280
  1093.5 6.2 stack.25
  1100.5 6.2 stack.26
  1106.8 2.6 multiply_subtract_fusion.1
  1109.4 1.3 copy-done.11
  1111.5 12.7 %multiply_subtract_fusion = (f32[2,332112]{1,0:T(2,128)}, f32[2,332112]{1,0:T(2,128)}, f32[2,332112]{1,0:T(2,128)}) fusion(f32[2,332112]{1,0:T(2,128)S(1)} %copy-done.7, f32[]{:T(128)S(6)} %div.61, f32[1,332112]{1,0:T(1,128)S(1)} %stack.26, f32[1,332112]{1,0:T(1,128)S(1)} %stack.25, f32[2,332112]{1,0:T(2,128)S(1)} %copy-done.11, f32[2,332112]{1,0:T(2,128)S(1)} %copy-done.12), kind=kLoop, calls=%fused_computation.4 | loop fusion | flops 10627584 | bytes 18598276 | tf_op jit(solution)/shard_map/sub | solution.py:1636
  (165 shorter events, 41.5 us)
Async XLA Ops:
  0.6 6.8 copy-start.8
  7.4 1.8 copy-start.6
  334.8 7.1 copy-start.1
  341.9 4.3 copy-start.4
  346.2 0.7 copy-start.3
  346.9 7.1 copy-start
  357.8 0.7 copy-start.2
  433.7 52.8 %copy-start.19 = (f32[8,768]{1,0:T(8,128)S(1)}, f32[8,768]{1,0:T(8,128)}, u32[]{:S(2)}) copy-start(f32[8,768]{1,0:T(8,128)} %get-tuple-element.94) | copy-start | bytes 73732
  491.9 52.7 %copy-start.5 = (bf16[16,768]{1,0:T(8,128)(2,1)S(1)}, bf16[16,768]{1,0:T(8,128)(2,1)}, u32[]{:S(2)}) copy-start(bf16[16,768]{1,0:T(8,128)(2,1)} %copy-done.4) | copy-start | bytes 73732
  604.9 1.9 copy-start.18
  605.0 2.1 copy-start.17
  625.0 1.3 copy-start.10
  1092.0 8.4 copy-start.13
  1100.4 6.3 copy-start.9
  1100.4 6.3 copy-start.14
  1100.4 6.3 copy-start.15
  1100.4 6.4 copy-start.16
  1106.7 2.7 copy-start.7
  1106.7 3.9 copy-start.11
  1106.8 4.7 copy-start.12

commit v2 on v1

--- a/solution.py
+++ b/solution.py
@@ -255,12 +255,15 @@
     return pl.pallas_call(
         functools.partial(gather_kernel, plans, zs),
         out_shape=[jax.ShapeDtypeStruct((n * p.per, ROWS, LANES), low_type) for p in plans],
-        in_specs=[pl.BlockSpec(memory_space=pl.ANY)] * nb,
-        out_specs=[pl.BlockSpec(memory_space=pl.ANY)] * nb,
+        in_specs=[pl.BlockSpec(memory_space=pltpu.HBM)] * nb,
+        out_specs=[pl.BlockSpec(memory_space=pltpu.HBM)] * nb,
         scratch_shapes=scratch,
         compiler_params=pltpu.CompilerParams(collective_id=0, has_side_effects=True, vmem_limit_bytes=48 * 1024 * 1024),
         name="gather_units",
     )(*raws)
+
+AHEAD = 4
+
 
 def reduce_kernel(plans, zs, *refs):
     nb = len(plans)
@@ -303,11 +306,6 @@
     def sibling(b, k, dy, dx):
         return remote(slot(b, k, dy, dx, 1), first[b].at[k, dy, dx], s1.at[b, k, dy, dx], r1.at[b, k, dy, dx], cpeer)
 
-    for b in range(nb):
-        for dy, dx in order:
-            for k in range(zs):
-                sibling(b, k, dy, dx).start()
-
     def add(p, dst, at, one, one_at, two, two_at):
         step = p.half // 2
 
@@ -319,6 +317,7 @@
         lax.fori_loop(0, 2, body, 0)
 
     ring = local.shape[0]
+    planes = list(range(1, zs)) + [0]
     used = []
 
     def send_of(b, h, k, dy, dx, src):
@@ -326,7 +325,7 @@
             return remote(src, two_a[b].at[k, dx], s2a.at[b, k, dx], r2a.at[b, k, dx], ypeer)
         return remote(src, two_b[b].at[k, dy], s2b.at[b, k, dy], r2b.at[b, k, dy], xpeer)
 
-    steps = [(b, dy, dx, k) for b in range(nb) for dy, dx in order for k in range(zs)]
+    steps = [(b, dy, dx, k) for b in range(nb) for k in planes for dy, dx in order]
 
     def loads(number):
         b, dy, dx, k = steps[number]
@@ -337,6 +336,7 @@
         return one, two
 
     pending = {}
+    steps_args = lambda number: (steps[number][0], steps[number][3], steps[number][1], steps[number][2])
 
     def prepare(number):
         b, dy, dx, k = steps[number]
@@ -352,7 +352,11 @@
         p = plans[b]
         at = number % ring
         if number == 0:
+            for ahead in range(AHEAD):
+                sibling(*steps_args(ahead)).start()
             prepare(0)
+        if number + AHEAD < len(steps):
+            sibling(*steps_args(number + AHEAD)).start()
         if number + 1 < len(steps):
             prepare(number + 1)
         for copy in loads(number):
@@ -382,28 +386,34 @@
         src = (three_a if h == 0 else three_b)[b].at[k]
         return remote(src, four[b].at[h, k - 1], s4.at[b, h, k - 1], r4.at[b, h, k - 1], below(k))
 
-    def phase_two(b):
+    def phase_two(b, k):
         p = plans[b]
         for far in (1, 0):
-            for k in range(zs):
-                for h, kept, two, sem in ((0, kept_a, two_a, r2a), (1, kept_b, two_b, r2b)):
-                    arrived(two[b].at[k, far], sem.at[b, k, far])
-                    if far:
-                        add(p, two[b].at[k, 1], 0, two[b].at[k, 1], 0, kept[b].at[k, 1], 0)
-                        three(b, h, k).start()
-                    else:
-                        add(p, kept[b].at[k, 0], 0, two[b].at[k, 0], 0, kept[b].at[k, 0], 0)
-
-    def phase_three(b):
+            for h, kept, two, sem in ((0, kept_a, two_a, r2a), (1, kept_b, two_b, r2b)):
+                arrived(two[b].at[k, far], sem.at[b, k, far])
+                if far:
+                    add(p, two[b].at[k, 1], 0, two[b].at[k, 1], 0, kept[b].at[k, 1], 0)
+                    three(b, h, k).start()
+                else:
+                    add(p, kept[b].at[k, 0], 0, two[b].at[k, 0], 0, kept[b].at[k, 0], 0)
+
+    def phase_three(b, k):
         p = plans[b]
-        for k in list(range(1, zs)) + [0]:
-            for h, kept, got, sem in ((0, kept_a, three_a, r3a), (1, kept_b, three_b, r3b)):
-                arrived(got[b].at[k], sem.at[b, k])
-                if k:
-                    add(p, got[b].at[k], 0, got[b].at[k], 0, kept[b].at[k, 0], 0)
-                    last(b, h, k).start()
-
-    def finish(b):
+        for h, kept, got, sem in ((0, kept_a, three_a, r3a), (1, kept_b, three_b, r3b)):
+            arrived(got[b].at[k], sem.at[b, k])
+            if k:
+                add(p, got[b].at[k], 0, got[b].at[k], 0, kept[b].at[k, 0], 0)
+                last(b, h, k).start()
+
+    def halo(b):
+        p = plans[b]
+        base = p.units_before
+        held = units_f.at[b % 2]
+        forward = remote(held.at[pl.ds(p.per, base)], from_prev[b], halo_s.at[b, 0], halo_r.at[b, 0], following)
+        backward = remote(held.at[pl.ds(base, p.units_after)], from_next[b], halo_s.at[b, 1], halo_r.at[b, 1], prev)
+        return forward, backward
+
+    def collect(b):
         p = plans[b]
         base = p.units_before
         for h, kept, got in ((0, kept_a, three_a), (1, kept_b, three_b)):
@@ -416,18 +426,21 @@
                 value = kept[b][0, 0, part].astype(full_type) + got[b][0, part].astype(full_type)
                 for k in range(1, zs):
                     value = value + four[b][h, k - 1, part].astype(full_type)
-                units_f[pl.ds(base + h * p.half + i * step, step)] = value
+                units_f[b % 2, pl.ds(base + h * p.half + i * step, step)] = value
                 return carry
 
             lax.fori_loop(0, 2, body, 0)
-        forward = remote(units_f.at[pl.ds(p.per, base)], from_prev[b], halo_s.at[b, 0], halo_r.at[b, 0], following)
-        backward = remote(units_f.at[pl.ds(base, p.units_after)], from_next[b], halo_s.at[b, 1], halo_r.at[b, 1], prev)
-        forward.start()
-        backward.start()
-        forward.wait()
-        backward.wait()
-        units_f[pl.ds(0, base)] = from_prev[b][...]
-        units_f[pl.ds(base + p.per, p.units_after)] = from_next[b][...]
+        for copy in halo(b):
+            copy.start()
+
+    def finish(b):
+        p = plans[b]
+        base = p.units_before
+        for copy in halo(b):
+            copy.wait()
+        held = b % 2
+        units_f[held, pl.ds(0, base)] = from_prev[b][...]
+        units_f[held, pl.ds(base + p.per, p.units_after)] = from_next[b][...]
         top = me * p.share // LANES - p.margin
         for origin, chunks, count, first_unit, _, _ in p.segments:
             lo = jnp.clip(p.per * me - base - first_unit, 0, count)
@@ -436,7 +449,7 @@
             def unit(u, carry):
                 block = u // chunks
                 row = origin + block * (ROWS * chunks) + (u - block * chunks) - top
-                value = units_f[first_unit + u - p.per * me + base]
+                value = units_f[held, first_unit + u - p.per * me + base]
                 if chunks == 1:
                     rows_f[pl.ds(row, ROWS), :] = value
                 else:
@@ -464,18 +477,24 @@
         pltpu.make_async_copy(flat_f.at[pl.ds(0, p.raw)], outs[b], out_sem.at[b]).start()
         return squares
 
-    per_bucket = 4 * zs
-    for b in range(nb):
-        for number in range(b * per_bucket, (b + 1) * per_bucket):
-            phase_one(number)
-        if b:
-            phase_two(b - 1)
-            phase_three(b - 1)
-    phase_two(nb - 1)
-    phase_three(nb - 1)
     squares = jnp.zeros((8, LANES), full_type)
-    for b in range(nb):
-        squares = squares + finish(b)
+    groups = [(b, k) for b in range(nb) for k in planes]
+    for g in range(len(groups) + 2):
+        if g < len(groups):
+            for number in range(4 * g, 4 * g + 4):
+                phase_one(number)
+        if 0 <= g - 1 < len(groups):
+            phase_two(*groups[g - 1])
+        if 0 <= g - 2 < len(groups):
+            phase_three(*groups[g - 2])
+        b = (g - 3) // zs - 1
+        if (g - 3) % zs == 0 and 0 <= b < nb - 1:
+            collect(b)
+        b = (g - 4) // zs - 1
+        if (g - 4) % zs == 0 and 0 <= b < nb - 1:
+            squares = squares + finish(b)
+    collect(nb - 1)
+    squares = squares + finish(nb - 1)
     pltpu.make_async_copy(flat_f.at[pl.ds(0, plans[nb - 1].raw)], outs[nb - 1], out_sem.at[nb - 1]).wait()
     total[0] = stats_in[...]
     total[1] = squares
@@ -518,9 +537,9 @@
     scratch += [half(p, zs, 2) for p in plans] + [half(p, zs, 2) for p in plans]
     scratch += [half(p, zs) for p in plans] + [half(p, zs) for p in plans]
     scratch += [half(p, 2, zs - 1) for p in plans]
-    ring = 4
+    ring = 8
     scratch += [pltpu.VMEM((ring, most) + tile, low_type), pltpu.VMEM((2, most) + tile, low_type)]
-    scratch += [pltpu.VMEM((max(p.units_before + p.per + p.units_after for p in plans),) + tile, full_type)]
+    scratch += [pltpu.VMEM((2, max(p.units_before + p.per + p.units_after for p in plans)) + tile, full_type)]
     scratch += [pltpu.VMEM((max(p.spread for p in plans), LANES), full_type)]
     scratch += [pltpu.VMEM((max(p.raw for p in plans), LANES), full_type)]
     scratch += [pltpu.VMEM((p.units_before,) + tile, full_type) for p in plans]
@@ -529,7 +548,7 @@
     scratch += [pltpu.VMEM((2, 8, LANES), full_type), pltpu.VMEM((hops, 2, 8, LANES), full_type)]
     scratch += [dma((nb, zs, 2, 2))] * 2 + [dma((nb, zs, 2))] * 4 + [dma((nb, zs))] * 4
     scratch += [dma((nb, 2, zs - 1))] * 2 + [dma((ring, 2)), dma((nb, 2)), dma((nb, 2)), dma((nb,)), dma((hops,)), dma((hops,))]
-    anywhere = pl.BlockSpec(memory_space=pl.ANY)
+    anywhere = pl.BlockSpec(memory_space=pltpu.HBM)
     inside = pl.BlockSpec(memory_space=pltpu.VMEM)
     out_shape = [jax.ShapeDtypeStruct((p.raw, LANES), full_type) for p in plans]
     out_shape += [jax.ShapeDtypeStruct((2, 8, LANES), full_type)]
@@ -1012,7 +1031,7 @@
     return pl.pallas_call(
         functools.partial(mods_kernel, plan),
         out_shape=jax.ShapeDtypeStruct((modulator.shape[0], 6 * D), full_type),
-        in_specs=[vm, vm, pl.BlockSpec(memory_space=pl.ANY)],
+        in_specs=[vm, vm, pl.BlockSpec(memory_space=pltpu.HBM)],
         out_specs=vm,
         scratch_shapes=[segment_scratch(plan, 4), pltpu.SemaphoreType.DMA],
         compiler_params=pltpu.CompilerParams(vmem_limit_bytes=32 * MB),
@@ -1045,7 +1064,7 @@
 
 def mods_back_call(plan, modulator, grad, units, grads):
     vm = pl.BlockSpec(memory_space=pltpu.VMEM)
-    anywhere = pl.BlockSpec(memory_space=pl.ANY)
+    anywhere = pl.BlockSpec(memory_space=pltpu.HBM)
     return pl.pallas_call(
         functools.partial(mods_back_kernel, plan),
         out_shape=[jax.ShapeDtypeStruct(grads.shape, low_type), jax.ShapeDtypeStruct((modulator.shape[0], D), full_type)],
@@ -1165,7 +1184,7 @@
 def layer_forward_call(plan, x, mod, biases, units):
     rows = x.shape[0]
     vm = pl.BlockSpec(memory_space=pltpu.VMEM)
-    anywhere = pl.BlockSpec(memory_space=pl.ANY)
+    anywhere = pl.BlockSpec(memory_space=pltpu.HBM)
     dma = pltpu.SemaphoreType.DMA
     shapes = [((rows, width), kind) for _, width, kind in SAVED]
     results = pl.pallas_call(
@@ -1362,7 +1381,7 @@
 def layer_backward_call(plan, x, grad, mod, saved, units):
     rows = x.shape[0]
     vm = pl.BlockSpec(memory_space=pltpu.VMEM)
-    anywhere = pl.BlockSpec(memory_space=pl.ANY)
+    anywhere = pl.BlockSpec(memory_space=pltpu.HBM)
     dma = pltpu.SemaphoreType.DMA
     shapes = [((rows, width), kind) for _, width, kind in SAVED]
     tile = (ROWS, LANES)
@@ -1562,7 +1581,7 @@
 def top_call(plan, sample_total, x, features, target, weight_t, modulator, biases, w_h, b_h, units):
     rows = x.shape[0]
     vm = pl.BlockSpec(memory_space=pltpu.VMEM)
-    anywhere = pl.BlockSpec(memory_space=pl.ANY)
+    anywhere = pl.BlockSpec(memory_space=pltpu.HBM)
     dma = pltpu.SemaphoreType.DMA
     few = modulator.shape[0]
     f32 = lambda *shape: pltpu.VMEM(shape, full_type)
@@ -1590,6 +1609,531 @@
     )(x, features, target, weight_t, modulator, *biases, w_h, b_h, units)
 
 
+def busy_loop(count, body, events=()):
+    size = max(1, -(-len(events) // count))
+
+    def step(i):
+        body(i)
+        for first in range(0, len(events), size):
+
+            @pl.when(i == first // size)
+            def _():
+                for event in events[first : first + size]:
+                    event()
+
+    loop(count, step)
+
+
+def spread(events, weights):
+    shares, done, total = [], 0, 0
+    for weight in weights:
+        total += weight
+        upto = len(events) * total // sum(weights)
+        shares.append(events[done:upto])
+        done = upto
+    return shares
+
+
+def row_vector(units, rows):
+    values = units.astype(full_type).reshape(-1, LANES)
+    return jnp.concatenate([values[r : r + 1, :] for r in range(rows)], axis=1)
+
+
+def pick(ref, here, *spots):
+    return ref.at[tuple(here.zero + spot for spot in spots)]
+
+
+class Place:
+    def __init__(self, zs):
+        self.zs = zs
+        self.n = zs * 8
+        self.me = lax.axis_index("fsdp")
+        self.zero = self.me * 0
+        self.z, self.y, self.x, self.c = place(self.me, zs)
+        self.prev = lax.rem(self.me + self.n - 1, self.n)
+        self.following = lax.rem(self.me + 1, self.n)
+        self.xpeer = self.index(self.z, self.y, 1 - self.x, self.c)
+        self.ypeer = self.index(self.z, 1 - self.y, self.x, self.c)
+        self.cpeer = self.index(self.z, self.y, self.x, 1 - self.c)
+
+    def index(self, z, y, x, c):
+        return ((z * 2 + y) * 2 + x) * 2 + c
+
+    def above(self, k):
+        return self.index(lax.rem(self.z + k, self.zs), self.y, self.x, self.c)
+
+    def below(self, k):
+        return self.index(lax.rem(self.z + self.zs - k, self.zs), self.y, self.x, self.c)
+
+    def slot(self, k, dy, dx, dc):
+        z = lax.rem(self.z + self.zs - k, self.zs)
+        flip = lambda value, change: 1 - value if change else value
+        return self.index(z, flip(self.y, dy), flip(self.x, dx), flip(self.c, dc))
+
+    def peers(self):
+        return [self.prev, self.following, self.xpeer, self.ypeer, self.cpeer] + [self.above(k) for k in range(1, self.zs)]
+
+    def greet(self):
+        barrier = pltpu.get_barrier_semaphore()
+        for peer in self.peers():
+            pl.semaphore_signal(barrier, inc=1, device_id=(peer,), device_id_type=MESH)
+
+    def met(self):
+        pl.semaphore_wait(pltpu.get_barrier_semaphore(), len(self.peers()))
+
+
+def remote(src, dst, send_sem, recv_sem, to):
+    return pltpu.make_async_remote_copy(src, dst, send_sem, recv_sem, device_id=(to,), device_id_type=MESH)
+
+
+def arrived(ref, sem):
+    pltpu.make_async_copy(ref, ref, sem).wait()
+
+
+class Gather:
+    def __init__(self, here, buckets, sems):
+        self.here = here
+        self.buckets = buckets
+        self.own_sem, self.send_sem, self.zr, self.xa, self.xb, self.yb, self.ya, self.cr = sems
+        self.sent = []
+        self.made = 0
+
+    def guarded(self, b, k, run):
+        plan, _, _, lo, hi = self.buckets[b]
+        if lo == 0 and hi == self.here.zs:
+            run()
+            return
+        source = lax.rem(self.here.z + self.here.zs - k, self.here.zs)
+        pl.when((source >= lo) & (source < hi))(run)
+
+    def sem(self, name, *spots):
+        return lambda: pick(getattr(self, name), self.here, *spots)
+
+    def send(self, b, k, src, dst, sem, to):
+        number = self.made
+        self.made += 1
+        make = lambda: remote(src(), dst(), pick(self.send_sem, self.here, number), sem(), to())
+        make().start()
+        self.sent.append((b, k, make))
+
+    def part(self, b, h, k, dy, dx, dc=0):
+        plan, units = self.buckets[b][:2]
+        return units.at[pl.ds(self.here.slot(k, dy, dx, dc) * plan.per + h * plan.half, plan.half)]
+
+    def whole(self, b, k, dy, dx, dc=0):
+        plan, units = self.buckets[b][:2]
+        return units.at[pl.ds(self.here.slot(k, dy, dx, dc) * plan.per, plan.per)]
+
+    def own_copy(self, b):
+        return pltpu.make_async_copy(self.buckets[b][2], self.whole(b, 0, 0, 0), pick(self.own_sem, self.here, b))
+
+    def start(self, b):
+        here, slot = self.here, self.buckets[b][2]
+        plan = self.buckets[b][0]
+
+        def run():
+            self.own_copy(b).start()
+            mine = lambda h: lambda: slot.at[pl.ds(h * plan.half, plan.half)]
+            to = lambda h: lambda: self.part(b, h, 0, 0, 0)
+            for k in range(1, here.zs):
+                for h in range(2):
+                    self.send(b, 0, mine(h), to(h), self.sem("zr", b, h, k), lambda k=k: here.above(k))
+            self.send(b, 0, mine(0), to(0), self.sem("xa", b, 0), lambda: here.xpeer)
+            self.send(b, 0, mine(1), to(1), self.sem("yb", b, 0), lambda: here.ypeer)
+            self.send(b, 0, mine(0), to(0), self.sem("ya", b, 0, 0), lambda: here.ypeer)
+            self.send(b, 0, mine(1), to(1), self.sem("xb", b, 0, 0), lambda: here.xpeer)
+            self.send(b, 0, lambda: slot, lambda: self.whole(b, 0, 0, 0), self.sem("cr", b, 0, 0, 0), lambda: here.cpeer)
+
+        self.guarded(b, 0, run)
+
+    def pass_on(self, b, k, h, dy, dx, sem, to):
+        ref = lambda: self.part(b, h, k, dy, dx)
+        self.send(b, k, ref, ref, sem, to)
+
+    def share(self, b, k, dy, dx):
+        ref = lambda: self.whole(b, k, dy, dx)
+        self.send(b, k, ref, ref, self.sem("cr", b, k, dy, dx), lambda: self.here.cpeer)
+
+    def events(self, b):
+        here = self.here
+        found = []
+
+        def add(k, run):
+            found.append(lambda: self.guarded(b, k, run))
+
+        for k in range(1, here.zs):
+
+            def from_z(k=k):
+                arrived(self.part(b, 0, k, 0, 0), pick(self.zr, self.here, b, 0, k))
+                self.pass_on(b, k, 0, 0, 0, self.sem("xa", b, k), lambda: here.xpeer)
+                arrived(self.part(b, 1, k, 0, 0), pick(self.zr, self.here, b, 1, k))
+                self.pass_on(b, k, 1, 0, 0, self.sem("yb", b, k), lambda: here.ypeer)
+                self.pass_on(b, k, 0, 0, 0, self.sem("ya", b, k, 0), lambda: here.ypeer)
+                self.pass_on(b, k, 1, 0, 0, self.sem("xb", b, k, 0), lambda: here.xpeer)
+                self.share(b, k, 0, 0)
+
+            add(k, from_z)
+        for k in range(here.zs):
+
+            def across(k=k):
+                arrived(self.part(b, 0, k, 0, 1), pick(self.xa, self.here, b, k))
+                self.pass_on(b, k, 0, 0, 1, self.sem("ya", b, k, 1), lambda: here.ypeer)
+                arrived(self.part(b, 1, k, 1, 0), pick(self.yb, self.here, b, k))
+                self.pass_on(b, k, 1, 1, 0, self.sem("xb", b, k, 1), lambda: here.xpeer)
+
+            add(k, across)
+        for k in range(here.zs):
+
+            def beside(k=k):
+                arrived(self.part(b, 1, k, 0, 1), pick(self.xb, self.here, b, k, 0))
+                self.share(b, k, 0, 1)
+                arrived(self.part(b, 0, k, 1, 0), pick(self.ya, self.here, b, k, 0))
+                self.share(b, k, 1, 0)
+
+            add(k, beside)
+        for k in range(here.zs):
+
+            def corner(k=k):
+                arrived(self.part(b, 1, k, 1, 1), pick(self.xb, self.here, b, k, 1))
+                arrived(self.part(b, 0, k, 1, 1), pick(self.ya, self.here, b, k, 1))
+                self.share(b, k, 1, 1)
+
+            add(k, corner)
+        return found
+
+    def complete(self, b):
+        self.guarded(b, 0, lambda: self.own_copy(b).wait())
+        for k in range(self.here.zs):
+
+            def run(k=k):
+                for dy in range(2):
+                    for dx in range(2):
+                        arrived(self.whole(b, k, dy, dx, 1), pick(self.cr, self.here, b, k, dy, dx))
+
+            self.guarded(b, k, run)
+
+    def drain(self):
+        for b, k, make in self.sent:
+            self.guarded(b, k, lambda: make().wait_send())
+
+
+FRONT = 7
+
+
+def cut_units(here, plan, ext, slot):
+    top = here.me * plan.share // LANES - plan.before
+    for base, chunks, count, first_unit, _, _ in plan.segments:
+        lo = jnp.clip(plan.per * here.me - first_unit, 0, count)
+        hi = jnp.clip(plan.per * here.me + plan.per - first_unit, 0, count)
+
+        def unit(u, carry):
+            block = u // chunks
+            row = base + block * (ROWS * chunks) + (u - block * chunks) - top
+            if chunks == 1:
+                value = ext[pl.ds(row, ROWS), :]
+            else:
+                value = ext[pl.ds(row, ROWS, stride=chunks), :]
+            slot[first_unit + u - plan.per * here.me] = value.astype(low_type)
+            return carry
+
+        lax.fori_loop(lo, hi, unit, 0)
+
+
+def forward_kernel(plans, zs, rows, *refs):
+    np_ = len(plans)
+    feed = iter(refs)
+    take = lambda count: tuple(next(feed) for _ in range(count))
+    one = lambda: next(feed)
+    raw_hbm = take(np_)
+    noisy, positions, basis, chosen = take(4)
+    units = take(np_)
+    stream = take(LAYERS + 1)
+    mods = take(LAYERS)
+    sums = take(LAYERS)
+    modulator, condition, time_pre = take(3)
+    saved_out = [take(len(SAVED)) for _ in range(LAYERS)]
+    from_prev, from_next, slots = take(np_), take(np_), take(np_)
+    raw_sem, halo_send, halo_recv, front_sem, load_sem, save_sem = take(6)
+    gather_sems = take(8)
+    here = Place(zs)
+    here.greet()
+    root = plans[0]
+    front_units = root.segments[FRONT][3]
+    front_planes = min(zs, -(-front_units // (8 * root.per)))
+    buckets = [(root, units[0], slots[0], 0, front_planes)]
+    buckets += [(plans[1 + i], units[1 + i], slots[1 + i], 0, zs) for i in range(LAYERS)]
+    buckets += [(root, units[0], slots[0], front_planes, zs)]
+    gather = Gather(here, buckets, gather_sems)
+    last = len(buckets) - 1
+    starts = [[0]] + [[1 + i] for i in range(LAYERS)]
+    starts[-1].append(last)
+
+    def prepare(*scratch):
+        raw, ext, tail = (scratch[i * np_ : (i + 1) * np_] for i in range(3))
+        loads = [pltpu.make_async_copy(raw_hbm[i], raw[i].at[pl.ds(8, p.raw)], raw_sem.at[i]) for i, p in enumerate(plans)]
+        for copy in loads:
+            copy.start()
+        lane = lax.broadcasted_iota(jnp.int32, (64, LANES), 1)
+        halos = []
+        for i, p in enumerate(plans):
+            shift = lax.rem(here.me * p.share, LANES)
+            delta = (here.me + 1) * p.share // LANES - here.me * p.share // LANES
+            raw[i][pl.ds(0, 8), :] = jnp.zeros((8, LANES), full_type)
+            ext[i][pl.ds(0, p.before), :] = jnp.zeros((p.before, LANES), full_type)
+            ext[i][pl.ds(p.before + p.raw, p.after), :] = jnp.zeros((p.after, LANES), full_type)
+            loads[i].wait()
+
+            def align(j):
+                row = pl.multiple_of(j * 64, 64)
+                level = pltpu.roll(raw[i][pl.ds(row + 8, 64), :], shift, 1)
+                above = pltpu.roll(raw[i][pl.ds(row + 7, 64), :], shift, 1)
+                ext[i][pl.ds(row + p.before, 64), :] = jnp.where(lane >= shift, level, above)
+
+            loop(p.raw // 64, align)
+            tail[i][...] = ext[i][pl.ds(delta, p.before + 8), :]
+            if i == 0:
+                here.met()
+            halos.append(remote(ext[i].at[pl.ds(p.before, p.after)], from_next[i], halo_send.at[2 * i], halo_recv.at[2 * i], here.prev))
+            halos.append(remote(tail[i], from_prev[i], halo_send.at[2 * i + 1], halo_recv.at[2 * i + 1], here.following))
+            halos[-2].start()
+            halos[-1].start()
+        for i, p in enumerate(plans):
+            delta = (here.me + 1) * p.share // LANES - here.me * p.share // LANES
+            halos[2 * i].wait()
+            halos[2 * i + 1].wait()
+            ext[i][pl.ds(0, p.before + 8), :] += from_prev[i][...]
+            ext[i][pl.ds(p.before + delta, p.after), :] += from_next[i][...]
+            cut_units(here, p, ext[i], slots[i])
+            for b in starts[i]:
+                gather.start(b)
+
+    f32 = lambda *dims: pltpu.VMEM(dims, full_type)
+    pl.run_scoped(
+        prepare,
+        *[f32(p.raw + 8, LANES) for p in plans],
+        *[f32(p.ext, LANES) for p in plans],
+        *[f32(p.before + 8, LANES) for p in plans],
+    )
+    for event in gather.events(0):
+        event()
+    gather.complete(0)
+
+    def compute(front, w_qkv, w_o, w_1, w_2, w_mod, raw_bias, *held):
+        copy = pltpu.make_async_copy(units[0].at[pl.ds(0, front_units)], front, front_sem)
+        copy.start()
+        copy.wait()
+        matrix = lambda number, blocks: front_matrix(front, root, number, blocks)
+        vector = lambda number: row_vector(front[pl.ds(root.segments[number][3], 1)], D // LANES)
+        events = spread(gather.events(1), (1, 1, 1, 1))
+        stream[0][...] = dot(noisy[...], matrix(0, 1)) + vector(1) + positions[...]
+        for event in events[0]:
+            event()
+        pre = dot(basis[...], matrix(2, FREQ // ROWS)) + vector(3)
+        time_pre[...] = pre
+        act = silu_parts(pre)[0].astype(low_type)
+        total = dot(act, matrix(4, D // ROWS)) + vector(5)
+        few = basis.shape[0]
+        first = root.segments[6][3]
+        picked = dot(chosen[...], front[pl.ds(first, root.segments[6][2])].reshape(-1, LANES))
+        total = total + jnp.concatenate([picked[i * few : (i + 1) * few, :] for i in range(D // LANES)], axis=1)
+        condition[...] = total
+        modulator[...] = silu_parts(total)[0].astype(low_type)
+        for group in events[1:]:
+            for event in group:
+                event()
+        for ordinal in range(LAYERS):
+            gather.complete(1 + ordinal)
+            queue = gather.events(2 + ordinal)
+            layer_forward_body(
+                plans[1 + ordinal], rows, stream[ordinal], modulator, mods[ordinal], units[1 + ordinal],
+                stream[ordinal + 1], sums[ordinal], saved_out[ordinal], held, (w_qkv, w_o, w_1, w_2, w_mod), raw_bias,
+                load_sem, save_sem, spread(queue, (18, 9, 12, 3, 12)),
+            )
+        gather.complete(last)
+
+    plan = plans[1]
+    bias_units = plan.units - plan.segments[5][3]
+    pl.run_scoped(
+        compute,
+        pltpu.VMEM((front_units, ROWS, LANES), low_type),
+        *[segment_scratch(plan, i) for i in range(5)],
+        pltpu.VMEM((bias_units, ROWS, LANES), low_type),
+        *[pltpu.VMEM((rows, width), kind) for _, width, kind in SAVED],
+    )
+    gather.drain()
+
+
+def front_matrix(front, plan, number, blocks):
+    _, chunks, _, first, _, _ = plan.segments[number]
+    columns = [jnp.concatenate([front[first + b * chunks + c] for b in range(blocks)], axis=0) for c in range(chunks)]
+    return jnp.concatenate(columns, axis=1)
+
+
+def layer_forward_body(plan, rows, x, modulator, mod, units, out, sums, saved_out, held, weights, raw_bias, load_sem, save_sem, events):
+    ns = len(SAVED)
+    h1, qkv, heads, attn, middle, h2, pre, mlp = held
+    w_qkv, w_o, w_1, w_2, w_mod = weights
+    bias_first = plan.segments[5][3]
+    loads = [pltpu.make_async_copy(segment_ref(units, plan, i), weights[i], load_sem.at[i]) for i in range(5)]
+    bias_load = pltpu.make_async_copy(units.at[pl.ds(bias_first, raw_bias.shape[0])], raw_bias, load_sem.at[5])
+    bias_load.start()
+    for i in (4, 0, 1, 2, 3):
+        loads[i].start()
+    saves = [pltpu.make_async_copy(held[i], saved_out[i], save_sem.at[i]) for i in range(ns)]
+    part = lambda s, i: mod[pl.ds(s, 1), i * D : (i + 1) * D]
+    per = SEQ // CHUNK
+    wide_at = lambda j: pl.ds(pl.multiple_of(j * WIDE, WIDE), WIDE)
+    chunk_at = lambda i: pl.ds(pl.multiple_of(i * CHUNK, CHUNK), CHUNK)
+    bias_load.wait()
+
+    def bias(number):
+        _, _, count, first, shape, _ = plan.segments[number]
+        return row_vector(raw_bias[pl.ds(first - bias_first, count)], shape[0] // LANES)
+
+    loads[4].wait()
+    mod[...] = jnp.broadcast_to(bias(10), mod.shape)
+    value_of = modulator[...]
+
+    def modulate(j):
+        mod[:, wide_at(j)] += dot(value_of, block_of(w_mod, 0, D // ROWS, 2 * j, 2))
+
+    busy_loop(6 * D // WIDE, modulate, events[0])
+
+    def norm_a(i):
+        s = i // per
+        hat, _ = norm_parts(x[chunk_at(i), :])
+        h1[chunk_at(i), :] = (hat * (1.0 + part(s, 1)) + part(s, 0)).astype(low_type)
+
+    loop(rows // CHUNK, norm_a)
+    saves[0].start()
+    loads[0].wait()
+    first_bias, value_bias = bias(5), bias(6)
+
+    def project_with(base, given, events):
+        pieces = D // WIDE
+
+        def project(j):
+            value = dot(h1[...], block_of(w_qkv, 0, D // ROWS, 2 * (base + j), 2))
+            cols = wide_at(base + j)
+            if given is not None:
+                value = value + mlp[0:1, wide_at(j)]
+            qkv[:, cols] = value.astype(low_type)
+
+        if given is not None:
+            mlp[0:1, :] = given
+        busy_loop(pieces, project, events)
+
+    third = spread(events[1], (1, 1, 1))
+    project_with(0, first_bias, third[0])
+    project_with(D // WIDE, None, third[1])
+    project_with(2 * D // WIDE, value_bias, third[2])
+    saves[1].start()
+    first = head_masks()
+
+    def attend(i):
+        s, j = i // (HEADS // 2), i % (HEADS // 2)
+        at = pl.ds(pl.multiple_of(s * SEQ, SEQ), SEQ)
+        cut = lambda o: qkv[at, pl.ds(pl.multiple_of(o * D + j * LANES, LANES), LANES)]
+        q, k, v = cut(0), cut(1), cut(2)
+        q = q * jnp.asarray(HD ** (-0.5), low_type)
+        zero = jnp.zeros_like(q)
+        halves = []
+        for mask in (first, ~first):
+            probs = softmax_f32(dot_nt(jnp.where(mask, q, zero), k)).astype(low_type)
+            halves.append(dot(probs, v))
+        heads[at, pl.ds(pl.multiple_of(j * LANES, LANES), LANES)] = jnp.where(first, halves[0], halves[1]).astype(low_type)
+
+    busy_loop(attention_pairs(rows), attend, events[2])
+    saves[2].start()
+    loads[1].wait()
+    attn[...] = jnp.broadcast_to(bias(7), (rows, D))
+
+    def project_out(j):
+        attn[:, wide_at(j)] += dot(heads[...], block_of(w_o, 0, D // ROWS, 2 * j, 2))
+
+    busy_loop(D // WIDE, project_out, events[3])
+    saves[3].start()
+    zero_sum = jnp.zeros((1, D), full_type)
+
+    def norm_m(i, total):
+        s = i // per
+        value = attn[chunk_at(i), :]
+        mid = x[chunk_at(i), :] + part(s, 2) * value
+        middle[chunk_at(i), :] = mid
+        hat, _ = norm_parts(mid)
+        h2[chunk_at(i), :] = (hat * (1.0 + part(s, 4)) + part(s, 3)).astype(low_type)
+        return total + rows_sum(value * value)
+
+    attn_sum = lax.fori_loop(0, rows // CHUNK, norm_m, zero_sum)
+    saves[4].start()
+    saves[5].start()
+    loads[2].wait()
+    loads[3].wait()
+    pre[0:1, :] = bias(8)
+    mlp[...] = jnp.broadcast_to(bias(9), (rows, D))
+
+    def feed(j):
+        value = dot(h2[...], block_of(w_1, 0, D // ROWS, 2 * j, 2)) + pre[0:1, wide_at(j)]
+        pre[:, wide_at(j)] = value
+        act = gelu_parts(value)[0].astype(low_type)
+        mlp[...] += dot(act, block_of(w_2, j * (WIDE // ROWS), WIDE // ROWS, 0, D // LANES))
+
+    busy_loop(FF // WIDE, feed, events[4])
+    saves[6].start()
+    saves[7].start()
+
+    def finish(i, carry):
+        value = mlp[chunk_at(i), :]
+        result = middle[chunk_at(i), :] + part(i // per, 5) * value
+        out[chunk_at(i), :] = result
+        return (carry[0] + rows_sum(result * result), carry[1] + rows_sum(value * value))
+
+    out_sum, mlp_sum = lax.fori_loop(0, rows // CHUNK, finish, (zero_sum, zero_sum))
+    sums[...] = jnp.zeros(sums.shape, full_type)
+    sums[0:1, :] = out_sum
+    sums[1:2, :] = attn_sum
+    sums[2:3, :] = mlp_sum
+    for copy in saves:
+        copy.wait()
+
+
+def forward_call(plans, raws, noisy, positions, basis, chosen):
+    n = plans[0].devices
+    zs = n // 8
+    rows, few = noisy.shape[0], basis.shape[0]
+    dma = pltpu.SemaphoreType.DMA
+    np_, nb = len(plans), len(plans) + 1
+    vm = pl.BlockSpec(memory_space=pltpu.VMEM)
+    hbm = pl.BlockSpec(memory_space=pltpu.HBM)
+    shape = jax.ShapeDtypeStruct
+    saved_shapes = [shape((rows, width), kind) for _, width, kind in SAVED]
+    out_shape = [shape((n * p.per, ROWS, LANES), low_type) for p in plans]
+    out_shape += [shape((rows, D), full_type)] * (LAYERS + 1)
+    out_shape += [shape((few, 6 * D), full_type)] * LAYERS + [shape((8, D), full_type)] * LAYERS
+    out_shape += [shape((few, D), low_type), shape((few, D), full_type), shape((few, D), full_type)]
+    out_shape += saved_shapes * LAYERS
+    scratch = [pltpu.VMEM((p.before + 8, LANES), full_type) for p in plans]
+    scratch += [pltpu.VMEM((p.after, LANES), full_type) for p in plans]
+    scratch += [pltpu.VMEM((p.per, ROWS, LANES), low_type) for p in plans]
+    scratch += [dma((np_,)), dma((2 * np_,)), dma((2 * np_,)), dma, dma((6,)), dma((len(SAVED),))]
+    scratch += [dma((nb,)), dma((nb * (2 * (zs - 1) + 10 * zs),)), dma((nb, 2, zs)), dma((nb, zs)), dma((nb, zs, 2))]
+    scratch += [dma((nb, zs)), dma((nb, zs, 2)), dma((nb, zs, 2, 2))]
+    results = pl.pallas_call(
+        functools.partial(forward_kernel, plans, zs, rows),
+        out_shape=out_shape,
+        in_specs=[hbm] * np_ + [vm] * 4,
+        out_specs=[hbm] * np_ + [vm] * (LAYERS + 1 + 2 * LAYERS + 3) + [hbm] * (len(SAVED) * LAYERS),
+        scratch_shapes=scratch,
+        compiler_params=pltpu.CompilerParams(collective_id=0, has_side_effects=True, vmem_limit_bytes=62 * MB),
+        name="gather_and_forward",
+    )(*raws, noisy, positions, basis, chosen)
+    feed = iter(results)
+    take = lambda count: [next(feed) for _ in range(count)]
+    units, stream, mods, sums = take(np_), take(LAYERS + 1), take(LAYERS), take(LAYERS)
+    modulator, condition, time_pre = take(3)
+    return units, stream, mods, sums, modulator, condition, time_pre, [take(len(SAVED)) for _ in range(LAYERS)]
+
+
 def model_step(layer_lists, pieces, latents, noise, times, labels, dropped, features, devices):
     sample_total = latents.shape[0] * devices
     residual, modulator, embed_saved = embed_forward(
@@ -1671,59 +2215,32 @@
     return vector.astype(full_type).reshape(1, -1)
 
 
-def embed_step(pieces, table_rows, latents, noise, times):
-    mixing = times[:, None, None]
-    noisy_bf = ((1.0 - mixing) * latents + mixing * noise).astype(low_type)
-    tokens = linear_fwd(noisy_bf, pieces[0]) + pieces[1] + position_table()
-    basis_bf = time_features(times).astype(low_type)
-    time_pre = linear_fwd(basis_bf, pieces[2]) + pieces[3]
-    time_act = jax.nn.silu(time_pre).astype(low_type)
-    condition = linear_fwd(time_act, pieces[4]) + pieces[5] + table_rows.astype(full_type)
-    saved = (noisy_bf, basis_bf, time_pre, time_act, condition)
-    return (tokens, jax.nn.silu(condition).astype(low_type), saved)
-
-
-def embed_step_back(pieces, saved, classes, grad_tokens, grad_modulator):
-    noisy_bf, basis_bf, time_pre, time_act, condition = saved
-    onehot = (classes[:, None] == jnp.arange(CLS, dtype=jnp.int32)[None, :]).astype(low_type)
-    return embed_backward(
-        pieces, (noisy_bf, basis_bf, time_pre, time_act, onehot, condition), grad_tokens, grad_modulator
-    )
-
-
 def by_kernels(plan, root_plan, layer_flat, root_flat, data, devices):
     latents, noise, times, labels, dropped, features = data
     samples = latents.shape[0]
     sample_total = samples * devices
     rows = samples * SEQ
+    few = up(samples, ROWS)
+    wide = D // LANES
     plans = (root_plan,) + (plan,) * LAYERS
     raws = [to_rows(root_flat, root_plan)]
     raws += [to_rows(layer_flat[ordinal], plan) for ordinal in range(LAYERS)]
-    root_units, *layer_units = gather_units(plans, raws)
-    early = [matrix_of(root_units, root_plan, i) if i % 2 == 0 else vector_of(root_units, root_plan, i) for i in range(6)]
+    mixing = times[:, None, None]
+    noisy_bf = ((1.0 - mixing) * latents + mixing * noise).astype(low_type)
+    positions = jnp.tile(position_table(), (samples, 1))
+    basis_bf = time_features(times).astype(low_type)
     classes = jnp.where(dropped == 1, CLS - 1, labels)
-    table_first = root_plan.segments[6][3]
-    table = root_units[table_first : table_first + root_plan.segments[6][2]].reshape(-1, LANES)
-    wide = D // LANES
-    table_rows = jnp.stack(
-        [lax.dynamic_slice(table, (classes[s] * wide, 0), (wide, LANES)).reshape(D) for s in range(samples)]
-    )
-    tokens, modulator, embed_saved = embed_step(early, table_rows, latents, noise, times)
-    few = up(samples, ROWS)
-    modulator_rows = jnp.pad(modulator, ((0, few - samples), (0, 0)))
-    residual = tokens.reshape(rows, D)
-    inputs, mods, kept, sums = [], [], [], []
-    for ordinal in range(LAYERS):
-        units = layer_units[ordinal]
-        b_q, b_v, b_o, b_1, b_2, b_mod = (as_row(vector_of(units, plan, i)) for i in range(5, 11))
-        bias_qkv = jnp.concatenate([b_q, jnp.zeros_like(b_q), b_v], axis=1)
-        mods.append(mods_call(plan, modulator_rows, b_mod, units))
-        inputs.append(residual)
-        residual, total, saved = layer_forward_call(
-            plan, residual, mods[ordinal], (bias_qkv, b_o, b_1, b_2), units
-        )
-        kept.append(saved)
-        sums.append(total)
+    extra = lambda value: jnp.pad(value, ((0, few - samples),) + ((0, 0),) * (value.ndim - 1))
+    wanted = jnp.pad(classes, (0, few - samples), constant_values=-1)
+    wanted = jnp.where(wanted < 0, -wide, wanted * wide)[None, :] + jnp.arange(wide)[:, None]
+    wanted = jnp.where(wanted < 0, -1, wanted).reshape(-1, 1)
+    table_rows = root_plan.segments[6][2] * ROWS
+    chosen = (wanted == jnp.arange(table_rows, dtype=jnp.int32)[None, :]).astype(low_type)
+    units, stream, mods, sums, modulator_rows, condition, time_pre, kept = forward_call(
+        plans, raws, noisy_bf.reshape(rows, PD), positions, extra(basis_bf), chosen
+    )
+    root_units, *layer_units = units
+    residual = stream[-1]
     target = jnp.pad((noise - latents).reshape(rows, PD), ((0, 0), (0, LANES - PD)))
     weight_t = jnp.broadcast_to(jnp.pad(1.0 + 2.0 * times, (0, 8 - samples))[:, None], (8, LANES))
     w_h = jnp.pad(vector_of(root_units, root_plan, 15), ((0, 0), (0, LANES - PD)))
@@ -1738,7 +2255,7 @@
     for ordinal in reversed(range(LAYERS)):
         units = layer_units[ordinal]
         grad, grad_mod, bias_grad, grads = layer_backward_call(
-            plan, inputs[ordinal], grad, mods[ordinal], kept[ordinal], units
+            plan, stream[ordinal], grad, mods[ordinal], kept[ordinal], units
         )
         low_mod = jnp.pad(grad_mod.astype(low_type), ((0, few - grad_mod.shape[0]), (0, 0)))
         grads, cond_part = mods_back_call(plan, modulator_rows, low_mod, units, grads)
@@ -1746,7 +2263,11 @@
         cuts = jnp.split(bias_grad[0], (D, 2 * D, 3 * D, 3 * D + FF))
         grad_b_mod = jnp.sum(low_mod.astype(full_type), axis=0)
         layer_grads[ordinal] = put_units(grads, plan, 5, cuts + [grad_b_mod])
-    embed_grads = embed_step_back(early, embed_saved, classes, grad.reshape(samples, SEQ, D), grad_cond)
+    pieces = {4: matrix_of(root_units, root_plan, 4), 2: None, 0: None}
+    onehot = (classes[:, None] == jnp.arange(CLS, dtype=jnp.int32)[None, :]).astype(low_type)
+    time_pre = time_pre[:samples]
+    embed_saved = (noisy_bf, basis_bf, time_pre, jax.nn.silu(time_pre).astype(low_type), onehot, condition[:samples])
+    embed_grads = embed_backward(pieces, embed_saved, grad.reshape(samples, SEQ, D), grad_cond)
     cuts = jnp.split(bias_grads[0], (PH, 2 * PH, 2 * PH + ZD, 2 * PH + ZD + 2 * D))
     for number, value in zip((8, 10, 12), cuts):
         root_grads = put_units(root_grads, root_plan, number, [value])
@@ -1759,8 +2280,8 @@
     numbers = stats[0].reshape(-1)
     shard_root = rows_out[0].reshape(-1)[: root_plan.share]
     shard_layers = jnp.stack([r.reshape(-1)[: plan.share] for r in rows_out[1:]])
-    stream = numbers[1 : 1 + 3 * LAYERS].reshape(LAYERS, 3)
-    return (shard_layers, shard_root, numbers[0], stream, jnp.sum(stats[1]))
+    stream_sums = numbers[1 : 1 + 3 * LAYERS].reshape(LAYERS, 3)
+    return (shard_layers, shard_root, numbers[0], stream_sums, jnp.sum(stats[1]))
 
 
 def by_collectives(layer_flat, root_flat, data, devices):

time: 1130 us -> 937 us (0.83)
  Pallas kernels: 1000 us -> 830 us
  local copies, waits for them, and re-layouts: 78.5 us -> 57.6 us
    pallas_call x1, Pallas kernels: 460 us -> 329 us  [reduce_units(): pl.pallas_call(functools.partial(reduce_kernel, plans, zs), out_shape=out...]
    pallas_call x5 -> x1, Pallas kernels: 372 us -> 333 us  [forward_call(): pl.pallas_call(functools.partial(forward_kernel, plans, zs, rows), out_sh...]
    unnamed x69 -> x48, local copies, waits for them, and re-layouts: 24.4 us -> 4.83 us
where the time goes in v2:
time: 937 us; the launch traced here: 929 us
  Pallas kernels  830 us (89%)
  local copies, waits for them, and re-layouts  57.6 us (6%)
  other arithmetic  33.6 us (4%)
    pallas_call x1, Pallas kernels, forward_call(): pl.pallas_call(functools.partial(forward_kernel, plans, zs, rows), out_sh...  333 us
    pallas_call x1, Pallas kernels, reduce_units(): pl.pallas_call(functools.partial(reduce_kernel, plans, zs), out_shape=out...  329 us
    pallas_call x2, Pallas kernels, layer_backward_call(): pl.pallas_call(functools.partial(layer_backward_kernel, plan, rows), out_...  102 us
    pallas_call x1, Pallas kernels, top_call(): pl.pallas_call(functools.partial(top_kernel, plan, rows, sample_total), o...  49 us

profile of v2, /device:TPU:6, one launch (start us, length us, event | category | flops | bytes accessed | tf_op | source)
XLA Modules:
  0.0 929.1 jit_solution(1355159898338523596)
XLA Ops:
  6.9 1.2 tile.20
  8.2 1.3 fusion.1.refs_6_
  9.4 1.1 pad_bitcast_fusion.2.refs_0_
  10.6 13.9 %slice_reduce_fusion = (f32[332112]{0:T(1024)S(1)}, f32[332112]{0:T(1024)S(1)}) fusion(f32[2,332112]{1,0:T(2,128)S(1)} %copy-done.1), kind=kLoop, calls=%fused_computation.13 | loop fusion | bytes 5313792 | tf_op jit(solution)/shard_map/slice | solution.py:2227
  24.4 1.9 pad_bitcast_fusion
  26.3 333.0 %gather_and_forward.1 = (bf16[4992,16,128]{2,1,0:T(8,128)(2,1)}, bf16[5248,16,128]{2,1,0:T(8,128)(2,1)}, bf16[5248,16,128]{2,1,0:T(8,128)(2,1)}, f32[512,768]{1,...) custom-call(f32[2496,128]{1,0:T(8,128)} %pad_bitcast_fusion.2.refs_0, ...), custom_call_target="tpu_custom_call" | custom-call | tf_op jit(solution)/shard_map/gather_and_forward/pallas_call | solution.py:2121
  363.7 1.3 slice_bitcast_fusion.1
  367.1 1.5 slice.139
  368.6 49.0 %projector_and_head.1 = (f32[512,768]{1,0:T(8,128)}, f32[8,128]{1,0:T(8,128)}, f32[16,768]{1,0:T(8,128)}, f32[1,6528]{1,0:T(1,128)}, f32[768,128]{1,0:T(8,128)}, /*index=5*/bf16[4992,16,128]{2,1,0:T(8,128)(2,1)}) custom-call(f32[512,768]{1,0:T(8,128)} %get-tuple-element.60.x, bf16[512,768]{1,0:T(8,128)(2,1)} %bitcast.127, f32[512,128]{1,0:T(8,128)} %pad.116.target, ...), custom_call_target="tpu_custom_call" | custom-call | tf_op jit(solution)/shard_map/projector_and_head/pallas_call | solution.py:1590
  417.6 1.3 slice_reduce_fusion.19
  419.6 1.2 slice.141
  424.8 1.0 slice.191
  427.0 50.6 %layer_backward.2 = (f32[512,768]{1,0:T(8,128)}, f32[8,4608]{1,0:T(8,128)}, f32[1,6144]{1,0:T(1,128)}, bf16[5248,16,128]{2,1,0:T(8,128)(2,1)}) custom-call(f32[512,768]{1,0:T(8,128)} %get-tuple-element.67.x, f32[512,768]{1,0:T(8,128)} %get-tuple-element.68.grad_in, f32[16,4608]{1,0:T(8,128)} %get-tuple-element.69.mod, ...), custom_call_target="tpu_custom_call" | custom-call | tf_op jit(solution)/shard_map/layer_backward/pallas_call | solution.py:1388
  478.5 0.9 convert_element_type.244
  479.5 8.8 modulation_back.2
  489.0 51.0 %layer_backward.3 = (f32[512,768]{1,0:T(8,128)}, f32[8,4608]{1,0:T(8,128)}, f32[1,6144]{1,0:T(1,128)}, bf16[5248,16,128]{2,1,0:T(8,128)(2,1)}) custom-call(f32[512,768]{1,0:T(8,128)} %get-tuple-element.66.x, f32[512,768]{1,0:T(8,128)} %get-tuple-element.79.grad_in, f32[16,4608]{1,0:T(8,128)} %get-tuple-element.80.mod, ...), custom_call_target="tpu_custom_call" | custom-call | tf_op jit(solution)/shard_map/layer_backward/pallas_call | solution.py:1388
  539.9 1.6 fusion.29
  542.1 8.8 modulation_back.3
  554.2 1.4 reshape.336
  555.6 1.2 copy.32
  556.8 1.5 convolution_convert_fusion
  558.3 1.3 reshape.339
  559.9 1.0 copy-done.5
  561.6 2.2 constant_dynamic-update-slice_fusion.21.refs_0_
  563.8 329.2 %reduce_units.1 = (f32[2496,128]{1,0:T(8,128)}, f32[2624,128]{1,0:T(8,128)}, f32[2624,128]{1,0:T(8,128)}, f32[2,8,128]{2,1,0:T(8,128)}, bf16[4,2,2,156,16,128]{5...) custom-call(bf16[4992,16,128]{2,1,0:T(8,128)(2,1)} %constant_dynamic-update-s, ...), custom_call_target="tpu_custom_call" | custom-call | tf_op jit(solution)/shard_map/reduce_units/pallas_call | solution.py:556
  893.0 1.3 slice_reduce_fusion.9
  895.6 1.5 slice.155
  897.1 6.2 stack.21
  904.1 6.2 stack.22
  910.4 2.6 multiply_subtract_fusion.1
  913.0 1.3 copy-done.6
  915.1 12.7 %multiply_subtract_fusion = (f32[2,332112]{1,0:T(2,128)}, f32[2,332112]{1,0:T(2,128)}, f32[2,332112]{1,0:T(2,128)}) fusion(f32[2,332112]{1,0:T(2,128)S(1)} %copy-done.2, f32[]{:T(128)S(6)} %div.60, f32[1,332112]{1,0:T(1,128)S(1)} %stack.22, f32[1,332112]{1,0:T(1,128)S(1)} %stack.21, f32[2,332112]{1,0:T(2,128)S(1)} %copy-done.6, f32[2,332112]{1,0:T(2,128)S(1)} %copy-done.7), kind=kLoop, calls=%fused_computation.4 | loop fusion | flops 10627584 | bytes 18598276 | tf_op jit(solution)/shard_map/sub | solution.py:2180
  (124 shorter events, 25.6 us)
Async XLA Ops:
  6.8 2.6 copy-start.3
  6.9 3.7 copy-start.1
  427.0 52.6 %copy-start = (bf16[16,768]{1,0:T(8,128)(2,1)S(1)}, bf16[16,768]{1,0:T(8,128)(2,1)}, u32[]{:S(2)}) copy-start(bf16[16,768]{1,0:T(8,128)(2,1)} %get-tuple-element.61.modulator) | copy-start | bytes 73732
  539.9 1.9 copy-start.13
  539.9 2.1 copy-start.12
  542.1 9.6 %copy-start.14 = (f32[16,768]{1,0:T(8,128)S(1)}, f32[16,768]{1,0:T(8,128)}, u32[]{:S(2)}) copy-start(f32[16,768]{1,0:T(8,128)} %get-tuple-element.99) | copy-start | bytes 147460
  559.6 1.3 copy-start.5
  895.6 8.4 copy-start.8
  904.0 6.3 copy-start.4
  904.0 6.3 copy-start.9
  904.0 6.3 copy-start.10
  904.0 6.4 copy-start.11
  910.4 2.7 copy-start.2
  910.4 3.9 copy-start.6
  910.4 4.7 copy-start.7

commit v3 on v2

--- a/solution.py
+++ b/solution.py
@@ -2134,6 +2134,817 @@
     return units, stream, mods, sums, modulator, condition, time_pre, [take(len(SAVED)) for _ in range(LAYERS)]
 
 
+class Reduce:
+    def __init__(self, here, buckets, first, buffers, sems, frees):
+        self.here = here
+        self.buckets = buckets
+        self.first = first
+        self.kept, self.two, self.three, self.four, self.ring, self.other, self.own = buffers
+        self.s1, self.r1, self.s2, self.r2, self.s3, self.r3, self.s4, self.r4, self.load_sem = sems
+        self.free_two, self.free_three, self.free_four = frees
+        self.planes = list(range(1, here.zs)) + [0]
+        self.groups = [(b, k) for b in range(len(buckets)) for k in self.planes]
+        self.order = ((1, 1), (1, 0), (0, 1), (0, 0))
+
+    def limits(self, b):
+        return self.buckets[b][2:4]
+
+    def meets(self, b, k):
+        lo, hi = self.limits(b)
+        if lo == 0 and hi == self.here.zs:
+            return None
+        plane = lax.rem(self.here.z + self.here.zs - k, self.here.zs)
+        return (plane >= lo) & (plane < hi)
+
+    def guarded(self, b, k, run):
+        test = self.meets(b, k)
+        if test is None:
+            run()
+        else:
+            pl.when(test)(run)
+
+    def overlaps(self, b, other):
+        return self.limits(b)[0] < self.limits(other)[1] and self.limits(other)[0] < self.limits(b)[1]
+
+    def before(self, b, k, run):
+        for other in range(b - 1, -1, -1):
+            if self.overlaps(b, other):
+                self.guarded(b, k, lambda: self.guarded(other, k, run))
+                return
+
+    def after(self, b, k, run):
+        for other in range(b + 1, len(self.buckets)):
+            if self.overlaps(b, other):
+                self.guarded(b, k, lambda: self.guarded(other, k, run))
+                self.after_rest(b, other, k, run)
+                return
+
+    def after_rest(self, b, done, k, run):
+        for other in range(done + 1, len(self.buckets)):
+            if self.overlaps(b, other) and not self.overlaps(done, other):
+                self.guarded(b, k, lambda: self.guarded(other, k, run))
+
+    def slot(self, b, k, dy, dx, dc):
+        plan, grads = self.buckets[b][:2]
+        return grads.at[pl.ds(self.here.slot(k, dy, dx, dc) * plan.per, plan.per)]
+
+    def landed(self, b, k, dy, dx):
+        return self.first[b].at[self.here.zero + k, self.here.zero + dy, self.here.zero + dx]
+
+    def sibling(self, b, k, dy, dx):
+        here = self.here
+        return remote(
+            self.slot(b, k, dy, dx, 1), self.landed(b, k, dy, dx), pick(self.s1, here, b, k, dy, dx), pick(self.r1, here, b, k, dy, dx), here.cpeer
+        )
+
+    def open(self, b):
+        for k in self.planes:
+
+            def run(k=k):
+                for dy, dx in self.order:
+                    self.sibling(b, k, dy, dx).start()
+
+            self.guarded(b, k, run)
+
+    def half(self, b):
+        return self.buckets[b][0].half
+
+    def buffer(self, ref, b, *spots):
+        view = ref.at[tuple(self.here.zero + s for s in spots)]
+        return view.at[pl.ds(0, self.half(b))]
+
+    def place_of(self, g, i):
+        return 6 if i == 3 else 3 * (g % 2) + i
+
+    def loads(self, g, i):
+        b, k = self.groups[g]
+        dy, dx = self.order[i]
+        per = self.buckets[b][0].per
+        here = self.here
+        at = self.place_of(g, i)
+        one = pltpu.make_async_copy(self.slot(b, k, dy, dx, 0), pick(self.ring, here, at).at[pl.ds(0, per)], pick(self.load_sem, here, at, 0))
+        two = pltpu.make_async_copy(self.landed(b, k, dy, dx), pick(self.other, here, i % 2).at[pl.ds(0, per)], pick(self.load_sem, here, at, 1))
+        return one, two
+
+    def prepare(self, g, i):
+        b, k = self.groups[g]
+        dy, dx = self.order[i]
+        one, two = self.loads(g, i)
+        one.start()
+        arrived(self.landed(b, k, dy, dx), pick(self.r1, self.here, b, k, dy, dx))
+        two.start()
+
+    def second(self, g, h, i):
+        b, k = self.groups[g]
+        dy, dx = self.order[i]
+        here, size = self.here, self.half(b)
+        src = pick(self.ring, here, self.place_of(g, i)).at[pl.ds(h * size, size)]
+        far = dx if h == 0 else dy
+        return remote(src, self.buffer(self.two[h], b, k, far), pick(self.s2, here, h, k, far), pick(self.r2, here, h, k, far), here.ypeer if h == 0 else here.xpeer)
+
+    def sends_of(self, g):
+        return [(h, i) for i, (dy, dx) in enumerate(self.order) for h in range(2) if (dy, dx)[h]]
+
+    def add(self, b, dst, at, one, one_at, two, two_at):
+        step = self.half(b) // 2
+
+        def body(i, carry):
+            span = lambda ref, off: ref[pl.ds(off + i * step, step)].astype(full_type)
+            dst[pl.ds(at + i * step, step)] = (span(one, one_at) + span(two, two_at)).astype(low_type)
+            return carry
+
+        lax.fori_loop(0, 2, body, 0)
+
+    def phase_one(self, g, i):
+        b, k = self.groups[g]
+        here, size = self.here, self.half(b)
+        if i == 0:
+            for h in range(2):
+                to_free = lambda h=h: pl.semaphore_wait(pick(self.free_two, here, h, k), 1)
+                self.before(b, k, to_free)
+
+        def run():
+            dy, dx = self.order[i]
+            if i == 0:
+                self.prepare(g, 0)
+            if i < 3:
+                self.prepare(g, i + 1)
+            for copy in self.loads(g, i):
+                copy.wait()
+            mine, theirs = pick(self.ring, here, self.place_of(g, i)), pick(self.other, here, i % 2)
+            for h, moves in enumerate((dy, dx)):
+                if moves:
+                    self.add(b, mine, h * size, mine, h * size, theirs, h * size)
+                    self.second(g, h, i).start()
+                else:
+                    self.add(b, self.buffer(self.kept[h], b, k, dx if h == 0 else dy), 0, mine, h * size, theirs, h * size)
+
+        self.guarded(b, k, run)
+
+    def third(self, g, h):
+        b, k = self.groups[g]
+        here = self.here
+        return remote(
+            self.buffer(self.two[h], b, k, 1), self.buffer(self.three[h], b, k), pick(self.s3, here, h, k), pick(self.r3, here, h, k), here.xpeer if h == 0 else here.ypeer
+        )
+
+    def phase_two(self, g, far):
+        b, k = self.groups[g]
+        here = self.here
+        if far:
+            for h in range(2):
+                self.before(b, k, lambda h=h: pl.semaphore_wait(pick(self.free_three, here, h, k), 1))
+
+        def run():
+            for h in range(2):
+                got, kept = self.buffer(self.two[h], b, k, far), self.buffer(self.kept[h], b, k, far)
+                arrived(got, pick(self.r2, here, h, k, far))
+                if far:
+                    self.add(b, got, 0, got, 0, kept, 0)
+                    self.third(g, h).start()
+                else:
+                    self.add(b, kept, 0, got, 0, kept, 0)
+
+        self.guarded(b, k, run)
+
+    def last(self, g, h):
+        b, k = self.groups[g]
+        here = self.here
+        return remote(self.buffer(self.three[h], b, k), self.buffer(self.four, b, h, k - 1), pick(self.s4, here, h, k - 1), pick(self.r4, here, h, k - 1), here.below(k))
+
+    def phase_three(self, g):
+        b, k = self.groups[g]
+        here, size = self.here, self.half(b)
+        if k:
+            self.before(b, k, lambda: pl.semaphore_wait(pick(self.free_four, here, k - 1), 1))
+
+        def run():
+            for h in range(2):
+                got, kept = self.buffer(self.three[h], b, k), self.buffer(self.kept[h], b, k, 0)
+                arrived(got, pick(self.r3, here, h, k))
+                if k:
+                    self.add(b, got, 0, got, 0, kept, 0)
+                    self.last(g, h).start()
+                else:
+                    step = size // 2
+
+                    def body(i, carry):
+                        part = pl.ds(i * step, step)
+                        self.own[pl.ds(h * size + i * step, step)] = got[part].astype(full_type) + kept[part].astype(full_type)
+                        return carry
+
+                    lax.fori_loop(0, 2, body, 0)
+
+        self.guarded(b, k, run)
+
+    def release_one(self, g):
+        b, k = self.groups[g]
+
+        def run():
+            for h, i in self.sends_of(g):
+                self.second(g, h, i).wait_send()
+
+        self.guarded(b, k, run)
+
+    def release_two(self, g):
+        b, k = self.groups[g]
+        here = self.here
+
+        def run():
+            for h in range(2):
+                self.third(g, h).wait_send()
+                if k:
+                    self.last(g, h).wait_send()
+
+        self.guarded(b, k, run)
+
+        def free():
+            for h in range(2):
+                two_from, three_from = (here.ypeer, here.xpeer) if h == 0 else (here.xpeer, here.ypeer)
+                pl.semaphore_signal(pick(self.free_two, here, h, k), inc=1, device_id=(two_from,), device_id_type=MESH)
+                pl.semaphore_signal(pick(self.free_three, here, h, k), inc=1, device_id=(three_from,), device_id_type=MESH)
+
+        self.after(b, k, free)
+
+    def collect(self, b, out, sem):
+        here, size = self.here, self.half(b)
+
+        def run():
+            for h in range(2):
+                for k in range(1, here.zs):
+                    arrived(self.buffer(self.four, b, h, k - 1), pick(self.r4, here, h, k - 1))
+                step = size // 2
+
+                def body(i, carry):
+                    part = pl.ds(i * step, step)
+                    where = pl.ds(h * size + i * step, step)
+                    value = self.own[where]
+                    for k in range(1, here.zs):
+                        value = value + self.buffer(self.four, b, h, k - 1)[part].astype(full_type)
+                    self.own[where] = value
+                    return carry
+
+                lax.fori_loop(0, 2, body, 0)
+            copy = pltpu.make_async_copy(self.own.at[pl.ds(0, 2 * size)], out, sem)
+            copy.start()
+            copy.wait()
+
+        self.guarded(b, 0, run)
+
+        def free():
+            for k in range(1, here.zs):
+                pl.semaphore_signal(pick(self.free_four, here, k - 1), inc=1, device_id=(here.above(k),), device_id_type=MESH)
+
+        self.after(b, 0, free)
+
+    def steps(self, g, outs, sem):
+        zs = self.here.zs
+        total = len(self.groups)
+        found = []
+        if (g - 2) % zs == 0 and 0 < (g - 2) // zs <= len(self.buckets):
+            b = (g - 2) // zs - 1
+            found.append(functools.partial(self.collect, b, outs[b], sem))
+        if g < total:
+            if g >= 2:
+                found.append(lambda: self.release_one(g - 2))
+            found += [functools.partial(self.phase_one, g, i) for i in range(4)]
+        if 0 <= g - 1 < total:
+            found += [functools.partial(self.phase_two, g - 1, 1), functools.partial(self.phase_two, g - 1, 0)]
+        if 0 <= g - 2 < total:
+            found.append(functools.partial(self.phase_three, g - 2))
+        if 0 <= g - 3 < total:
+            found.append(lambda: self.release_two(g - 3))
+        return found
+
+    def close(self):
+        total = len(self.groups)
+        for g in (total - 2, total - 1):
+            self.release_one(g)
+        for b in range(len(self.buckets)):
+            for k in self.planes:
+
+                def run(b=b, k=k):
+                    for dy, dx in self.order:
+                        self.sibling(b, k, dy, dx).wait_send()
+
+                self.guarded(b, k, run)
+
+
+def unpack_rows(here, plan, units_f, rows_f, flat_f, held_before):
+    top = here.me * plan.share // LANES - plan.margin
+    for origin, chunks, count, first_unit, _, _ in plan.segments:
+        lo = jnp.clip(plan.per * here.me - held_before - first_unit, 0, count)
+        hi = jnp.clip(plan.per * here.me + plan.per + plan.units_after - first_unit, 0, count)
+
+        def unit(u, carry):
+            block = u // chunks
+            row = origin + block * (ROWS * chunks) + (u - block * chunks) - top
+            value = units_f[first_unit + u - plan.per * here.me + held_before]
+            if chunks == 1:
+                rows_f[pl.ds(row, ROWS), :] = value
+            else:
+                rows_f[pl.ds(row, ROWS, stride=chunks), :] = value
+            return carry
+
+        lax.fori_loop(lo, hi, unit, 0)
+    shift = lax.rem(here.me * plan.share, LANES)
+    turn = lax.rem(LANES - shift, LANES)
+    lane = lax.broadcasted_iota(jnp.int32, (64, LANES), 1)
+    spot = lax.broadcasted_iota(jnp.int32, (64, LANES), 0) * LANES + lane
+
+    def unalign(i, squares):
+        row = pl.multiple_of(i * 64, 64)
+        level = pltpu.roll(rows_f[pl.ds(row + plan.margin, 64), :], turn, 1)
+        below = pltpu.roll(rows_f[pl.ds(row + plan.margin + 1, 64), :], turn, 1)
+        value = jnp.where(lane < LANES - shift, level, below)
+        value = jnp.where(spot + row * LANES < plan.share, value, 0.0)
+        flat_f[pl.ds(row, 64), :] = value
+        return squares + jnp.sum((value * value).reshape(8, 8, LANES), axis=0)
+
+    return lax.fori_loop(0, plan.raw // 64, unalign, jnp.zeros((8, LANES), full_type))
+
+
+def put_row(stage, first, vector):
+    for r in range(vector.shape[1] // LANES):
+        stage[first + r : first + r + 1, :] = vector[:, r * LANES : (r + 1) * LANES]
+
+
+B_Q, B_V, B_O, B_1, B_2 = 0, D, 2 * D, 3 * D, 3 * D + FF
+
+
+def layer_backward_body(plan, rows, x_hbm, saved, units, grads, mod, grad, modulator_t, cond, held, sems, events):
+    (qkv, heads, h_low, wide_f, tall_f, pre, w_1, w_2, w_qkv, w_o, d_qkv, g_low, slim, turned, dx, d_one, d_two, grad_mod, bias_out, bias_f, bias_low) = held
+    load_sem, chunk_sem, out_sem = sems
+    h1_h, qkv_h, heads_h, attn_h, middle_h, h2_h, pre_h, mlp_h = saved
+    fetch = lambda i, src, dst: pltpu.make_async_copy(src, dst, load_sem.at[i])
+    load_mlp, load_attn = fetch(0, mlp_h, wide_f), fetch(0, attn_h, wide_f)
+    load_middle, load_x = fetch(1, middle_h, tall_f), fetch(1, x_hbm, tall_f)
+    load_h2, load_h1 = fetch(2, h2_h, h_low), fetch(2, h1_h, h_low)
+    load_heads, load_qkv = fetch(3, heads_h, heads), fetch(4, qkv_h, qkv)
+    load_w_o, load_w_qkv = fetch(5, segment_ref(units, plan, 1), w_o), fetch(6, segment_ref(units, plan, 0), w_qkv)
+    half = WIDE // ROWS
+    wide_at = lambda j, base=0: pl.ds(pl.multiple_of(base + j * WIDE, LANES), WIDE)
+
+    def chunk_loads(j):
+        at = j % 2
+        return (
+            pltpu.make_async_copy(segment_ref(units, plan, 3).at[pl.ds(j * half, half)], w_2.at[at], chunk_sem.at[at, 0]),
+            pltpu.make_async_copy(segment_ref(units, plan, 2).at[:, pl.ds(2 * j, 2)], w_1.at[at], chunk_sem.at[at, 1]),
+            pltpu.make_async_copy(pre_h.at[:, wide_at(j)], pre.at[at], chunk_sem.at[at, 2]),
+        )
+
+    def mod_load(j):
+        return pltpu.make_async_copy(segment_ref(units, plan, 4).at[:, pl.ds(2 * j, 2)], w_1.at[j % 2], chunk_sem.at[j % 2, 1])
+
+    for copy in (load_mlp, load_h2) + chunk_loads(0) + (load_middle, load_w_o, load_heads, load_qkv, load_w_qkv):
+        copy.start()
+    part = lambda s, i: mod[pl.ds(s, 1), i * D : (i + 1) * D]
+    per = SEQ // CHUNK
+    grad_mod[...] = jnp.zeros(grad_mod.shape, full_type)
+    bias_out[...] = jnp.zeros(bias_out.shape, full_type)
+
+    def add_mod(s, i, value):
+        grad_mod[pl.ds(s, 1), i * D : (i + 1) * D] += value
+
+    def each_chunk(body):
+        loop(rows // CHUNK, lambda i: body(pl.ds(pl.multiple_of(i * CHUNK, CHUNK), CHUNK), i // per))
+
+    load_mlp.wait()
+
+    def start_mlp(at, s):
+        value = grad[at, :]
+        low = (part(s, 5) * value).astype(low_type)
+        g_low[at, :] = low
+        bias_out[:, B_2 : B_2 + D] += rows_sum(low.astype(full_type))
+        add_mod(s, 5, rows_sum(wide_f[at, :] * value))
+
+    each_chunk(start_mlp)
+    load_attn.start()
+    load_h2.wait()
+    turned[...] = h_low[...].astype(full_type).T.astype(low_type)
+    load_h1.start()
+    dx[...] = jnp.zeros(dx.shape, full_type)
+
+    def outer(slot, segment, block, blocks, chunk, chunks, buffer):
+        target = segment_ref(grads, plan, segment).at[pl.ds(block, blocks), pl.ds(chunk, chunks)]
+        return pltpu.make_async_copy(buffer, target, out_sem.at[slot])
+
+    def mlp_store(j, kind):
+        at = j % 2
+        if kind == 0:
+            return outer(2 * at, 3, j * half, half, 0, D // LANES, d_one.at[at])
+        return outer(2 * at + 1, 2, 0, D // ROWS, 2 * j, 2, d_two.at[at])
+
+    steps = FF // WIDE
+
+    def feed_back(j):
+        at = j % 2
+
+        @pl.when(j + 1 < steps)
+        def _():
+            for copy in chunk_loads(j + 1):
+                copy.start()
+
+        for copy in chunk_loads(j):
+            copy.wait()
+
+        @pl.when(j >= 2)
+        def _():
+            mlp_store(j - 2, 0).wait()
+            mlp_store(j - 2, 1).wait()
+
+        act, slope = gelu_parts(pre[at])
+        grad_act = dot_nt(g_low[...], block_of(w_2.at[at], 0, half, 0, D // LANES))
+        low = (grad_act * slope).astype(low_type)
+        slim[...] = low
+        bias_out[:, wide_at(j, B_1)] += rows_sum(low.astype(full_type))
+        put_block(d_one.at[at], 0, 0, dot_tn(act.astype(low_type), g_low[...]))
+        mlp_store(j, 0).start()
+        put_block(d_two.at[at], 0, 0, dot(turned[...], slim[...]))
+        mlp_store(j, 1).start()
+        dx[...] += dot_nt(slim[...], block_of(w_1.at[at], 0, D // ROWS, 0, 2))
+
+    busy_loop(steps, feed_back, events[0])
+    load_middle.wait()
+    load_attn.wait()
+
+    def middle_back(at, s):
+        value = dx[at, :]
+        back, scaled = norm_back(tall_f[at, :], value, 1.0 + part(s, 4))
+        add_mod(s, 3, rows_sum(value))
+        add_mod(s, 4, rows_sum(scaled))
+        total = grad[at, :] + back
+        grad[at, :] = total
+        low = (part(s, 2) * total).astype(low_type)
+        g_low[at, :] = low
+        bias_out[:, B_O : B_O + D] += rows_sum(low.astype(full_type))
+        add_mod(s, 2, rows_sum(wide_f[at, :] * total))
+
+    each_chunk(middle_back)
+    load_x.start()
+    load_w_o.wait()
+    load_heads.wait()
+    for j in (steps - 2, steps - 1):
+        mlp_store(j, 0).wait()
+        mlp_store(j, 1).wait()
+    mod_load(0).start()
+    turned[...] = heads[...].astype(full_type).T.astype(low_type)
+
+    def wo_store(j):
+        return outer(j % 2, 1, 0, D // ROWS, 2 * j, 2, d_two.at[j % 2])
+
+    def out_back(j):
+        @pl.when(j >= 2)
+        def _():
+            wo_store(j - 2).wait()
+
+        put_block(d_two.at[j % 2], 0, 0, dot(turned[...], g_low[:, wide_at(j)]))
+        wo_store(j).start()
+        heads[:, wide_at(j)] = dot_nt(g_low[...], block_of(w_o, j * half, half, 0, D // LANES)).astype(low_type)
+
+    busy_loop(D // WIDE, out_back, events[1])
+    load_qkv.wait()
+    first = head_masks()
+
+    def attend_back(i):
+        s, j = i // (HEADS // 2), i % (HEADS // 2)
+        at = pl.ds(pl.multiple_of(s * SEQ, SEQ), SEQ)
+        cut = lambda o: qkv[at, pl.ds(pl.multiple_of(o * D + j * LANES, LANES), LANES)]
+        q, k, v = cut(0), cut(1), cut(2)
+        go = heads[at, pl.ds(pl.multiple_of(j * LANES, LANES), LANES)]
+        q = q * jnp.asarray(HD ** (-0.5), low_type)
+        zero = jnp.zeros_like(q)
+        dq, dk, dv = [], 0.0, 0.0
+        for mask in (first, ~first):
+            q_h, go_h = jnp.where(mask, q, zero), jnp.where(mask, go, zero)
+            probs = softmax_f32(dot_nt(q_h, k))
+            grad_probs = dot_nt(go_h, v)
+            dv = dv + dot_tn(probs.astype(low_type), go_h)
+            inner = jnp.sum(probs * grad_probs, axis=-1, keepdims=True)
+            ds = (probs * (grad_probs - inner)).astype(low_type)
+            dq.append(dot(ds, k) * HD ** (-0.5))
+            dk = dk + dot_tn(ds, q_h)
+        for o, value in enumerate((jnp.where(first, dq[0], dq[1]), dk, dv)):
+            low = value.astype(low_type)
+            d_qkv[at, pl.ds(pl.multiple_of(o * D + j * LANES, LANES), LANES)] = low
+            if o != 1:
+                start = (B_Q if o == 0 else B_V) + j * LANES
+                bias_out[:, pl.ds(pl.multiple_of(start, LANES), LANES)] += rows_sum(low.astype(full_type))
+
+    busy_loop(attention_pairs(rows), attend_back, events[2])
+    load_h1.wait()
+    load_w_qkv.wait()
+    wo_store(1).wait()
+    wo_store(2).wait()
+    turned[...] = h_low[...].astype(full_type).T.astype(low_type)
+    dx[...] = jnp.zeros(dx.shape, full_type)
+
+    def qkv_store(j):
+        return outer(j % 2, 0, 0, D // ROWS, 2 * j, 2, d_two.at[j % 2])
+
+    def project_back(j):
+        @pl.when(j >= 2)
+        def _():
+            qkv_store(j - 2).wait()
+
+        put_block(d_two.at[j % 2], 0, 0, dot(turned[...], d_qkv[:, wide_at(j)]))
+        qkv_store(j).start()
+        dx[...] += dot_nt(d_qkv[:, wide_at(j)], block_of(w_qkv, 0, D // ROWS, 2 * j, 2))
+
+    count = 3 * D // WIDE
+    busy_loop(count, project_back, events[3])
+    load_x.wait()
+
+    def input_back(at, s):
+        value = dx[at, :]
+        back, scaled = norm_back(tall_f[at, :], value, 1.0 + part(s, 1))
+        add_mod(s, 0, rows_sum(value))
+        add_mod(s, 1, rows_sum(scaled))
+        grad[at, :] += back
+
+    each_chunk(input_back)
+    for j in (count - 2, count - 1):
+        qkv_store(j).wait()
+    mod_steps = 6 * D // WIDE
+
+    def mod_store(j):
+        return outer(j % 2, 4, 0, D // ROWS, 2 * j, 2, d_two.at[j % 2])
+
+    def mod_back(j):
+        @pl.when(j + 1 < mod_steps)
+        def _():
+            mod_load(j + 1).start()
+
+        mod_load(j).wait()
+
+        @pl.when(j >= 2)
+        def _():
+            mod_store(j - 2).wait()
+
+        low = grad_mod[:, wide_at(j)].astype(low_type)
+        put_block(d_two.at[j % 2], 0, 0, dot(modulator_t[...], low))
+        mod_store(j).start()
+        cond[...] += dot_nt(low, block_of(w_1.at[j % 2], 0, D // ROWS, 0, 2))
+
+    busy_loop(mod_steps, mod_back, events[4])
+    bias_f[...] = jnp.zeros(bias_f.shape, full_type)
+    bias_first = plan.segments[5][3]
+    low_sum = rows_sum(grad_mod[...].astype(low_type).astype(full_type))
+    for number, value in zip(range(5, 11), (bias_out[:, B_Q : B_Q + D], bias_out[:, B_V : B_V + D], bias_out[:, B_O : B_O + D], bias_out[:, B_1 : B_1 + FF], bias_out[:, B_2 : B_2 + D], low_sum)):
+        put_row(bias_f, (plan.segments[number][3] - bias_first) * ROWS, value)
+    bias_low[...] = bias_f[...].astype(low_type).reshape(bias_low.shape)
+    store = pltpu.make_async_copy(bias_low, grads.at[pl.ds(bias_first, bias_low.shape[0])], out_sem.at[2])
+    store.start()
+    store.wait()
+    for j in (mod_steps - 2, mod_steps - 1):
+        mod_store(j).wait()
+
+
+def backward_kernel(plans, zs, rows, *refs):
+    np_ = len(plans)
+    feed = iter(refs)
+    take = lambda count: tuple(next(feed) for _ in range(count))
+    one = lambda: next(feed)
+    one()
+    units = take(np_)
+    stream = take(LAYERS)
+    saved = [take(len(SAVED)) for _ in range(LAYERS)]
+    grad_in, = take(1)
+    mods = take(LAYERS)
+    modulator, condition, time_pre, cond_in, noisy, basis, chosen, stats_in = take(8)
+    root_grads = one()
+    layer_grads = take(LAYERS)
+    flats = take(np_)
+    stats_out = one()
+    first = take(np_ + 1)
+    own_units = take(np_)
+    halo_before, halo_after = take(np_), take(np_)
+    buffers = ((one(), one()), (one(), one()), (one(), one()), one(), one(), one(), one())
+    total, total_in = take(2)
+    sems = take(9)
+    frees = take(3)
+    load_sem, chunk_sem, out_sem, own_sem, halo_s, halo_r, ss, sr = take(8)
+    here = Place(zs)
+    here.greet()
+    root = plans[0]
+    front_units = root.segments[FRONT][3]
+    front_planes = min(zs, -(-front_units // (8 * root.per)))
+    layers = list(reversed(range(LAYERS)))
+    buckets = [(root, root_grads, front_planes, zs)]
+    buckets += [(plans[1 + i], layer_grads[i], 0, zs) for i in layers]
+    buckets += [(root, root_grads, 0, front_planes)]
+    outs = [own_units[0]] + [own_units[1 + i] for i in layers] + [own_units[0]]
+    work = Reduce(here, buckets, first, buffers, sems, frees)
+    here.met()
+    work.open(0)
+    steps = [work.steps(g, outs, own_sem) for g in range(len(work.groups) + 4)]
+    of_bucket = lambda b: [step for group in steps[b * zs : (b + 1) * zs] for step in group]
+
+    def compute(grad, cond, modulator_t, *held):
+        grad[...] = grad_in[...]
+        cond[...] = cond_in[...]
+        modulator_t[...] = modulator[...].astype(full_type).T.astype(low_type)
+        for position, ordinal in enumerate(layers):
+            layer_backward_body(
+                plans[1 + ordinal], rows, stream[ordinal], saved[ordinal], units[1 + ordinal], layer_grads[ordinal],
+                mods[ordinal], grad, modulator_t, cond, held, (load_sem, chunk_sem, out_sem), spread(of_bucket(position), (14, 3, 14, 8, 10)),
+            )
+            work.open(1 + position)
+        embed_back(grad, cond)
+
+    def embed_back(grad, cond):
+        def run(front_w, front_f, front_low):
+            load = pltpu.make_async_copy(units[0].at[pl.ds(root.segments[4][3], root.segments[4][2])], front_w, load_sem.at[0])
+            load.start()
+            events = spread(of_bucket(LAYERS), (1, 1, 1, 1))
+            first_of = lambda number: root.segments[number][3]
+
+            def put(number, value):
+                chunks = value.shape[1] // LANES
+                blocks = value.shape[0] // ROWS
+                for b in range(blocks):
+                    for c in range(chunks):
+                        front_low[first_of(number) + b * chunks + c] = value[b * ROWS : (b + 1) * ROWS, c * LANES : (c + 1) * LANES].astype(low_type)
+
+            def put_bias(number, value):
+                front_f[...] = jnp.zeros(front_f.shape, full_type)
+                put_row(front_f, 0, value)
+                front_low[first_of(number)] = front_f[...].astype(low_type)
+
+            for event in events[0]:
+                event()
+            low = grad[...].astype(low_type)
+            put(0, dot_tn(noisy[...], low))
+            put_bias(1, rows_sum(low.astype(full_type)))
+            for event in events[1]:
+                event()
+            gate = silu_parts(condition[...])[1] * cond[...]
+            g_low = gate.astype(low_type)
+            pre = time_pre[...]
+            act, slope = silu_parts(pre)
+            put(4, dot_tn(act.astype(low_type), g_low))
+            put_bias(5, rows_sum(g_low.astype(full_type)))
+            few = g_low.shape[0]
+            stacked = jnp.concatenate([gate[:, c * LANES : (c + 1) * LANES] for c in range(D // LANES)], axis=0)
+            for event in events[2]:
+                event()
+            span = 16 * ROWS
+            table_first, table_count = first_of(6), root.segments[6][2]
+            for start in range(0, table_count * ROWS, span):
+                size = min(span, table_count * ROWS - start)
+                value = dot_tn(chosen[:, start : start + size], stacked.astype(low_type))
+                front_low[table_first + start // ROWS : table_first + (start + size) // ROWS] = value.astype(low_type).reshape(size // ROWS, ROWS, LANES)
+            load.wait()
+            w_t2 = jnp.concatenate(
+                [jnp.concatenate([front_w[b * (D // LANES) + c] for b in range(D // ROWS)], axis=0) for c in range(D // LANES)], axis=1
+            )
+            grad_pre = (dot_nt(g_low, w_t2) * slope).astype(low_type)
+            put(2, dot_tn(basis[...], grad_pre))
+            put_bias(3, rows_sum(grad_pre.astype(full_type)))
+            store = pltpu.make_async_copy(front_low, root_grads.at[pl.ds(0, front_units)], load_sem.at[1])
+            store.start()
+            for event in events[3]:
+                event()
+            store.wait()
+
+        pl.run_scoped(
+            run,
+            pltpu.VMEM((root.segments[4][2], ROWS, LANES), low_type),
+            pltpu.VMEM((ROWS, LANES), full_type),
+            pltpu.VMEM((front_units, ROWS, LANES), low_type),
+        )
+
+    plan = plans[1]
+    bias_units = plan.units - plan.segments[5][3]
+    f32 = lambda *dims: pltpu.VMEM(dims, full_type)
+    bf16 = lambda *dims: pltpu.VMEM(dims, low_type)
+    tile = (ROWS, LANES)
+    few = modulator.shape[0]
+    pl.run_scoped(
+        compute,
+        f32(rows, D), f32(few, D), bf16(D, few),
+        bf16(rows, 3 * D), bf16(rows, D), bf16(rows, D), f32(rows, D), f32(rows, D), f32(2, rows, WIDE),
+        bf16(2, D // ROWS, 2, *tile), bf16(2, WIDE // ROWS, D // LANES, *tile),
+        segment_scratch(plan, 0), segment_scratch(plan, 1),
+        bf16(rows, 3 * D), bf16(rows, D), bf16(rows, WIDE), bf16(D, rows), f32(rows, D),
+        bf16(2, WIDE // ROWS, D // LANES, *tile), bf16(2, D // ROWS, 2, *tile),
+        f32(few, 6 * D), f32(1, 4 * D + FF), f32(bias_units * ROWS, LANES), bf16(bias_units, *tile),
+    )
+    final = len(buckets) - 1
+    work.open(final)
+
+    def unpack(units_f, rows_f, flat_f):
+        def halo(i):
+            p = plans[i]
+            forward = remote(own_units[i].at[pl.ds(p.per - p.units_before, p.units_before)], halo_before[i], halo_s.at[i, 0], halo_r.at[i, 0], here.following)
+            backward = remote(own_units[i].at[pl.ds(0, p.units_after)], halo_after[i], halo_s.at[i, 1], halo_r.at[i, 1], here.prev)
+            return forward, backward
+
+        def finish(i):
+            p = plans[i]
+            base = p.units_before
+            for copy in halo(i):
+                copy.wait()
+            parts = (
+                pltpu.make_async_copy(halo_before[i], units_f.at[pl.ds(0, base)], load_sem.at[0]),
+                pltpu.make_async_copy(own_units[i], units_f.at[pl.ds(base, p.per)], load_sem.at[1]),
+                pltpu.make_async_copy(halo_after[i], units_f.at[pl.ds(base + p.per, p.units_after)], load_sem.at[2]),
+            )
+            for copy in parts:
+                copy.start()
+            for copy in parts:
+                copy.wait()
+            squares = unpack_rows(here, p, units_f, rows_f, flat_f, base)
+            store = pltpu.make_async_copy(flat_f.at[pl.ds(0, p.raw)], flats[i], load_sem.at[3])
+            store.start()
+            store.wait()
+            total[1] += squares
+
+        total[0] = stats_in[...]
+        total[1] = jnp.zeros((8, LANES), full_type)
+        begun, done = {}, set()
+        for g in range((LAYERS + 1) * zs, len(steps) + 1):
+            for position, ordinal in enumerate(layers):
+                i = 1 + ordinal
+                if i not in begun and g > zs * (position + 2) + 2:
+                    begun[i] = g
+                    for copy in halo(i):
+                        copy.start()
+                elif i in begun and i not in done and g > begun[i]:
+                    done.add(i)
+                    finish(i)
+            for step in steps[g] if g < len(steps) else ():
+                step()
+        for copy in halo(0):
+            copy.start()
+        finish(0)
+
+    most = max(p.units_before + p.per + p.units_after for p in plans)
+    pl.run_scoped(
+        unpack,
+        f32(most, *tile), f32(max(p.spread for p in plans), LANES), f32(max(p.raw for p in plans), LANES),
+    )
+    step = 0
+    for to in ((here.cpeer,), (here.xpeer,), (here.ypeer,), tuple(here.above(k) for k in range(1, zs))):
+        copies = []
+        for peer in to:
+            copies.append(remote(total, total_in.at[step], ss.at[step], sr.at[step], peer))
+            copies[-1].start()
+            step += 1
+        for copy in copies:
+            copy.wait()
+        value = total[...]
+        for i in range(len(to)):
+            value = value + total_in[step - 1 - i]
+        total[...] = value
+    stats_out[...] = total[...]
+    work.close()
+
+
+def backward_call(plans, units, stream, saved, grad, mods, small, stats, root_grads):
+    n = plans[0].devices
+    zs = n // 8
+    rows = grad.shape[0]
+    np_, nb = len(plans), len(plans) + 1
+    vm = pl.BlockSpec(memory_space=pltpu.VMEM)
+    hbm = pl.BlockSpec(memory_space=pltpu.HBM)
+    shape = jax.ShapeDtypeStruct
+    dma, regular = pltpu.SemaphoreType.DMA, pltpu.SemaphoreType.REGULAR
+    tile = (ROWS, LANES)
+    layers = list(reversed(range(LAYERS)))
+    order = [plans[0]] + [plans[1 + i] for i in layers] + [plans[0]]
+    all_units = lambda p: shape((n * p.per,) + tile, low_type)
+    out_shape = [all_units(p) for p in plans]
+    out_shape += [shape((p.raw, LANES), full_type) for p in plans]
+    out_shape += [shape((2, 8, LANES), full_type)]
+    out_shape += [shape((zs, 2, 2, p.per) + tile, low_type) for p in order]
+    out_shape += [shape((p.per,) + tile, full_type) for p in plans]
+    out_shape += [shape((p.units_before,) + tile, full_type) for p in plans]
+    out_shape += [shape((p.units_after,) + tile, full_type) for p in plans]
+    most = max(p.per for p in plans)
+    half = lambda *lead: pltpu.VMEM(lead + (most // 2,) + tile, low_type)
+    hops = 2 + zs
+    scratch = [half(zs, 2)] * 4 + [half(zs)] * 2 + [half(2, zs - 1)]
+    scratch += [pltpu.VMEM((7, most) + tile, low_type), pltpu.VMEM((2, most) + tile, low_type)]
+    scratch += [pltpu.VMEM((most,) + tile, full_type)]
+    scratch += [pltpu.VMEM((2, 8, LANES), full_type), pltpu.VMEM((hops, 2, 8, LANES), full_type)]
+    scratch += [dma((nb, zs, 2, 2))] * 2 + [dma((2, zs, 2))] * 2 + [dma((2, zs))] * 2 + [dma((2, zs - 1))] * 2 + [dma((7, 2))]
+    scratch += [regular((2, zs)), regular((2, zs)), regular((zs - 1,))]
+    scratch += [dma((7,)), dma((2, 3)), dma((4,)), dma, dma((np_, 2)), dma((np_, 2)), dma((hops,)), dma((hops,))]
+    flat_saved = [array for group in saved for array in group]
+    results = pl.pallas_call(
+        functools.partial(backward_kernel, plans, zs, rows),
+        out_shape=out_shape,
+        in_specs=[hbm] * (1 + np_ + LAYERS + len(flat_saved)) + [vm] * (1 + LAYERS + len(small) + 1),
+        out_specs=[hbm] * (2 * np_) + [vm] + [hbm] * (nb + 3 * np_),
+        input_output_aliases={0: 0},
+        scratch_shapes=scratch,
+        compiler_params=pltpu.CompilerParams(collective_id=1, has_side_effects=True, vmem_limit_bytes=62 * MB),
+        name="backward_and_reduce",
+    )(root_grads, *units, *stream, *flat_saved, grad, *mods, *small, stats)
+    return results[np_ : 2 * np_], results[2 * np_]
+
+
 def model_step(layer_lists, pieces, latents, noise, times, labels, dropped, features, devices):
     sample_total = latents.shape[0] * devices
     residual, modulator, embed_saved = embed_forward(
@@ -2250,33 +3061,17 @@
         root_plan, sample_total, residual, features.reshape(rows, ZD), target, weight_t, modulator_rows, biases, w_h, b_h, root_units
     )
     loss_part = -proj_coeff / SEQ * losses[0, 0] + jnp.sum(losses[1]) / (SEQ * PD)
-    grad_cond = grad_cond[:samples]
-    layer_grads = [None] * LAYERS
-    for ordinal in reversed(range(LAYERS)):
-        units = layer_units[ordinal]
-        grad, grad_mod, bias_grad, grads = layer_backward_call(
-            plan, stream[ordinal], grad, mods[ordinal], kept[ordinal], units
-        )
-        low_mod = jnp.pad(grad_mod.astype(low_type), ((0, few - grad_mod.shape[0]), (0, 0)))
-        grads, cond_part = mods_back_call(plan, modulator_rows, low_mod, units, grads)
-        grad_cond = grad_cond + cond_part[:samples]
-        cuts = jnp.split(bias_grad[0], (D, 2 * D, 3 * D, 3 * D + FF))
-        grad_b_mod = jnp.sum(low_mod.astype(full_type), axis=0)
-        layer_grads[ordinal] = put_units(grads, plan, 5, cuts + [grad_b_mod])
-    pieces = {4: matrix_of(root_units, root_plan, 4), 2: None, 0: None}
-    onehot = (classes[:, None] == jnp.arange(CLS, dtype=jnp.int32)[None, :]).astype(low_type)
-    time_pre = time_pre[:samples]
-    embed_saved = (noisy_bf, basis_bf, time_pre, jax.nn.silu(time_pre).astype(low_type), onehot, condition[:samples])
-    embed_grads = embed_backward(pieces, embed_saved, grad.reshape(samples, SEQ, D), grad_cond)
     cuts = jnp.split(bias_grads[0], (PH, 2 * PH, 2 * PH + ZD, 2 * PH + ZD + 2 * D))
     for number, value in zip((8, 10, 12), cuts):
         root_grads = put_units(root_grads, root_plan, number, [value])
     root_grads = put_units(root_grads, root_plan, 14, [cuts[3], grad_w_h[:, :PD], cuts[4][:PD]])
-    root_grads = put_units(root_grads, root_plan, 0, embed_grads)
     square_sums = jnp.stack([jnp.sum(total[:3], axis=1) for total in sums])
     numbers = jnp.concatenate([loss_part[None], square_sums.reshape(-1)])
     stats = jnp.pad(numbers, (0, 8 * LANES - numbers.shape[0])).reshape(8, LANES)
-    rows_out, stats = reduce_units(plans, [root_grads] + layer_grads, stats)
+    small = (modulator_rows, condition, time_pre, grad_cond, noisy_bf.reshape(rows, PD), extra(basis_bf), chosen)
+    rows_out, stats = backward_call(
+        plans, units, stream[:-1], kept, grad, mods, small, stats, root_grads
+    )
     numbers = stats[0].reshape(-1)
     shard_root = rows_out[0].reshape(-1)[: root_plan.share]
     shard_layers = jnp.stack([r.reshape(-1)[: plan.share] for r in rows_out[1:]])

time: 937 us -> 851 us (0.908)
  Pallas kernels: 830 us -> 760 us
  local copies, waits for them, and re-layouts: 57.6 us -> 46.3 us
    pallas_call x5 -> x1, Pallas kernels: 448 us -> 378 us  [backward_call(): pl.pallas_call(functools.partial(backward_kernel, plans, zs, rows), out_s...]
where the time goes in v3:
time: 851 us; the launch traced here: 841 us
  Pallas kernels  760 us (89%)
  local copies, waits for them, and re-layouts  46.3 us (5%)
  other arithmetic  30 us (4%)
    pallas_call x1, Pallas kernels, backward_call(): pl.pallas_call(functools.partial(backward_kernel, plans, zs, rows), out_s...  378 us
    pallas_call x1, Pallas kernels, forward_call(): pl.pallas_call(functools.partial(forward_kernel, plans, zs, rows), out_sh...  333 us
    pallas_call x1, Pallas kernels, top_call(): pl.pallas_call(functools.partial(top_kernel, plan, rows, sample_total), o...  49 us

profile of v3, /device:TPU:6, one launch (start us, length us, event | category | flops | bytes accessed | tf_op | source)
XLA Modules:
  0.0 840.8 jit_solution(15137646040823106856)
XLA Ops:
  1.3 0.8 fusion.9
  4.3 0.9 fusion.13
  5.2 0.8 copy.24
  6.1 0.7 pad.59.target
  6.9 1.2 tile.20
  8.2 1.3 fusion.1.refs_6_.refs_31_
  9.4 1.1 pad_bitcast_fusion.2.refs_0_
  10.6 13.9 %slice_reduce_fusion = (f32[332112]{0:T(1024)S(1)}, f32[332112]{0:T(1024)S(1)}) fusion(f32[2,332112]{1,0:T(2,128)S(1)} %copy-done), kind=kLoop, calls=%fused_computation.11 | loop fusion | bytes 5313792 | tf_op jit(solution)/shard_map/slice | solution.py:3038
  24.4 1.9 pad_bitcast_fusion
  26.3 333.3 %gather_and_forward.1 = (bf16[4992,16,128]{2,1,0:T(8,128)(2,1)}, bf16[5248,16,128]{2,1,0:T(8,128)(2,1)}, bf16[5248,16,128]{2,1,0:T(8,128)(2,1)}, f32[512,768]{1,...) custom-call(f32[2496,128]{1,0:T(8,128)} %pad_bitcast_fusion.2.refs_0, ...), custom_call_target="tpu_custom_call" | custom-call | tf_op jit(solution)/shard_map/gather_and_forward/pallas_call | solution.py:2121
  359.6 0.9 slice_reduce_fusion.3
  360.5 0.9 slice_reduce_fusion.2
  361.5 0.7 convert_bitcast_fusion.1
  362.7 0.7 convert_bitcast_fusion
  364.0 1.3 slice_bitcast_fusion.1
  365.8 0.7 slice.92
  366.8 0.7 pad.61.w_h
  367.5 49.0 %projector_and_head.1 = (f32[512,768]{1,0:T(8,128)}, f32[8,128]{1,0:T(8,128)}, f32[16,768]{1,0:T(8,128)}, f32[1,6528]{1,0:T(1,128)}, f32[768,128]{1,0:T(8,128)}, /*index=5*/bf16[4992,16,128]{2,1,0:T(8,128)(2,1)}) custom-call(f32[512,768]{1,0:T(8,128)} %get-tuple-element.48.x, bf16[512,768]{1,0:T(8,128)(2,1)} %bitcast.64, f32[512,128]{1,0:T(8,128)} %pad.59.target, ...), custom_call_target="tpu_custom_call" | custom-call | tf_op jit(solution)/shard_map/projector_and_head/pallas_call | solution.py:1590
  416.5 1.3 slice_reduce_fusion.9
  418.4 1.2 slice.97
  420.9 0.8 convert.25
  423.6 1.0 slice.134
  425.4 377.7 %backward_and_reduce.1 = (bf16[4992,16,128]{2,1,0:T(8,128)(2,1)}, bf16[5248,16,128]{2,1,0:T(8,128)(2,1)}, bf16[5248,16,128]{2,1,0:T(8,128)(2,1)}, f32[2496,128]{...) custom-call(bf16[4992,16,128]{2,1,0:T(8,128)(2,1)} %maximum_dynamic-, ...), custom_call_target="tpu_custom_call", output_to_operand_aliasing={{0}: (0, {})} | custom-call | tf_op jit(solution)/shard_map/backward_and_reduce/pallas_call | solution.py:2935
  803.2 1.3 slice_reduce_fusion.7
  805.8 1.4 slice.111
  807.2 6.2 stack.21
  814.0 1.5 slice.112
  815.6 6.2 stack.22
  821.9 2.6 multiply_subtract_fusion.1
  824.5 1.3 copy-done.3
  825.8 0.8 copy-done.4
  826.6 12.7 %multiply_subtract_fusion = (f32[2,332112]{1,0:T(2,128)}, f32[2,332112]{1,0:T(2,128)}, f32[2,332112]{1,0:T(2,128)}) fusion(f32[2,332112]{1,0:T(2,128)S(1)} %copy-done.1, f32[]{:T(128)S(6)} %div.49, f32[1,332112]{1,0:T(1,128)S(1)} %stack.22, f32[1,332112]{1,0:T(1,128)S(1)} %stack.21, f32[2,332112]{1,0:T(2,128)S(1)} %copy-done.3, f32[2,332112]{1,0:T(2,128)S(1)} %copy-done.4), kind=kLoop, calls=%fused_computation.4 | loop fusion | flops 10627584 | bytes 18598276 | tf_op jit(solution)/shard_map/sub | solution.py:2991
  (53 shorter events, 9.7 us)
Async XLA Ops:
  6.9 2.5 copy-start.2
  8.2 2.4 copy-start
  814.0 7.8 copy-start.7
  815.6 6.3 copy-start.5
  815.6 6.3 copy-start.6
  821.8 2.6 copy-start.1
  821.8 3.9 copy-start.3
  821.9 4.7 copy-start.4

commit v4 on v3

--- a/solution.py
+++ b/solution.py
@@ -44,7 +44,7 @@
     return -(-value // step) * step
 
 class Plan:
-    def __init__(self, layout, length, devices):
+    def __init__(self, layout, length, devices, reduced):
         self.length = length
         self.devices = devices
         self.share = length // devices
@@ -59,6 +59,8 @@
             offset += amount
             units += count
         self.units = units
+        self.reduced = self.segments[reduced[0] : reduced[1]]
+        self.moved = lambda u: self.reduced[0][3] <= u < self.reduced[-1][3] + self.reduced[-1][2]
         self.per = up(up(units, devices) // devices, 4)
         rows_of = []
         for base, chunks, count, _, _, _ in self.segments:
@@ -74,6 +76,8 @@
         self.before, self.after = up(before, 8), up(after, 8)
         units_before = units_after = 0
         for u, (lo, hi) in enumerate(rows_of):
+            if not self.moved(u):
+                continue
             first = lo * LANES // self.share
             last = min(((hi + 1) * LANES - 1) // self.share, devices - 1)
             for d in range(first, last + 1):
@@ -2134,6 +2138,9 @@
     return units, stream, mods, sums, modulator, condition, time_pre, [take(len(SAVED)) for _ in range(LAYERS)]
 
 
+LOOK = 1
+
+
 class Reduce:
     def __init__(self, here, buckets, first, buffers, sems, frees):
         self.here = here
@@ -2214,7 +2221,7 @@
         return view.at[pl.ds(0, self.half(b))]
 
     def place_of(self, g, i):
-        return 6 if i == 3 else 3 * (g % 2) + i
+        return 3 * (LOOK + 1) if i == 3 else 3 * (g % (LOOK + 1)) + i
 
     def loads(self, g, i):
         b, k = self.groups[g]
@@ -2310,13 +2317,15 @@
     def last(self, g, h):
         b, k = self.groups[g]
         here = self.here
-        return remote(self.buffer(self.three[h], b, k), self.buffer(self.four, b, h, k - 1), pick(self.s4, here, h, k - 1), pick(self.r4, here, h, k - 1), here.below(k))
+        return remote(self.buffer(self.three[h], b, k), self.buffer(self.four, b, b % 2, h, k - 1), pick(self.s4, here, b % 2, h, k - 1), pick(self.r4, here, b % 2, h, k - 1), here.below(k))
 
     def phase_three(self, g):
         b, k = self.groups[g]
         here, size = self.here, self.half(b)
         if k:
-            self.before(b, k, lambda: pl.semaphore_wait(pick(self.free_four, here, k - 1), 1))
+            if b >= 2:
+                to_free = lambda: pl.semaphore_wait(pick(self.free_four, here, k - 1), 1)
+                self.guarded(b, k, lambda: self.guarded(b - 2, k, to_free))
 
         def run():
             for h in range(2):
@@ -2353,16 +2362,31 @@
         def run():
             for h in range(2):
                 self.third(g, h).wait_send()
-                if k:
-                    self.last(g, h).wait_send()
 
         self.guarded(b, k, run)
 
         def free():
             for h in range(2):
-                two_from, three_from = (here.ypeer, here.xpeer) if h == 0 else (here.xpeer, here.ypeer)
-                pl.semaphore_signal(pick(self.free_two, here, h, k), inc=1, device_id=(two_from,), device_id_type=MESH)
-                pl.semaphore_signal(pick(self.free_three, here, h, k), inc=1, device_id=(three_from,), device_id_type=MESH)
+                to = here.ypeer if h == 0 else here.xpeer
+                pl.semaphore_signal(pick(self.free_two, here, h, k), inc=1, device_id=(to,), device_id_type=MESH)
+
+        self.after(b, k, free)
+
+    def release_three(self, g):
+        b, k = self.groups[g]
+        here = self.here
+
+        def run():
+            for h in range(2):
+                self.last(g, h).wait_send()
+
+        if k:
+            self.guarded(b, k, run)
+
+        def free():
+            for h in range(2):
+                to = here.xpeer if h == 0 else here.ypeer
+                pl.semaphore_signal(pick(self.free_three, here, h, k), inc=1, device_id=(to,), device_id_type=MESH)
 
         self.after(b, k, free)
 
@@ -2372,7 +2396,7 @@
         def run():
             for h in range(2):
                 for k in range(1, here.zs):
-                    arrived(self.buffer(self.four, b, h, k - 1), pick(self.r4, here, h, k - 1))
+                    arrived(self.buffer(self.four, b, b % 2, h, k - 1), pick(self.r4, here, b % 2, h, k - 1))
                 step = size // 2
 
                 def body(i, carry):
@@ -2380,7 +2404,7 @@
                     where = pl.ds(h * size + i * step, step)
                     value = self.own[where]
                     for k in range(1, here.zs):
-                        value = value + self.buffer(self.four, b, h, k - 1)[part].astype(full_type)
+                        value = value + self.buffer(self.four, b, b % 2, h, k - 1)[part].astype(full_type)
                     self.own[where] = value
                     return carry
 
@@ -2395,31 +2419,37 @@
             for k in range(1, here.zs):
                 pl.semaphore_signal(pick(self.free_four, here, k - 1), inc=1, device_id=(here.above(k),), device_id_type=MESH)
 
-        self.after(b, 0, free)
+        if b + 2 < len(self.buckets):
+            self.guarded(b, 0, lambda: self.guarded(b + 2, 0, free))
 
     def steps(self, g, outs, sem):
         zs = self.here.zs
         total = len(self.groups)
         found = []
-        if (g - 2) % zs == 0 and 0 < (g - 2) // zs <= len(self.buckets):
-            b = (g - 2) // zs - 1
+        done = g - LOOK - 1
+        if done % zs == 0 and 0 < done // zs <= len(self.buckets):
+            b = done // zs - 1
             found.append(functools.partial(self.collect, b, outs[b], sem))
         if g < total:
-            if g >= 2:
-                found.append(lambda: self.release_one(g - 2))
+            if g >= LOOK + 1:
+                found.append(functools.partial(self.release_one, g - LOOK - 1))
             found += [functools.partial(self.phase_one, g, i) for i in range(4)]
-        if 0 <= g - 1 < total:
-            found += [functools.partial(self.phase_two, g - 1, 1), functools.partial(self.phase_two, g - 1, 0)]
-        if 0 <= g - 2 < total:
-            found.append(functools.partial(self.phase_three, g - 2))
-        if 0 <= g - 3 < total:
-            found.append(lambda: self.release_two(g - 3))
+        if 0 <= g - LOOK - zs < total - zs:
+            found.append(functools.partial(self.release_three, g - LOOK - zs))
+        if 0 <= g - LOOK < total:
+            found += [functools.partial(self.phase_two, g - LOOK, 1), functools.partial(self.phase_two, g - LOOK, 0)]
+        if 0 <= g - LOOK - 1 < total:
+            found.append(functools.partial(self.phase_three, g - LOOK - 1))
+        if 0 <= g - LOOK - 2 < total:
+            found.append(functools.partial(self.release_two, g - LOOK - 2))
         return found
 
     def close(self):
         total = len(self.groups)
-        for g in (total - 2, total - 1):
+        for g in range(total - LOOK - 1, total):
             self.release_one(g)
+        for g in range(total - self.here.zs, total):
+            self.release_three(g)
         for b in range(len(self.buckets)):
             for k in self.planes:
 
@@ -2430,9 +2460,9 @@
                 self.guarded(b, k, run)
 
 
-def unpack_rows(here, plan, units_f, rows_f, flat_f, held_before):
+def unpack_rows(here, plan, segments, units_f, rows_f, flat_f, held_before):
     top = here.me * plan.share // LANES - plan.margin
-    for origin, chunks, count, first_unit, _, _ in plan.segments:
+    for origin, chunks, count, first_unit, _, _ in segments:
         lo = jnp.clip(plan.per * here.me - held_before - first_unit, 0, count)
         hi = jnp.clip(plan.per * here.me + plan.per + plan.units_after - first_unit, 0, count)
 
@@ -2472,8 +2502,8 @@
 B_Q, B_V, B_O, B_1, B_2 = 0, D, 2 * D, 3 * D, 3 * D + FF
 
 
-def layer_backward_body(plan, rows, x_hbm, saved, units, grads, mod, grad, modulator_t, cond, held, sems, events):
-    (qkv, heads, h_low, wide_f, tall_f, pre, w_1, w_2, w_qkv, w_o, d_qkv, g_low, slim, turned, dx, d_one, d_two, grad_mod, bias_out, bias_f, bias_low) = held
+def layer_backward_body(plan, rows, x_hbm, saved, units, grads, mod, grad, modulator, cond, note, samples, held, sems, events):
+    (qkv, heads, h_low, wide_f, tall_f, pre, w_1, w_2, w_qkv, w_o, d_qkv, g_low, slim, turned, dx, d_one, d_two, grad_mod, bias_out) = held
     load_sem, chunk_sem, out_sem = sems
     h1_h, qkv_h, heads_h, attn_h, middle_h, h2_h, pre_h, mlp_h = saved
     fetch = lambda i, src, dst: pltpu.make_async_copy(src, dst, load_sem.at[i])
@@ -2667,37 +2697,186 @@
         qkv_store(j).wait()
     mod_steps = 6 * D // WIDE
 
-    def mod_store(j):
-        return outer(j % 2, 4, 0, D // ROWS, 2 * j, 2, d_two.at[j % 2])
-
     def mod_back(j):
         @pl.when(j + 1 < mod_steps)
         def _():
             mod_load(j + 1).start()
 
         mod_load(j).wait()
-
-        @pl.when(j >= 2)
-        def _():
-            mod_store(j - 2).wait()
-
         low = grad_mod[:, wide_at(j)].astype(low_type)
-        put_block(d_two.at[j % 2], 0, 0, dot(modulator_t[...], low))
-        mod_store(j).start()
         cond[...] += dot_nt(low, block_of(w_1.at[j % 2], 0, D // ROWS, 0, 2))
 
     busy_loop(mod_steps, mod_back, events[4])
-    bias_f[...] = jnp.zeros(bias_f.shape, full_type)
-    bias_first = plan.segments[5][3]
-    low_sum = rows_sum(grad_mod[...].astype(low_type).astype(full_type))
-    for number, value in zip(range(5, 11), (bias_out[:, B_Q : B_Q + D], bias_out[:, B_V : B_V + D], bias_out[:, B_O : B_O + D], bias_out[:, B_1 : B_1 + FF], bias_out[:, B_2 : B_2 + D], low_sum)):
-        put_row(bias_f, (plan.segments[number][3] - bias_first) * ROWS, value)
-    bias_low[...] = bias_f[...].astype(low_type).reshape(bias_low.shape)
-    store = pltpu.make_async_copy(bias_low, grads.at[pl.ds(bias_first, bias_low.shape[0])], out_sem.at[2])
-    store.start()
-    store.wait()
-    for j in (mod_steps - 2, mod_steps - 1):
-        mod_store(j).wait()
+    put_samples(note, 0, grad_mod[...], samples)
+    put_row(note, samples * MOD_CHUNKS, bias_out[...])
+    put_samples(note, samples * MOD_CHUNKS + BIAS_ROWS, modulator[...].astype(full_type), samples)
+
+
+MOD_CHUNKS = 6 * D // LANES
+BIAS_ROWS = (4 * D + FF) // LANES
+WIDTH = D // LANES
+FREQ_CHUNKS = FREQ // LANES
+
+
+def note_rows(samples):
+    layer = samples * (MOD_CHUNKS + WIDTH) + BIAS_ROWS
+    front = samples * (3 * WIDTH + FREQ_CHUNKS + 1) + WIDTH + ROWS * WIDTH
+    return up(max(layer, front), ROWS)
+
+
+def put_samples(stage, first, values, samples):
+    for j in range(values.shape[1] // LANES):
+        stage[first + j * samples : first + (j + 1) * samples, :] = values[0:samples, j * LANES : (j + 1) * LANES]
+
+
+class Notes:
+    def __init__(self, here, count, samples, owners, boxes, low, send_sem, recv_sem, own_sem):
+        self.here, self.count, self.samples = here, count, samples
+        self.owners, self.boxes, self.low = owners, boxes, low
+        self.send_sem, self.recv_sem, self.own_sem = send_sem, recv_sem, own_sem
+
+    def owned(self, i):
+        first, last = self.owners[i]
+        return (self.here.me >= first) & (self.here.me <= last)
+
+    def copies(self, i):
+        here = self.here
+        first, last = self.owners[i]
+        box = self.boxes[i].at[here.me]
+        for to in range(first, last + 1):
+            make = lambda to=to: remote(self.low.at[here.zero + i], box, pick(self.send_sem, here, i, to - first), pick(self.recv_sem, here, i), to)
+            yield to, make
+
+    def own(self, i):
+        return pltpu.make_async_copy(self.low.at[self.here.zero + i], self.boxes[i].at[self.here.me], pick(self.own_sem, self.here, i))
+
+    def send(self, i, stage):
+        self.low[i] = stage[...].astype(low_type)
+        for to, make in self.copies(i):
+            pl.when(self.here.me != to)(lambda: make().start())
+        pl.when(self.owned(i))(lambda: self.own(i).start())
+
+    def receive(self, i):
+        n = self.here.n
+        arrived(self.boxes[i].at[pl.ds(0, n - 1)], pick(self.recv_sem, self.here, i))
+        self.own(i).wait()
+
+    def drain(self, count):
+        for i in range(count):
+            for to, make in self.copies(i):
+                pl.when(self.here.me != to)(lambda: make().wait_send())
+
+
+def all_samples(notes_f, count, n, samples, first, chunk):
+    row = first + chunk * samples
+    return jnp.concatenate([notes_f[pl.ds(row + s, n, stride=count), :] for s in range(samples)], axis=0)
+
+
+def all_summed(notes_f, count, n, first, rows):
+    def body(d, value):
+        return value + notes_f[pl.ds(d * count + first, rows), :]
+
+    return lax.fori_loop(0, n, body, jnp.zeros((rows, LANES), full_type))
+
+
+def window(plan, chunks):
+    return up(-(-plan.raw // chunks) + 1, 8)
+
+
+def first_of_window(here, plan, base, chunks, depth):
+    start = here.me * plan.share // LANES
+    far = plan.length // LANES + 1
+    first = (start - base + far * chunks) // chunks - far
+    first = jnp.clip(first, -window(plan, chunks), depth)
+    return first, first * chunks + base - (start - plan.margin)
+
+
+def add_outer(here, plan, base, chunks, depth, rows_f, left_of, right_of):
+    size = window(plan, chunks)
+    first, row = first_of_window(here, plan, base, chunks, depth)
+    left = left_of(first, size)
+    near = (row >= 0) & (row + size * chunks <= rows_f.shape[0])
+
+    @pl.when(near)
+    def _():
+        for c in range(chunks):
+            rows_f[pl.ds(row + c, size, stride=chunks), :] += dot(left, right_of(c))
+
+
+def add_rows(here, plan, base, rows_f, value):
+    start = here.me * plan.share // LANES
+    stop = (here.me + 1) * plan.share // LANES
+
+    @pl.when((base >= start) & (base < stop))
+    def _():
+        rows_f[pl.ds(base - start + plan.margin, value.shape[0]), :] += value
+
+
+def turned_left(turned, size, depth, chunk_of):
+    turned[...] = jnp.zeros(turned.shape, full_type)
+    for j in range(depth // LANES):
+        turned[size + j * LANES : size + (j + 1) * LANES, :] = chunk_of(j).T
+    return lambda first, count: turned[pl.ds(first + size, count), :].astype(low_type)
+
+
+def layer_extra(here, plan, notes_f, count, n, samples, turned, rows_f):
+    base = plan.segments[4][0]
+    read = lambda first, chunk: all_samples(notes_f, count, n, samples, first, chunk)
+    modulator_first = samples * MOD_CHUNKS + BIAS_ROWS
+    left_of = turned_left(turned, window(plan, MOD_CHUNKS), D, lambda j: read(modulator_first, j))
+    add_outer(here, plan, base, MOD_CHUNKS, D, rows_f, left_of, lambda c: read(0, c).astype(low_type))
+    add_rows(here, plan, plan.segments[5][0], rows_f, all_summed(notes_f, count, n, samples * MOD_CHUNKS, BIAS_ROWS))
+    mod_bias = jnp.concatenate([rows_sum(read(0, c)) for c in range(MOD_CHUNKS)], axis=0)
+    add_rows(here, plan, plan.segments[10][0], rows_f, mod_bias)
+
+
+def front_extra(here, plan, notes_f, count, n, samples, turned, rows_f):
+    read = lambda first, chunk: all_samples(notes_f, count, n, samples, first, chunk)
+    base = lambda number: plan.segments[number][0]
+    g_cond, g_time = 0, samples * WIDTH
+    act, basis, classes = 2 * samples * WIDTH, 3 * samples * WIDTH, samples * (3 * WIDTH + FREQ_CHUNKS)
+    patch_bias = classes + samples
+    add_rows(here, plan, base(0), rows_f, all_summed(notes_f, count, n, patch_bias + WIDTH, ROWS * WIDTH))
+    add_rows(here, plan, base(1), rows_f, all_summed(notes_f, count, n, patch_bias, WIDTH))
+    size = window(plan, WIDTH)
+    low = lambda first: lambda c: read(first, c).astype(low_type)
+    add_outer(here, plan, base(2), WIDTH, FREQ, rows_f, turned_left(turned, size, FREQ, lambda j: read(basis, j)), low(g_time))
+    add_outer(here, plan, base(4), WIDTH, D, rows_f, turned_left(turned, size, D, lambda j: read(act, j)), low(g_cond))
+    kind = read(classes, 0).T
+    kind = kind[0:1, :] * CLASS_SPLIT + kind[HD : HD + 1, :]
+
+    def picked(first, rows):
+        line = lax.broadcasted_iota(jnp.int32, (rows, n * samples), 0) + first
+        return (line.astype(full_type) == kind).astype(low_type)
+
+    add_outer(here, plan, base(6), WIDTH, CLS, rows_f, picked, low(g_cond))
+    for number, first in ((3, g_time), (5, g_cond)):
+        value = jnp.concatenate([rows_sum(read(first, c)) for c in range(WIDTH)], axis=0)
+        add_rows(here, plan, base(number), rows_f, value)
+
+
+CLASS_SPLIT = 32
+
+
+def owner_range(plan, numbers):
+    first = plan.segments[numbers[0]][0] * LANES // plan.share
+    stop = plan.segments[numbers[-1]]
+    end = stop[0] * LANES + math.prod(stop[4])
+    return first, min((end - 1) // plan.share, plan.devices - 1)
+
+
+def held_whole(plan, numbers):
+    for number in numbers:
+        base, _, _, _, shape, _ = plan.segments[number]
+        start, stop = base * LANES // plan.share, (base * LANES + math.prod(shape) - 1) // plan.share
+        if start != stop or base < start * plan.share // LANES or base >= (start + 1) * plan.share // LANES:
+            return False
+    return True
+
+
+SHARES = (1.0, 1.0, 0.2)
+LAST_PHASE = LAYERS
+WEIGHTS = (14, 3, 14, 8, 10)
 
 
 def backward_kernel(plans, zs, rows, *refs):
@@ -2705,135 +2884,118 @@
     feed = iter(refs)
     take = lambda count: tuple(next(feed) for _ in range(count))
     one = lambda: next(feed)
-    one()
+    root_grads = one()
     units = take(np_)
     stream = take(LAYERS)
     saved = [take(len(SAVED)) for _ in range(LAYERS)]
     grad_in, = take(1)
     mods = take(LAYERS)
-    modulator, condition, time_pre, cond_in, noisy, basis, chosen, stats_in = take(8)
-    root_grads = one()
+    modulator, condition, time_pre, cond_in, noisy, basis, classes, stats_in = take(8)
     layer_grads = take(LAYERS)
     flats = take(np_)
     stats_out = one()
-    first = take(np_ + 1)
+    first = take(np_)
     own_units = take(np_)
-    halo_before, halo_after = take(np_), take(np_)
+    halo_before, halo_after, boxes = take(np_), take(np_), take(np_)
     buffers = ((one(), one()), (one(), one()), (one(), one()), one(), one(), one(), one())
     total, total_in = take(2)
     sems = take(9)
     frees = take(3)
-    load_sem, chunk_sem, out_sem, own_sem, halo_s, halo_r, ss, sr = take(8)
+    load_sem, chunk_sem, out_sem, own_sem, halo_s, halo_r, ss, sr, note_s, note_r, note_own = take(11)
+    note, note_low = take(2)
     here = Place(zs)
     here.greet()
     root = plans[0]
-    front_units = root.segments[FRONT][3]
-    front_planes = min(zs, -(-front_units // (8 * root.per)))
+    samples = rows // SEQ
     layers = list(reversed(range(LAYERS)))
-    buckets = [(root, root_grads, front_planes, zs)]
-    buckets += [(plans[1 + i], layer_grads[i], 0, zs) for i in layers]
-    buckets += [(root, root_grads, 0, front_planes)]
-    outs = [own_units[0]] + [own_units[1 + i] for i in layers] + [own_units[0]]
+    planes = lambda p: min(zs, -(-p.segments[4][3] // (8 * p.per)))
+    buckets = [(root, root_grads, 0, zs)]
+    buckets += [(plans[1 + i], layer_grads[i], 0, planes(plans[1 + i])) for i in layers]
+    outs = [own_units[0]] + [own_units[1 + i] for i in layers]
+    owners = [owner_range(root, range(FRONT))] + [owner_range(p, range(4, 11)) for p in plans[1:]]
+    notes = Notes(here, note.shape[0], samples, owners, boxes, note_low, note_s, note_r, note_own)
+    hosts = sorted({d for lo, hi in owners for d in range(lo, hi + 1)})
+    hosting = functools.reduce(lambda a, b: a | b, [notes.owned(i) for i in range(np_)])
+
+    @pl.when(hosting)
+    def _():
+        for to in range(here.n):
+
+            @pl.when(here.me != to)
+            def _():
+                pl.semaphore_signal(pltpu.get_barrier_semaphore(), inc=1, device_id=(to,), device_id_type=MESH)
+
+    pl.semaphore_wait(pltpu.get_barrier_semaphore(), len(here.peers()) + len(hosts) - hosting.astype(jnp.int32))
     work = Reduce(here, buckets, first, buffers, sems, frees)
-    here.met()
     work.open(0)
-    steps = [work.steps(g, outs, own_sem) for g in range(len(work.groups) + 4)]
-    of_bucket = lambda b: [step for group in steps[b * zs : (b + 1) * zs] for step in group]
-
-    def compute(grad, cond, modulator_t, *held):
+    steps = [work.steps(g, outs, own_sem) for g in range(len(work.groups) + LOOK + 2)]
+    flat = [(g, step) for g, group in enumerate(steps) for step in group]
+    upto = lambda b: sum(len(group) for group in steps[: b * zs])
+    cuts = [0]
+    for position, share in enumerate(SHARES):
+        cuts.append(max(cuts[-1], upto(position) + int(share * (upto(position + 1) - upto(position)))))
+    of_phase = lambda p: [step for _, step in flat[cuts[p] : cuts[p + 1]]]
+
+    def compute(grad, cond, *held):
         grad[...] = grad_in[...]
         cond[...] = cond_in[...]
-        modulator_t[...] = modulator[...].astype(full_type).T.astype(low_type)
         for position, ordinal in enumerate(layers):
             layer_backward_body(
                 plans[1 + ordinal], rows, stream[ordinal], saved[ordinal], units[1 + ordinal], layer_grads[ordinal],
-                mods[ordinal], grad, modulator_t, cond, held, (load_sem, chunk_sem, out_sem), spread(of_bucket(position), (14, 3, 14, 8, 10)),
+                mods[ordinal], grad, modulator, cond, note, samples, held, (load_sem, chunk_sem, out_sem), spread(of_phase(position), WEIGHTS),
             )
             work.open(1 + position)
+            notes.send(1 + ordinal, note)
         embed_back(grad, cond)
 
     def embed_back(grad, cond):
-        def run(front_w, front_f, front_low):
+        def run(front_w):
             load = pltpu.make_async_copy(units[0].at[pl.ds(root.segments[4][3], root.segments[4][2])], front_w, load_sem.at[0])
             load.start()
-            events = spread(of_bucket(LAYERS), (1, 1, 1, 1))
-            first_of = lambda number: root.segments[number][3]
-
-            def put(number, value):
-                chunks = value.shape[1] // LANES
-                blocks = value.shape[0] // ROWS
-                for b in range(blocks):
-                    for c in range(chunks):
-                        front_low[first_of(number) + b * chunks + c] = value[b * ROWS : (b + 1) * ROWS, c * LANES : (c + 1) * LANES].astype(low_type)
-
-            def put_bias(number, value):
-                front_f[...] = jnp.zeros(front_f.shape, full_type)
-                put_row(front_f, 0, value)
-                front_low[first_of(number)] = front_f[...].astype(low_type)
-
+            events = spread(of_phase(LAYERS), (1, 1))
+            low = grad[...].astype(low_type)
+            patch = dot_tn(noisy[...], low)
+            at = samples * (3 * WIDTH + FREQ_CHUNKS)
+            note[at : at + samples, :] = classes[0:samples, :]
+            put_row(note, at + samples, rows_sum(low.astype(full_type)))
+            for c in range(WIDTH):
+                note[pl.ds(at + samples + WIDTH + c, ROWS, stride=WIDTH), :] = patch[:, c * LANES : (c + 1) * LANES]
             for event in events[0]:
                 event()
-            low = grad[...].astype(low_type)
-            put(0, dot_tn(noisy[...], low))
-            put_bias(1, rows_sum(low.astype(full_type)))
+            g_low = (silu_parts(condition[...])[1] * cond[...]).astype(low_type)
+            act, slope = silu_parts(time_pre[...])
+            load.wait()
+            w_t2 = jnp.concatenate(
+                [jnp.concatenate([front_w[b * WIDTH + c] for b in range(D // ROWS)], axis=0) for c in range(WIDTH)], axis=1
+            )
+            grad_pre = dot_nt(g_low, w_t2) * slope
+            put_samples(note, 0, g_low.astype(full_type), samples)
+            put_samples(note, samples * WIDTH, grad_pre, samples)
+            put_samples(note, 2 * samples * WIDTH, act, samples)
+            put_samples(note, 3 * samples * WIDTH, basis[...].astype(full_type), samples)
+            notes.send(0, note)
             for event in events[1]:
                 event()
-            gate = silu_parts(condition[...])[1] * cond[...]
-            g_low = gate.astype(low_type)
-            pre = time_pre[...]
-            act, slope = silu_parts(pre)
-            put(4, dot_tn(act.astype(low_type), g_low))
-            put_bias(5, rows_sum(g_low.astype(full_type)))
-            few = g_low.shape[0]
-            stacked = jnp.concatenate([gate[:, c * LANES : (c + 1) * LANES] for c in range(D // LANES)], axis=0)
-            for event in events[2]:
-                event()
-            span = 16 * ROWS
-            table_first, table_count = first_of(6), root.segments[6][2]
-            for start in range(0, table_count * ROWS, span):
-                size = min(span, table_count * ROWS - start)
-                value = dot_tn(chosen[:, start : start + size], stacked.astype(low_type))
-                front_low[table_first + start // ROWS : table_first + (start + size) // ROWS] = value.astype(low_type).reshape(size // ROWS, ROWS, LANES)
-            load.wait()
-            w_t2 = jnp.concatenate(
-                [jnp.concatenate([front_w[b * (D // LANES) + c] for b in range(D // ROWS)], axis=0) for c in range(D // LANES)], axis=1
-            )
-            grad_pre = (dot_nt(g_low, w_t2) * slope).astype(low_type)
-            put(2, dot_tn(basis[...], grad_pre))
-            put_bias(3, rows_sum(grad_pre.astype(full_type)))
-            store = pltpu.make_async_copy(front_low, root_grads.at[pl.ds(0, front_units)], load_sem.at[1])
-            store.start()
-            for event in events[3]:
-                event()
-            store.wait()
-
-        pl.run_scoped(
-            run,
-            pltpu.VMEM((root.segments[4][2], ROWS, LANES), low_type),
-            pltpu.VMEM((ROWS, LANES), full_type),
-            pltpu.VMEM((front_units, ROWS, LANES), low_type),
-        )
+
+        pl.run_scoped(run, pltpu.VMEM((root.segments[4][2], ROWS, LANES), low_type))
 
     plan = plans[1]
-    bias_units = plan.units - plan.segments[5][3]
     f32 = lambda *dims: pltpu.VMEM(dims, full_type)
     bf16 = lambda *dims: pltpu.VMEM(dims, low_type)
     tile = (ROWS, LANES)
     few = modulator.shape[0]
     pl.run_scoped(
         compute,
-        f32(rows, D), f32(few, D), bf16(D, few),
+        f32(rows, D), f32(few, D),
         bf16(rows, 3 * D), bf16(rows, D), bf16(rows, D), f32(rows, D), f32(rows, D), f32(2, rows, WIDE),
         bf16(2, D // ROWS, 2, *tile), bf16(2, WIDE // ROWS, D // LANES, *tile),
         segment_scratch(plan, 0), segment_scratch(plan, 1),
         bf16(rows, 3 * D), bf16(rows, D), bf16(rows, WIDE), bf16(D, rows), f32(rows, D),
         bf16(2, WIDE // ROWS, D // LANES, *tile), bf16(2, D // ROWS, 2, *tile),
-        f32(few, 6 * D), f32(1, 4 * D + FF), f32(bias_units * ROWS, LANES), bf16(bias_units, *tile),
+        f32(few, 6 * D), f32(1, 4 * D + FF),
     )
-    final = len(buckets) - 1
-    work.open(final)
-
-    def unpack(units_f, rows_f, flat_f):
+
+    def unpack(units_f, rows_f, flat_f, box, notes_f, *turned):
         def halo(i):
             p = plans[i]
             forward = remote(own_units[i].at[pl.ds(p.per - p.units_before, p.units_before)], halo_before[i], halo_s.at[i, 0], halo_r.at[i, 0], here.following)
@@ -2854,7 +3016,24 @@
                 copy.start()
             for copy in parts:
                 copy.wait()
-            squares = unpack_rows(here, p, units_f, rows_f, flat_f, base)
+            rows_f[...] = jnp.zeros(rows_f.shape, full_type)
+
+            @pl.when(notes.owned(i))
+            def _():
+                notes.receive(i)
+                copy = pltpu.make_async_copy(boxes[i], box, load_sem.at[4])
+                copy.start()
+                copy.wait()
+                count = box.shape[1]
+
+                def widen(d):
+                    notes_f[pl.ds(pl.multiple_of(d * count, ROWS), count), :] = box[d].astype(full_type)
+
+                loop(here.n, widen)
+                extra = layer_extra if i else front_extra
+                extra(here, p, notes_f, count, here.n, samples, turned[1 if i else 0], rows_f)
+
+            squares = unpack_rows(here, p, p.reduced, units_f, rows_f, flat_f, base)
             store = pltpu.make_async_copy(flat_f.at[pl.ds(0, p.raw)], flats[i], load_sem.at[3])
             store.start()
             store.wait()
@@ -2862,27 +3041,36 @@
 
         total[0] = stats_in[...]
         total[1] = jnp.zeros((8, LANES), full_type)
+        ready = [0] + [1 + ordinal for ordinal in layers]
         begun, done = {}, set()
-        for g in range((LAYERS + 1) * zs, len(steps) + 1):
-            for position, ordinal in enumerate(layers):
-                i = 1 + ordinal
-                if i not in begun and g > zs * (position + 2) + 2:
+
+        def between(g):
+            for b, i in enumerate(ready):
+                if i not in begun and g > zs * (b + 1) + LOOK + 1:
                     begun[i] = g
                     for copy in halo(i):
                         copy.start()
                 elif i in begun and i not in done and g > begun[i]:
                     done.add(i)
                     finish(i)
-            for step in steps[g] if g < len(steps) else ():
-                step()
-        for copy in halo(0):
-            copy.start()
-        finish(0)
+                    return
+
+        seen = -1
+        for g, step in flat[cuts[-1] :]:
+            if g != seen and g > LAST_PHASE * zs:
+                between(g)
+            seen = g
+            step()
+        for extra in range(2 * len(ready)):
+            between(len(steps) + extra)
 
     most = max(p.units_before + p.per + p.units_after for p in plans)
     pl.run_scoped(
         unpack,
-        f32(most, *tile), f32(max(p.spread for p in plans), LANES), f32(max(p.raw for p in plans), LANES),
+        f32(most, *tile), f32(max(max(p.spread, p.margin + c * window(p, c)) for p in plans for c in (WIDTH, MOD_CHUNKS)), LANES),
+        f32(max(p.raw for p in plans), LANES),
+        pltpu.VMEM(boxes[0].shape, low_type), f32(boxes[0].shape[0] * boxes[0].shape[1], LANES),
+        f32(D + 2 * window(root, WIDTH), samples * here.n), f32(D + 2 * window(plan, MOD_CHUNKS), samples * here.n),
     )
     step = 0
     for to in ((here.cpeer,), (here.xpeer,), (here.ypeer,), tuple(here.above(k) for k in range(1, zs))):
@@ -2898,6 +3086,7 @@
             value = value + total_in[step - 1 - i]
         total[...] = value
     stats_out[...] = total[...]
+    notes.drain(np_)
     work.close()
 
 
@@ -2905,44 +3094,47 @@
     n = plans[0].devices
     zs = n // 8
     rows = grad.shape[0]
-    np_, nb = len(plans), len(plans) + 1
+    np_ = nb = len(plans)
+    count = note_rows(rows // SEQ)
     vm = pl.BlockSpec(memory_space=pltpu.VMEM)
     hbm = pl.BlockSpec(memory_space=pltpu.HBM)
     shape = jax.ShapeDtypeStruct
     dma, regular = pltpu.SemaphoreType.DMA, pltpu.SemaphoreType.REGULAR
     tile = (ROWS, LANES)
     layers = list(reversed(range(LAYERS)))
-    order = [plans[0]] + [plans[1 + i] for i in layers] + [plans[0]]
+    order = [plans[0]] + [plans[1 + i] for i in layers]
     all_units = lambda p: shape((n * p.per,) + tile, low_type)
-    out_shape = [all_units(p) for p in plans]
+    out_shape = [all_units(p) for p in plans[1:]]
     out_shape += [shape((p.raw, LANES), full_type) for p in plans]
     out_shape += [shape((2, 8, LANES), full_type)]
     out_shape += [shape((zs, 2, 2, p.per) + tile, low_type) for p in order]
     out_shape += [shape((p.per,) + tile, full_type) for p in plans]
     out_shape += [shape((p.units_before,) + tile, full_type) for p in plans]
     out_shape += [shape((p.units_after,) + tile, full_type) for p in plans]
+    out_shape += [shape((n, count, LANES), low_type) for p in plans]
     most = max(p.per for p in plans)
     half = lambda *lead: pltpu.VMEM(lead + (most // 2,) + tile, low_type)
     hops = 2 + zs
-    scratch = [half(zs, 2)] * 4 + [half(zs)] * 2 + [half(2, zs - 1)]
-    scratch += [pltpu.VMEM((7, most) + tile, low_type), pltpu.VMEM((2, most) + tile, low_type)]
+    scratch = [half(zs, 2)] * 4 + [half(zs)] * 2 + [half(2, 2, zs - 1)]
+    scratch += [pltpu.VMEM((3 * LOOK + 4, most) + tile, low_type), pltpu.VMEM((2, most) + tile, low_type)]
     scratch += [pltpu.VMEM((most,) + tile, full_type)]
     scratch += [pltpu.VMEM((2, 8, LANES), full_type), pltpu.VMEM((hops, 2, 8, LANES), full_type)]
-    scratch += [dma((nb, zs, 2, 2))] * 2 + [dma((2, zs, 2))] * 2 + [dma((2, zs))] * 2 + [dma((2, zs - 1))] * 2 + [dma((7, 2))]
+    scratch += [dma((nb, zs, 2, 2))] * 2 + [dma((2, zs, 2))] * 2 + [dma((2, zs))] * 2 + [dma((2, 2, zs - 1))] * 2 + [dma((3 * LOOK + 4, 2))]
     scratch += [regular((2, zs)), regular((2, zs)), regular((zs - 1,))]
     scratch += [dma((7,)), dma((2, 3)), dma((4,)), dma, dma((np_, 2)), dma((np_, 2)), dma((hops,)), dma((hops,))]
+    scratch += [dma((np_, n)), dma((np_,)), dma((np_,))]
+    scratch += [pltpu.VMEM((count, LANES), full_type), pltpu.VMEM((np_, count, LANES), low_type)]
     flat_saved = [array for group in saved for array in group]
     results = pl.pallas_call(
         functools.partial(backward_kernel, plans, zs, rows),
         out_shape=out_shape,
         in_specs=[hbm] * (1 + np_ + LAYERS + len(flat_saved)) + [vm] * (1 + LAYERS + len(small) + 1),
-        out_specs=[hbm] * (2 * np_) + [vm] + [hbm] * (nb + 3 * np_),
-        input_output_aliases={0: 0},
+        out_specs=[hbm] * (2 * np_ - 1) + [vm] + [hbm] * (nb + 4 * np_),
         scratch_shapes=scratch,
         compiler_params=pltpu.CompilerParams(collective_id=1, has_side_effects=True, vmem_limit_bytes=62 * MB),
         name="backward_and_reduce",
     )(root_grads, *units, *stream, *flat_saved, grad, *mods, *small, stats)
-    return results[np_ : 2 * np_], results[2 * np_]
+    return results[np_ - 1 : 2 * np_ - 1], results[2 * np_ - 1]
 
 
 def model_step(layer_lists, pieces, latents, noise, times, labels, dropped, features, devices):
@@ -3068,7 +3260,9 @@
     square_sums = jnp.stack([jnp.sum(total[:3], axis=1) for total in sums])
     numbers = jnp.concatenate([loss_part[None], square_sums.reshape(-1)])
     stats = jnp.pad(numbers, (0, 8 * LANES - numbers.shape[0])).reshape(8, LANES)
-    small = (modulator_rows, condition, time_pre, grad_cond, noisy_bf.reshape(rows, PD), extra(basis_bf), chosen)
+    class_parts = jnp.stack([classes // CLASS_SPLIT, classes % CLASS_SPLIT], axis=1)
+    class_rows = extra(jnp.repeat(class_parts.astype(full_type), LANES // 2, axis=1))
+    small = (modulator_rows, condition, time_pre, grad_cond, noisy_bf.reshape(rows, PD), extra(basis_bf), class_rows)
     rows_out, stats = backward_call(
         plans, units, stream[:-1], kept, grad, mods, small, stats, root_grads
     )
@@ -3115,9 +3309,10 @@
 ):
     devices = lax.axis_size("fsdp")
     data = (latents, noise, times, labels, dropped, features)
-    plan = Plan(layer_layout(), layer_flat.shape[1] * devices, devices)
-    root_plan = Plan(root_layout(), root_flat.shape[0] * devices, devices)
-    if devices % 8 == 0 and plan.fits and root_plan.fits:
+    plan = Plan(layer_layout(), layer_flat.shape[1] * devices, devices, (0, 4))
+    root_plan = Plan(root_layout(), root_flat.shape[0] * devices, devices, (FRONT, None))
+    alone = held_whole(plan, range(5, 11)) and held_whole(root_plan, (0, 1, 3, 5))
+    if devices % 8 == 0 and plan.fits and root_plan.fits and alone:
         reduced = by_kernels(plan, root_plan, layer_flat, root_flat, data, devices)
     else:
         reduced = by_collectives(layer_flat, root_flat, data, devices)

time: 851 us -> 797 us (0.937)
  Pallas kernels: 760 us -> 705 us
    pallas_call x1, Pallas kernels: 378 us -> 323 us  [backward_call(): pl.pallas_call(functools.partial(backward_kernel, plans, zs, rows), out_s...]
where the time goes in v4:
time: 797 us; the launch traced here: 786 us
  Pallas kernels  705 us (88%)
  local copies, waits for them, and re-layouts  47.1 us (6%)
  other arithmetic  30 us (4%)
    pallas_call x1, Pallas kernels, forward_call(): pl.pallas_call(functools.partial(forward_kernel, plans, zs, rows), out_sh...  333 us
    pallas_call x1, Pallas kernels, backward_call(): pl.pallas_call(functools.partial(backward_kernel, plans, zs, rows), out_s...  323 us
    pallas_call x1, Pallas kernels, top_call(): pl.pallas_call(functools.partial(top_kernel, plan, rows, sample_total), o...  49.2 us

profile of v4, /device:TPU:6, one launch (start us, length us, event | category | flops | bytes accessed | tf_op | source)
XLA Modules:
  0.0 786.2 jit_solution(17870885078294213038)
XLA Ops:
  0.7 0.8 fusion.9
  1.4 0.7 fusion.12
  5.2 0.9 fusion.15
  6.0 0.8 copy.24
  6.9 0.7 pad.63.target
  7.8 1.2 tile.20
  9.0 1.3 fusion.1.refs_6_
  10.3 1.1 pad_bitcast_fusion.2.refs_0_
  11.4 13.9 %slice_reduce_fusion = (f32[332112]{0:T(1024)S(1)}, f32[332112]{0:T(1024)S(1)}) fusion(f32[2,332112]{1,0:T(2,128)S(1)} %copy-done), kind=kLoop, calls=%fused_computation.11 | loop fusion | bytes 5313792 | tf_op jit(solution)/shard_map/slice | solution.py:3230
  25.3 1.9 pad_bitcast_fusion
  27.2 332.8 %gather_and_forward.1 = (bf16[4992,16,128]{2,1,0:T(8,128)(2,1)}, bf16[5248,16,128]{2,1,0:T(8,128)(2,1)}, bf16[5248,16,128]{2,1,0:T(8,128)(2,1)}, f32[512,768]{1,...) custom-call(f32[2496,128]{1,0:T(8,128)} %pad_bitcast_fusion.2.refs_0, ...), custom_call_target="tpu_custom_call" | custom-call | tf_op jit(solution)/shard_map/gather_and_forward/pallas_call | solution.py:2125
  360.0 0.9 slice_reduce_fusion.3
  360.8 0.9 slice_reduce_fusion.2
  361.8 0.7 convert_bitcast_fusion.1
  364.4 1.3 slice_bitcast_fusion.1
  366.2 0.7 slice.92
  367.1 0.7 pad.65.w_h
  367.9 49.2 %projector_and_head.1 = (f32[512,768]{1,0:T(8,128)}, f32[8,128]{1,0:T(8,128)}, f32[16,768]{1,0:T(8,128)}, f32[1,6528]{1,0:T(1,128)}, f32[768,128]{1,0:T(8,128)}, /*index=5*/bf16[4992,16,128]{2,1,0:T(8,128)(2,1)}) custom-call(f32[512,768]{1,0:T(8,128)} %get-tuple-element.48.x, bf16[512,768]{1,0:T(8,128)(2,1)} %bitcast.68, f32[512,128]{1,0:T(8,128)} %pad.63.target, ...), custom_call_target="tpu_custom_call" | custom-call | tf_op jit(solution)/shard_map/projector_and_head/pallas_call | solution.py:1594
  417.1 1.3 slice_reduce_fusion.9
  419.0 1.2 slice.97
  421.5 0.8 convert.25
  424.2 1.0 slice.134
  426.0 322.7 %backward_and_reduce.1 = (bf16[5248,16,128]{2,1,0:T(8,128)(2,1)}, bf16[5248,16,128]{2,1,0:T(8,128)(2,1)}, f32[2496,128]{1,0:T(8,128)}, f32[2624,128]{1,0:T(8,128...) custom-call(bf16[4992,16,128]{2,1,0:T(8,128)(2,1)} %maximum_dynamic-, ...), custom_call_target="tpu_custom_call" | custom-call | tf_op jit(solution)/shard_map/backward_and_reduce/pallas_call | solution.py:3128
  748.7 1.3 slice_reduce_fusion.7
  751.4 1.4 slice.111
  752.8 6.2 stack.33
  759.6 1.5 slice.112
  761.2 6.2 stack.34
  767.5 2.6 multiply_subtract_fusion.1
  770.1 1.3 copy-done.3
  771.4 0.8 copy-done.4
  772.2 12.7 %multiply_subtract_fusion = (f32[2,332112]{1,0:T(2,128)}, f32[2,332112]{1,0:T(2,128)}, f32[2,332112]{1,0:T(2,128)}) fusion(f32[2,332112]{1,0:T(2,128)S(1)} %copy-done.1, f32[]{:T(128)S(6)} %div.65, f32[1,332112]{1,0:T(1,128)S(1)} %stack.34, f32[1,332112]{1,0:T(1,128)S(1)} %stack.33, f32[2,332112]{1,0:T(2,128)S(1)} %copy-done.3, f32[2,332112]{1,0:T(2,128)S(1)} %copy-done.4), kind=kLoop, calls=%fused_computation.4 | loop fusion | flops 10627584 | bytes 18598276 | tf_op jit(solution)/shard_map/sub | solution.py:3183
  (59 shorter events, 10.6 us)
Async XLA Ops:
  7.8 2.5 copy-start.2
  9.0 2.4 copy-start
  759.6 7.8 copy-start.7
  761.2 6.3 copy-start.5
  761.2 6.3 copy-start.6
  767.4 2.6 copy-start.1
  767.4 3.9 copy-start.3
  767.4 4.7 copy-start.4

commit v5 on v4

--- a/solution.py
+++ b/solution.py
@@ -1848,7 +1848,7 @@
     feed = iter(refs)
     take = lambda count: tuple(next(feed) for _ in range(count))
     one = lambda: next(feed)
-    raw_hbm = take(np_)
+    raw_hbm = take(2)
     noisy, positions, basis, chosen = take(4)
     units = take(np_)
     stream = take(LAYERS + 1)
@@ -1873,24 +1873,35 @@
     starts[-1].append(last)
 
     def prepare(*scratch):
-        raw, ext, tail = (scratch[i * np_ : (i + 1) * np_] for i in range(3))
-        loads = [pltpu.make_async_copy(raw_hbm[i], raw[i].at[pl.ds(8, p.raw)], raw_sem.at[i]) for i, p in enumerate(plans)]
-        for copy in loads:
-            copy.start()
+        raw, ext, tail = scratch[:2], scratch[2 : 2 + np_], scratch[2 + np_ :]
+        counts = (1,) + (LAYERS,) * LAYERS
+        pad = 8 * LAYERS
+        loads = [pltpu.make_async_copy(raw_hbm[i], raw[i].at[pl.ds(pad, raw_hbm[i].shape[0])], raw_sem.at[i]) for i in range(2)]
+        for i in range(2):
+            loads[i].start()
+            raw[i][pl.ds(0, pad), :] = jnp.zeros((pad, LANES), full_type)
         lane = lax.broadcasted_iota(jnp.int32, (64, LANES), 1)
         halos = []
         for i, p in enumerate(plans):
             shift = lax.rem(here.me * p.share, LANES)
             delta = (here.me + 1) * p.share // LANES - here.me * p.share // LANES
-            raw[i][pl.ds(0, 8), :] = jnp.zeros((8, LANES), full_type)
             ext[i][pl.ds(0, p.before), :] = jnp.zeros((p.before, LANES), full_type)
             ext[i][pl.ds(p.before + p.raw, p.after), :] = jnp.zeros((p.after, LANES), full_type)
-            loads[i].wait()
+            if i < 2:
+                loads[i].wait()
+            every = counts[i]
+
+            def rows_from(start):
+                source = raw[min(i, 1)]
+                first = pad + every * start + max(i - 1, 0)
+                if every == 1:
+                    return source[pl.ds(first, 64), :]
+                return source[pl.ds(first, 64, stride=every), :]
 
             def align(j):
                 row = pl.multiple_of(j * 64, 64)
-                level = pltpu.roll(raw[i][pl.ds(row + 8, 64), :], shift, 1)
-                above = pltpu.roll(raw[i][pl.ds(row + 7, 64), :], shift, 1)
+                level = pltpu.roll(rows_from(row), shift, 1)
+                above = pltpu.roll(rows_from(row - 1), shift, 1)
                 ext[i][pl.ds(row + p.before, 64), :] = jnp.where(lane >= shift, level, above)
 
             loop(p.raw // 64, align)
@@ -1914,7 +1925,7 @@
     f32 = lambda *dims: pltpu.VMEM(dims, full_type)
     pl.run_scoped(
         prepare,
-        *[f32(p.raw + 8, LANES) for p in plans],
+        f32(plans[0].raw + 8 * LAYERS, LANES), f32(LAYERS * (plans[1].raw + 8), LANES),
         *[f32(p.ext, LANES) for p in plans],
         *[f32(p.before + 8, LANES) for p in plans],
     )
@@ -2125,7 +2136,7 @@
     results = pl.pallas_call(
         functools.partial(forward_kernel, plans, zs, rows),
         out_shape=out_shape,
-        in_specs=[hbm] * np_ + [vm] * 4,
+        in_specs=[hbm] * 2 + [vm] * 4,
         out_specs=[hbm] * np_ + [vm] * (LAYERS + 1 + 2 * LAYERS + 3) + [hbm] * (len(SAVED) * LAYERS),
         scratch_shapes=scratch,
         compiler_params=pltpu.CompilerParams(collective_id=0, has_side_effects=True, vmem_limit_bytes=62 * MB),
@@ -3226,8 +3237,9 @@
     few = up(samples, ROWS)
     wide = D // LANES
     plans = (root_plan,) + (plan,) * LAYERS
-    raws = [to_rows(root_flat, root_plan)]
-    raws += [to_rows(layer_flat[ordinal], plan) for ordinal in range(LAYERS)]
+    padded = jnp.pad(layer_flat, ((0, 0), (0, plan.raw * LANES - plan.share)))
+    turns = padded.reshape(LAYERS, plan.raw, LANES).transpose(1, 0, 2).reshape(LAYERS * plan.raw, LANES)
+    raws = [to_rows(root_flat, root_plan), turns]
     mixing = times[:, None, None]
     noisy_bf = ((1.0 - mixing) * latents + mixing * noise).astype(low_type)
     positions = jnp.tile(position_table(), (samples, 1))

time: 797 us -> 781 us (0.980)
  local copies, waits for them, and re-layouts: 47.1 us -> 34.5 us
    slice x1 -> x0, local copies, waits for them, and re-layouts: 13.9 us -> none  [by_kernels(): raws += [to_rows(layer_flat[ordinal], plan) for ordinal in range(LAYERS)]]
where the time goes in v5:
time: 781 us; the launch traced here: 773 us
  Pallas kernels  705 us (90%)
  local copies, waits for them, and re-layouts  34.5 us (4%)
  other arithmetic  29.2 us (4%)
    pallas_call x1, Pallas kernels, forward_call(): pl.pallas_call(functools.partial(forward_kernel, plans, zs, rows), out_sh...  333 us
    pallas_call x1, Pallas kernels, backward_call(): pl.pallas_call(functools.partial(backward_kernel, plans, zs, rows), out_s...  323 us
    pallas_call x1, Pallas kernels, top_call(): pl.pallas_call(functools.partial(top_kernel, plan, rows, sample_total), o...  49.2 us

profile of v5, /device:TPU:6, one launch (start us, length us, event | category | flops | bytes accessed | tf_op | source)
XLA Modules:
  0.0 772.8 jit_solution(8506005389304429378)
XLA Ops:
  0.7 0.8 fusion.9
  1.4 0.7 fusion.12
  5.2 0.9 fusion.15
  6.0 0.8 copy.26
  6.9 0.7 pad.59.target
  7.8 1.2 tile.20
  9.0 1.3 fusion.1.refs_5_
  10.3 1.1 pad_bitcast_fusion.refs_0_
  11.4 3.0 pad.56
  14.5 332.8 %gather_and_forward.1 = (bf16[4992,16,128]{2,1,0:T(8,128)(2,1)}, bf16[5248,16,128]{2,1,0:T(8,128)(2,1)}, bf16[5248,16,128]{2,1,0:T(8,128)(2,1)}, f32[512,768]{1,...) custom-call(f32[2496,128]{1,0:T(8,128)} %pad_bitcast_fusion.refs_0_,, ...), custom_call_target="tpu_custom_call" | custom-call | tf_op jit(solution)/shard_map/gather_and_forward/pallas_call | solution.py:2136
  347.3 0.9 slice_reduce_fusion
  348.3 0.7 convert_bitcast_fusion.1
  349.6 0.7 convert_bitcast_fusion
  350.9 1.3 slice_bitcast_fusion.1
  352.7 0.7 slice.84
  353.7 0.7 pad.61.w_h
  354.4 49.2 %projector_and_head.1 = (f32[512,768]{1,0:T(8,128)}, f32[8,128]{1,0:T(8,128)}, f32[16,768]{1,0:T(8,128)}, f32[1,6528]{1,0:T(1,128)}, f32[768,128]{1,0:T(8,128)}, /*index=5*/bf16[4992,16,128]{2,1,0:T(8,128)(2,1)}) custom-call(f32[512,768]{1,0:T(8,128)} %get-tuple-element.48.x, bf16[512,768]{1,0:T(8,128)(2,1)} %bitcast.70, f32[512,128]{1,0:T(8,128)} %pad.59.target, ...), custom_call_target="tpu_custom_call" | custom-call | tf_op jit(solution)/shard_map/projector_and_head/pallas_call | solution.py:1594
  403.6 1.3 slice_reduce_fusion.7
  405.5 1.2 slice.89
  407.4 0.7 fusion.8.refs_32_
  408.1 0.8 convert.25
  410.7 1.0 slice.124
  412.5 322.7 %backward_and_reduce.1 = (bf16[5248,16,128]{2,1,0:T(8,128)(2,1)}, bf16[5248,16,128]{2,1,0:T(8,128)(2,1)}, f32[2496,128]{1,0:T(8,128)}, f32[2624,128]{1,0:T(8,128...) custom-call(bf16[4992,16,128]{2,1,0:T(8,128)(2,1)} %maximum_dynamic-, ...), custom_call_target="tpu_custom_call" | custom-call | tf_op jit(solution)/shard_map/backward_and_reduce/pallas_call | solution.py:3139
  735.3 1.3 slice_reduce_fusion.5
  737.9 1.4 slice.103
  739.3 6.2 stack.33
  746.2 1.6 slice.104
  747.7 6.2 stack.34
  754.0 2.6 multiply_subtract_fusion.1
  756.6 1.3 copy-done.3
  757.9 0.8 copy-done.4
  758.7 12.7 %multiply_subtract_fusion = (f32[2,332112]{1,0:T(2,128)}, f32[2,332112]{1,0:T(2,128)}, f32[2,332112]{1,0:T(2,128)}) fusion(f32[2,332112]{1,0:T(2,128)S(1)} %copy-done.1, f32[]{:T(128)S(6)} %div.65, f32[1,332112]{1,0:T(1,128)S(1)} %stack.34, f32[1,332112]{1,0:T(1,128)S(1)} %stack.33, f32[2,332112]{1,0:T(2,128)S(1)} %copy-done.3, f32[2,332112]{1,0:T(2,128)S(1)} %copy-done.4), kind=kLoop, calls=%fused_computation.4 | loop fusion | flops 10627584 | bytes 18598276 | tf_op jit(solution)/shard_map/sub | solution.py:3194
  (56 shorter events, 9.2 us)
Async XLA Ops:
  7.7 2.6 copy-start.2
  9.0 2.4 copy-start
  746.1 7.8 %copy-start.5 = (f32[315904]{0:T(1024)S(1)}, f32[315904]{0:T(1024)}, u32[]{:S(2)}) copy-start(f32[315904]{0:T(1024)} %param.22) | copy-start | bytes 3790852
  746.2 7.8 %copy-start.6 = (f32[315904]{0:T(1024)S(1)}, f32[315904]{0:T(1024)}, u32[]{:S(2)}) copy-start(f32[315904]{0:T(1024)} %param.23) | copy-start | bytes 3790852
  746.2 7.8 %copy-start.7 = (f32[2496,128]{1,0:T(8,128)S(1)}, f32[2496,128]{1,0:T(8,128)}, u32[]{:S(2)}) copy-start(f32[2496,128]{1,0:T(8,128)} %get-tuple-element.86) | copy-start | bytes 3833860
  754.0 2.6 copy-start.1
  754.0 3.9 copy-start.3
  754.0 4.7 copy-start.4
